TPU v7x, 512 devices: a whole 4x8x8 slice. The times are simulated.
512 devices in a mesh: row: 8 (over y), col: 8 (over z_lo, x), depth: 8 (over z_hi, core).
Axes of the slice: x: 4, y: 8, z: 8 (z_hi: 4, z_lo: 2; z = z_hi * 2 + z_lo), core: 2. Of those that a mesh axis runs over, the one named last changes fastest.
Arguments:
- amplitudes: float32 [32, 32, 512, 512], P('row', 'col', 'depth'), may hold values from -6 to 6
- ladder_ints: float32 [512, 512, 640], P('depth', ('row', 'col')), may hold values from -0.01171875 to 0.01171875
- cycle_ints: float32 [32, 512, 128], P(None, ('row', 'col')), may hold values from -0.125 to 0.125
- occ_irrep: int32 [32], replicated, may hold values from 0 to 7
- vir_irrep: int32 [512], replicated, may hold values from 0 to 7
- pair_irrep: int32 [128], replicated, may hold values from 0 to 7
Outputs:
- ladder_resid: float32 [1024, 640], P(('row', 'col', 'depth'))
- cycle_resid: float32 [32, 512, 128], P(None, 'depth', ('row', 'col'))
All inputs are finite; a program needn't handle non-finite values.
Results may differ from a plain program's by a relative error of at most 0.00007.
Values sent between devices are 32-bit elements; how exact they have to be, the bound alone decides.
No kernel may reach another device: no remote copies, remote signals or barrier semaphores. Data moves between devices by JAX's collectives and lax.ppermute only.
A program may use at most 128 MiB of HBM per device.

v0:
```python
import jax
import jax.numpy as jnp
from jax import lax
from jax.sharding import PartitionSpec as P


def body(amplitudes, ladder_ints, cycle_ints, occ_irrep, vir_irrep, pair_irrep):
    highest = lax.Precision.HIGHEST
    regrouped = lax.all_to_all(
        lax.all_to_all(amplitudes, "row", split_axis=3, concat_axis=0, tiled=True),
        "col",
        split_axis=3,
        concat_axis=1,
        tiled=True,
    )
    occ_count = regrouped.shape[0]
    first_block = regrouped.shape[2]
    second_block = regrouped.shape[3]
    slab_cols = ladder_ints.shape[2]
    ladder_part = jnp.dot(
        regrouped.reshape(occ_count * occ_count, first_block * second_block),
        ladder_ints.reshape(first_block * second_block, slab_cols),
        precision=highest,
        preferred_element_type=jnp.float32,
    )
    block_start = lax.axis_index(("row", "col")) * second_block
    local_labels = lax.dynamic_slice_in_dim(vir_irrep, block_start, second_block)
    allowed = (
        jnp.bitwise_xor(occ_irrep[:, None, None], local_labels[None, :, None])
        == pair_irrep[None, None, :]
    )
    masked = jnp.where(allowed, cycle_ints, jnp.zeros_like(cycle_ints))
    cycle_part = jnp.einsum(
        "ikac,kcf->iaf", regrouped, masked, precision=highest, preferred_element_type=jnp.float32
    )
    ladder_resid = lax.psum_scatter(
        ladder_part, ("row", "col", "depth"), scatter_dimension=0, tiled=True
    )
    cycle_resid = lax.psum_scatter(cycle_part, ("row", "col"), scatter_dimension=2, tiled=True)
    return (ladder_resid, cycle_resid)


def solution(mesh):
    in_specs = (
        P("row", "col", "depth", None),
        P("depth", ("row", "col"), None),
        P(None, ("row", "col"), None),
        P(),
        P(),
        P(),
    )
    out_specs = (P(("row", "col", "depth"), None), P(None, "depth", ("row", "col")))
    return jax.shard_map(body, mesh=mesh, in_specs=in_specs, out_specs=out_specs, check_vma=False)
```

profile of v0, /device:TPU:6, one launch (start us, length us, event | category | flops | bytes accessed | tf_op | source)
XLA Modules:
  0.0 538.6 jit_solution(3229110020632788655)
XLA Ops:
  8.0 0.0 copy-start
  8.0 0.0 all-reduce.3.cloned.1.call-start
  8.1 5.0 copy.20
  13.0 6.8 %reshape.48 = f32[8,1,65536]{2,1,0:T(1,128)S(1)} reshape(f32[512,4,4,64]{3,2,1,0:T(4,128)} %bitcast.32) | data formatting | bytes 4194304
  19.8 58.2 %all_to_all.36 = f32[8,1,65536]{2,1,0:T(1,128)} all-to-all(f32[8,1,65536]{2,1,0:T(1,128)S(1)} %reshape.48), channel_id=1, replica_groups=mesh['row'=8,'col'=8,'depth'=8] {'row'}, dimensions={0} | all-to-all | bytes 4194304 | tf_op jit(solution)/shard_map/all_to_all | solution.py:10
  78.0 0.5 broadcast.24
  78.6 7.2 %reduce = f32[8,65536]{1,0:T(8,128)S(1)} reduce(f32[8,1,65536]{2,1,0:T(1,128)} %all_to_all.36, f32[]{:T(128)} %broadcast.24), dimensions={1}, to_apply=%all_to_all.26.reduce_sub_computation | reduce | bytes 4194308 | tf_op jit(solution)/shard_map/all_to_all | solution.py:10
  85.8 4.8 reshape.49
  90.6 5.4 %copy.31 = f32[4,4,64,8,64]{4,2,1,0,3:T(8,128)} copy(f32[4,4,64,8,64]{2,1,0,4,3:T(4,128)} %bitcast.34) | data formatting | bytes 4194304 | tf_op jit(solution)/shard_map/all_to_all | solution.py:10
  96.0 6.3 %copy.23 = f32[32,4,64,64]{2,1,0,3:T(4,128)} copy(f32[32,4,64,64]{3,2,1,0:T(8,128)} %bitcast.35) | data formatting | bytes 4194304 | tf_op jit(solution)/shard_map/all_to_all | solution.py:10
  102.3 6.8 %reshape.50 = f32[8,1,65536]{2,1,0:T(1,128)S(1)} reshape(f32[64,32,4,64]{3,2,1,0:T(4,128)} %bitcast.36) | data formatting | bytes 4194304
  109.1 29.2 %all_to_all.37 = f32[8,1,65536]{2,1,0:T(1,128)} all-to-all(f32[8,1,65536]{2,1,0:T(1,128)S(1)} %reshape.50), channel_id=1, replica_groups=mesh['row'=8,'col'=8,'depth'=8] {'col'}, dimensions={0} | all-to-all | bytes 4194304 | tf_op jit(solution)/shard_map/all_to_all | solution.py:9
  138.3 7.2 %reduce.1 = f32[8,65536]{1,0:T(8,128)S(1)} reduce(f32[8,1,65536]{2,1,0:T(1,128)} %all_to_all.37, f32[]{:T(128)} %broadcast.24), dimensions={1}, to_apply=%all_to_all.30.reduce_sub_computation | reduce | bytes 4194308 | tf_op jit(solution)/shard_map/all_to_all | solution.py:9
  145.5 4.8 reshape.51
  150.3 6.7 %copy.33 = f32[32,4,64,64]{2,3,1,0:T(8,128)} copy(f32[32,4,64,64]{2,1,0,3:T(4,128)} %bitcast.37) | data formatting | bytes 4194304 | tf_op jit(solution)/shard_map/all_to_all | solution.py:9
  157.0 17.8 %copy.25 = f32[32,8,4,64,8]{4,3,2,1,0:T(8,128)} copy(f32[32,8,4,64,8]{3,4,1,2,0:T(8,128)} %bitcast.30) | data formatting | bytes 4194304 | tf_op jit(solution)/shard_map/all_to_all | solution.py:9
  174.8 24.0 %reshape.44 = f32[1024,512]{1,0:T(8,128)S(1)} reshape(f32[32,8,4,64,8]{4,3,2,1,0:T(8,128)} %copy.25) | data formatting | bytes 4194304 | tf_op jit(solution)/shard_map/reshape | solution.py:21
  198.8 0.0 copy-done
  198.8 6.7 %fusion = f32[1024,640]{1,0:T(8,128)} fusion(f32[1024,512]{1,0:T(8,128)S(1)} %reshape.44, f32[64,8,640]{2,1,0:T(8,128)S(1)} %copy-done), kind=kOutput, calls=%fused_computation.2 | convolution fusion | flops 4026531840 | bytes 6029312 | tf_op jit(solution)/shard_map/dot_general | solution.py:20
  205.5 0.0 copy-start.3
  205.5 0.0 all-reduce.3.cloned.1.call-update
  205.5 0.3 reduce-scatter.2.cloned.1.call-start
  205.9 0.8 dynamic_slice.3
  206.6 0.0 copy-done.3
  206.6 0.1 broadcast_xor_fusion
  206.7 0.0 copy-start.1
  206.7 0.0 copy-start.2
  206.7 2.8 copy.26
  209.5 0.0 copy-done.1
  209.5 0.0 copy-done.2
  209.5 6.7 %convolution_bitcast_fusion = f32[32,64,128]{2,1,0:T(8,128)S(1)} fusion(f32[32,32,64,8]{2,3,1,0:T(8,128)S(1)} %bitcast.33, f32[32,8,128]{2,1,0:T(8,128)S(1)} %copy-done.1, s32[128]{0:T(128)S(1)} %copy-done.2, s32[32,8]{1,0:T(8,128)S(1)} %broadcast_xor_fusion), kind=kOutput, calls=%fused_computation.1 | convolution fusion | flops 805371904 | bytes 3278336 | tf_op jit(solution)/shard_map/ikac,kcf->iaf/dot_general | solution.py:33
  216.2 2.9 copy.27
  219.1 0.0 reduce-scatter.2.cloned.1.call-update
  219.1 266.9 %all-reduce.3.cloned.1.call-done = f32[1024,640]{1,0:T(8,128)} async-done(((f32[1024,640]{1,0:T(8,128)}), f32[1024,640]{1,0:T(8,128)}) %all-reduce.3.cloned.1.call-update) | async-done | bytes 2621456
  486.0 1.3 constant_dynamic-slice_fusion
  487.3 42.5 %reduce-scatter.2.cloned.1.call-done = f32[32,64,2]{1,0,2:T(8,128)} async-done(((f32[32,64,128]{1,0,2:T(8,128)}), f32[32,64,2]{1,0,2:T(8,128)}) %reduce-scatter.2.cloned.1.call-update) | async-done | bytes 16400 | tf_op jit(solution)/shard_map/reduce_scatter | solution.py:39
  529.8 1.4 copy.28
Async XLA Ops:
  8.0 190.8 %copy-start = (f32[64,8,640]{2,1,0:T(8,128)S(1)}, f32[64,8,640]{2,1,0:T(8,128)}, u32[]{:S(2)}) copy-start(f32[64,8,640]{2,1,0:T(8,128)} %param.7) | copy-start | bytes 3932164
  8.0 478.0 %all-reduce.3.cloned.1.call-start = ((), (), s32[]{:S(2)}) async-start(), calls=%async_computation.4 | async-start | bytes 5242880
  205.5 1.1 copy-start.3
  205.5 324.2 %reduce-scatter.2.cloned.1.call-start = ((), (), s32[]{:S(2)}) async-start(), calls=%async_computation.3 | async-start | bytes 2129920 | tf_op jit(solution)/shard_map/reduce_scatter | solution.py:39
  206.7 2.8 copy-start.1
  206.7 2.8 copy-start.2
Sparse Core Ops, SparseCore 0:
  205.7 280.2 all-reduce.2
Sparse Core Ops, SparseCore 1:
  219.2 310.5 reduce-scatter.1
where the time goes:
time: 548 us; the launch traced here: 539 us
  waiting for transfers between devices  309 us (56%)
  local copies, waits for them, and re-layouts  98 us (18%)
  blocking collectives  87.4 us (16%)
  between operations  15.6 us (3%)
  other arithmetic  14.5 us (3%)
  matrix products  13.4 us (2%)
    unnamed x3, waiting for transfers between devices  267 us
    all_to_all x1, blocking collectives, body(): lax.all_to_all(amplitudes, 'row', split_axis=3, concat_axis=0, tiled=True)  58.2 us
    reduce_scatter x1, waiting for transfers between devices, body(): lax.psum_scatter(cycle_part, ('row', 'col'), scatter_dimension=2, tiled=T...  42.5 us
    unnamed x15, local copies, waits for them, and re-layouts  30.9 us
    all_to_all x1, blocking collectives, body(): lax.all_to_all(lax.all_to_all(amplitudes, 'row', split_axis=3, concat_axi...  29.2 us
    all_to_all x3, local copies, waits for them, and re-layouts, body(): lax.all_to_all(lax.all_to_all(amplitudes, 'row', split_axis=3, concat_axi...  27.3 us
    reshape x1, local copies, waits for them, and re-layouts, body(): regrouped.reshape(occ_count * occ_count, first_block * second_block)  24 us
    all_to_all x3, local copies, waits for them, and re-layouts, body(): lax.all_to_all(amplitudes, 'row', split_axis=3, concat_axis=0, tiled=True)  12.2 us
  transfers between devices with their start and end apart: 2, of which 2 were waited for; matrix products, arithmetic and copies ran while one was open for 3% of the time, Pallas kernels for 0%

commit v1 on v0

v1 whole, which is shorter than its diff:
```python
import jax
import jax.numpy as jnp
from jax import lax
from jax.experimental import pallas as pl
from jax.experimental.pallas import tpu as pltpu
from jax.sharding import Mesh, PartitionSpec as P

F32 = jnp.float32
BF16 = jnp.bfloat16
VMEM_LIMIT = 16 * 1024 * 1024


def split(v):
    hi = v.astype(BF16)
    lo = (v - hi.astype(F32)).astype(BF16)
    return hi, lo


def dot3(xh, xl, bh, bl):
    def mm(p, q):
        return jnp.dot(p, q, preferred_element_type=F32)

    return mm(xh, bh) + (mm(xh, bl) + mm(xl, bh))


def regroup_kernel(a_ref, o_ref):
    rows = a_ref.reshape(512, 128)
    lane = lax.broadcasted_iota(jnp.int32, (8, 128), 1)
    low = lane < 64
    even = (lane & 32) == 0

    def swap(keep, p, q, width):
        return (
            jnp.where(keep, p, pltpu.roll(q, width, 1)),
            jnp.where(keep, pltpu.roll(p, 128 - width, 1), q),
        )

    for q in range(16):
        v = [rows[pl.ds(4 * q + c, 8, stride=64), :] for c in range(4)]
        t0, t2 = swap(low, v[0], v[2], 64)
        t1, t3 = swap(low, v[1], v[3], 64)
        o0, o1 = swap(even, t0, t1, 32)
        o2, o3 = swap(even, t2, t3, 32)
        for g, o in enumerate((o0, o1, o2, o3)):
            o_ref[g, :, pl.ds(q * 128, 128)] = o


def regroup(amplitudes):
    a = amplitudes.reshape(4, 2, 2, 64, 512)
    return pl.pallas_call(
        regroup_kernel,
        grid=(4, 2),
        in_specs=[pl.BlockSpec((4, None, 2, 64, 128), lambda b, h: (0, h, 0, 0, b))],
        out_specs=pl.BlockSpec((4, None, 8, 2048), lambda b, h: (b, h, 0, 0)),
        out_shape=jax.ShapeDtypeStruct((16, 2, 8, 2048), F32),
        compiler_params=pltpu.CompilerParams(vmem_limit_bytes=VMEM_LIMIT),
        cost_estimate=pl.CostEstimate(flops=2**20, bytes_accessed=2**22, transcendentals=0),
    )(a)


def ladder_kernel(x_ref, b0, b1, b3, near, far, o_ref, held):
    me = lax.axis_index("x")
    for k in range(8):
        part = pl.ds(k * 8, 8)
        held[me] = b0[part]
        held[lax.rem(me + 1, 4)] = b3[part]
        held[lax.rem(me + 2, 4)] = (near if k < 4 else far)[pl.ds(k % 4 * 8, 8)]
        held[lax.rem(me + 3, 4)] = b1[part]
        lanes = pl.ds(k * 256, 256)
        x = jnp.concatenate([x_ref[:, h, :, lanes].reshape(128, 256) for h in range(2)], axis=0)
        xh, xl = split(x)
        b = jnp.concatenate([held[o, c] for c in range(8) for o in range(4)], axis=0)
        bh, bl = split(b)
        total = dot3(xh, xl, bh, bl).reshape(2, 128, 640)
        if k == 0:
            o_ref[...] = total
        else:
            o_ref[...] += total


def ladder(x, *blocks):
    return pl.pallas_call(
        ladder_kernel,
        in_specs=[pl.BlockSpec(memory_space=pltpu.VMEM)] * 6,
        out_specs=pl.BlockSpec(memory_space=pltpu.VMEM),
        out_shape=jax.ShapeDtypeStruct((2, 128, 640), F32),
        scratch_shapes=[pltpu.VMEM((4, 8, 8, 640), F32)],
        compiler_params=pltpu.CompilerParams(vmem_limit_bytes=VMEM_LIMIT),
        cost_estimate=pl.CostEstimate(
            flops=3 * 2 * 256 * 2048 * 640, bytes_accessed=8 * 2**20, transcendentals=0
        ),
    )(x, *blocks)


def cycle_kernel(occ_ref, a_ref, own_ref, other_ref, vir_ref, pair_ref, o_ref, turned):
    first = (lax.axis_index("zl") * 4 + lax.axis_index("x")) * 4
    core = lax.axis_index("core")
    total = jnp.zeros((256, 128), F32)
    for s, (half, w_ref) in enumerate(((core, own_ref), (1 - core, other_ref)) * 2):
        k = 2 * half + s // 2
        allowed = jnp.bitwise_xor(vir_ref[...], occ_ref[first + k]) == pair_ref[...]
        w = jnp.where(allowed, w_ref[:, s // 2].reshape(512, 128), 0.0)
        ah, al = split(a_ref[:, k].reshape(256, 512))
        wh, wl = split(w)
        total = total + dot3(ah, al, wh, wl)
    turned[...] = total.T
    for x in range(4):
        for d in range(16):
            o_ref[x, pl.ds(2 * d, 2), :] = turned[pl.ds(8 * d + 2 * x, 2), :]


def cycle(occ, amplitudes, own, other, vir, pair):
    return pl.pallas_call(
        cycle_kernel,
        in_specs=[pl.BlockSpec(memory_space=pltpu.SMEM)]
        + [pl.BlockSpec(memory_space=pltpu.VMEM)] * 5,
        out_specs=pl.BlockSpec(memory_space=pltpu.VMEM),
        out_shape=jax.ShapeDtypeStruct((4, 32, 256), F32),
        scratch_shapes=[pltpu.VMEM((128, 256), F32)],
        compiler_params=pltpu.CompilerParams(vmem_limit_bytes=VMEM_LIMIT),
        cost_estimate=pl.CostEstimate(
            flops=3 * 2 * 256 * 2048 * 128, bytes_accessed=3 * 2**20, transcendentals=0
        ),
    )(occ, amplitudes, own, other, vir, pair)


def pack_kernel(part_ref, c0, c1, c2, c3, o_ref, ladder_sum, cycle_sum):
    ladder_sum[...] = part_ref[0] + part_ref[1]
    cycle_sum[...] = (c0[...] + c1[...]) + (c2[...] + c3[...])
    for d in range(64):
        o_ref[d, :, pl.ds(0, 640)] = ladder_sum[pl.ds(2 * d, 2), :]
        o_ref[d, :, pl.ds(640, 256)] = cycle_sum[pl.ds(d // 4 * 2, 2), :]


def pack(part, parts):
    return pl.pallas_call(
        pack_kernel,
        out_shape=jax.ShapeDtypeStruct((64, 2, 896), F32),
        scratch_shapes=[pltpu.VMEM((128, 640), F32), pltpu.VMEM((32, 256), F32)],
        compiler_params=pltpu.CompilerParams(vmem_limit_bytes=VMEM_LIMIT),
        cost_estimate=pl.CostEstimate(flops=2**18, bytes_accessed=2**20, transcendentals=0),
    )(part, *parts)


def finish_kernel(p_ref, ladder_ref, cycle_ref):
    zh = lax.axis_index("zh")
    total = [p_ref[d, :, pl.ds(0, 640)] for d in range(8)]
    for d in range(8, 64):
        total[d % 8] += p_ref[d, :, pl.ds(0, 640)]
    while len(total) > 1:
        total = [p + q for p, q in zip(total[::2], total[1::2])]
    ladder_ref[...] = total[0]
    for y in range(8):
        cycle_ref[y] = (
            p_ref[y * 8 + zh, :, pl.ds(640, 256)] + p_ref[y * 8 + 4 + zh, :, pl.ds(640, 256)]
        )


def finish(p):
    return pl.pallas_call(
        finish_kernel,
        out_shape=[
            jax.ShapeDtypeStruct((2, 640), F32),
            jax.ShapeDtypeStruct((8, 2, 256), F32),
        ],
        compiler_params=pltpu.CompilerParams(vmem_limit_bytes=VMEM_LIMIT),
        cost_estimate=pl.CostEstimate(flops=2**17, bytes_accessed=2**19, transcendentals=0),
    )(p)


def exchange(v, axes):
    return lax.all_to_all(v, axes, split_axis=0, concat_axis=0, tiled=True)


def body(amplitudes, ladder_ints, cycle_ints, occ_irrep, vir_irrep, pair_irrep):
    w = exchange(cycle_ints.reshape(8, 4, 8, 128), ("zl", "x"))

    ring = [[(i, (i + s) % 4) for i in range(4)] for s in range(4)]
    sent = regroup(amplitudes)
    x = exchange(sent, ("y", "zl"))
    w = lax.dynamic_index_in_dim(
        w.reshape(8, 2, 2, 8, 128), lax.axis_index("core"), axis=1, keepdims=False
    )
    w = lax.all_gather(w, "y", axis=0, tiled=True)
    other = lax.ppermute(w, "core", [(0, 1), (1, 0)])
    _, ladder_ints, vir_irrep = lax.optimization_barrier((sent, ladder_ints, vir_irrep))
    b1 = lax.ppermute(ladder_ints, "x", ring[1])
    b3 = lax.ppermute(ladder_ints, "x", ring[3])
    from_b1, from_b3, w = lax.optimization_barrier((b1, b3, w))
    near = lax.ppermute(from_b1[:32], "x", ring[1])
    far = lax.ppermute(from_b3[32:], "x", ring[3])

    vir = jnp.broadcast_to(vir_irrep[:, None], (512, 128))
    parts = cycle(occ_irrep, amplitudes, w, other, vir, pair_irrep[None])
    at = lax.axis_index("x")
    parts = [
        lax.dynamic_index_in_dim(parts, lax.rem(at + s, 4), keepdims=False) for s in range(4)
    ]
    parts = parts[:1] + [lax.ppermute(parts[s], "x", ring[s]) for s in (1, 2, 3)]

    part = exchange(ladder(x, ladder_ints, b1, b3, near, far), ("core",))
    part, cycle_part = finish(exchange(pack(part, parts), ("y", "zl", "zh")))
    cycle_resid = cycle_part.reshape(8, 2, 4, 64).transpose(0, 2, 3, 1).reshape(32, 64, 2)
    move = [
        ((s * 4 + a) * 4 + hi * 2 + lo, (hi * 4 + lo * 2 + s) * 4 + a)
        for s in range(2)
        for a in range(4)
        for hi in range(2)
        for lo in range(2)
    ]
    ladder_resid = lax.ppermute(part, ("zl", "x", "zh"), move)
    return ladder_resid, cycle_resid


def solution(mesh):
    fine = Mesh(mesh.devices.reshape(8, 2, 4, 4, 2), ("y", "zl", "x", "zh", "core"))
    col, depth = ("zl", "x"), ("zh", "core")
    in_specs = (
        P("y", col, depth, None),
        P(depth, ("y", "zl", "x"), None),
        P(None, ("y", "zl", "x"), None),
        P(),
        P(),
        P(),
    )
    out_specs = (P(("y", "zl", "x", "zh", "core"), None), P(None, depth, ("y", "zl", "x")))
    return jax.shard_map(body, mesh=fine, in_specs=in_specs, out_specs=out_specs, check_vma=False)
```

time: 548 us -> 177 us (0.32); the launches traced: 539 us -> 176 us
  waiting for transfers between devices: 309 us -> 9.32 us
  local copies, waits for them, and re-layouts: 98 us -> 7.3 us
  starting transfers between devices: 0.34 us -> 48.6 us
  between operations: 15.6 us -> 0.91 us
  other arithmetic: 14.5 us -> 0 us
  Pallas kernels: 0 us -> 14.1 us
  matrix products: 13.4 us -> 0 us
  blocking collectives: 87.4 us -> 95.5 us
    unnamed x3 -> x0, waiting for transfers between devices: 267 us -> none
    all_gather x0 -> x1, blocking collectives: none -> 62.9 us  [body(): w = lax.all_gather(w, 'y', axis=0, tiled=True)]
    all_to_all x2 -> x1, blocking collectives: 87.4 us -> 32.7 us  [exchange(): return lax.all_to_all(v, axes, split_axis=0, concat_axis=0, tiled=True)]
    reduce_scatter x1 -> x0, waiting for transfers between devices: 42.5 us -> none  [body(): lax.psum_scatter(cycle_part, ('row', 'col'), scatter_dimension=2, tiled=T...]
    all_to_all x6 -> x0, local copies, waits for them, and re-layouts: 39.5 us -> none  [the longest x3 27.3 us: body(): lax.all_to_all(lax.all_to_all(amplitudes, 'row', split_axis=3, concat_axi...]
    ppermute x0 -> x9, starting transfers between devices: none -> 30.4 us  [the longest x3 8.97 us: body(): lax.ppermute(parts[s], 'x', ring[s])]
    unnamed x15 -> x13, local copies, waits for them, and re-layouts: 30.9 us -> 3.53 us
    reshape x1, local copies, waits for them, and re-layouts: 24 us -> 0.09 us  [body(): cycle_part.reshape(8, 2, 4, 64).transpose(0, 2, 3, 1).reshape(32, 64, 2)]
  transfers between devices with their start and end apart: 2 -> 12, of which waited for: 2 -> 4; matrix products, arithmetic and copies ran while one was open for 3% -> 2% of each run, Pallas kernels for 0% -> 8%
where the time goes in v1:
time: 177 us; the launch traced here: 176 us
  blocking collectives  95.5 us (54%)
  starting transfers between devices  48.6 us (27%)
  Pallas kernels  14.1 us (8%)
  waiting for transfers between devices  9.32 us (5%)
  local copies, waits for them, and re-layouts  7.3 us (4%)
    all_gather x1, blocking collectives, body(): w = lax.all_gather(w, 'y', axis=0, tiled=True)  62.9 us
    all_to_all x1, blocking collectives, exchange(): return lax.all_to_all(v, axes, split_axis=0, concat_axis=0, tiled=True)  32.7 us
    all_to_all x3, starting transfers between devices, exchange(): return lax.all_to_all(v, axes, split_axis=0, concat_axis=0, tiled=True)  18.3 us
    ppermute x3, starting transfers between devices, body(): lax.ppermute(parts[s], 'x', ring[s])  8.97 us
    pallas_call x1, Pallas kernels, ladder(): pl.pallas_call(ladder_kernel, in_specs=[pl.BlockSpec(memory_space=pltpu.V...  6.93 us
    ppermute x1, starting transfers between devices, body(): ladder_resid = lax.ppermute(part, ('zl', 'x', 'zh'), move)  5.23 us
    pallas_call x1, Pallas kernels, regroup(): pl.pallas_call(regroup_kernel, grid=(4, 2), in_specs=[pl.BlockSpec((4, No...  4.55 us
    ppermute x1, starting transfers between devices, body(): b1 = lax.ppermute(ladder_ints, 'x', ring[1])  4.29 us
  transfers between devices with their start and end apart: 12, of which 4 were waited for; matrix products, arithmetic and copies ran while one was open for 2% of the time, Pallas kernels for 8%

profile of v1, /device:TPU:6, one launch (start us, length us, event | category | flops | bytes accessed | tf_op | source)
XLA Modules:
  0.0 175.8 jit_solution(2269637425374058221)
XLA Ops:
  0.6 9.1 %all-to-all-start.1 = ((f32[8,4,8,128]{3,2,1,0:T(8,128)}), f32[8,4,8,128]{3,2,1,0:T(8,128)S(1)}, u32[]{:S(2)}, u32[]{:S(2)}) async-start(f32[8,4,8,128]{3,2,1,0:T(8,128)} %bitcast.18), calls=%async_computation.1 | async-start | bytes 262144 | tf_op jit(solution)/shard_map/all_to_all | solution.py:172
  9.8 0.0 copy-start
  9.8 1.6 copy-done
  11.4 4.5 %shard_map.77 = f32[16,2,8,2048]{3,2,1,0:T(8,128)} custom-call(f32[4,2,2,64,512]{4,3,2,1,0:T(8,128)S(1)} %bitcast.15), custom_call_target="tpu_custom_call" | custom-call | flops 1048576 | bytes 4194304 | tf_op jit(solution)/shard_map/pallas_call | solution.py:50
  15.9 0.0 all-to-all-done.1
  15.9 5.6 %all-to-all-start = ((f32[16,2,8,2048]{3,2,1,0:T(8,128)}), f32[16,2,8,2048]{3,2,1,0:T(8,128)}, u32[]{:S(2)}, u32[]{:S(2)}) async-start(f32[16,2,8,2048]{3,2,1,0:T(8,128)} %shard_map.77), calls=%async_computation | async-start | bytes 4194304 | tf_op jit(solution)/shard_map/all_to_all | solution.py:172
  21.5 0.0 copy-start.5
  21.5 0.0 copy-start.1
  21.6 0.0 copy-start.3
  21.6 0.0 copy-start.4
  21.6 2.9 %collective-permute-start.1 = (f32[64,8,640]{2,1,0:T(8,128)}, f32[64,8,640]{2,1,0:T(8,128)S(1)}, u32[]{:S(2)}, u32[]{:S(2)}) collective-permute-start(f32[64,8,640]{2,1,0:T(8,128)} %b0), channel_id=1, source_target_pairs={{0,24},{8,0},{16,8},{24,16},{1,25},{9,1},{17,9},{25,17},{2,26},{10... | collective-permute-start | bytes 3932168 | tf_op jit(solution)/shard_map/ppermute | solution.py:188
  24.5 4.3 %collective-permute-start = (f32[64,8,640]{2,1,0:T(8,128)}, f32[64,8,640]{2,1,0:T(8,128)}, u32[]{:S(2)}, u32[]{:S(2)}) collective-permute-start(f32[64,8,640]{2,1,0:T(8,128)} %b0), channel_id=1, source_target_pairs={{0,8},{8,16},{16,24},{24,0},{1,9},{9,17},{17,25},{25,1},{2,10},{10... | collective-permute-start | bytes 3932168 | tf_op jit(solution)/shard_map/ppermute | solution.py:187
  28.8 62.9 %all-gather = f32[64,1,2,8,128]{4,3,2,1,0:T(8,128)} all-gather(f32[8,1,2,8,128]{4,3,2,1,0:T(8,128)S(1)} %constant_dynamic-slice_fusion), channel_id=2, replica_groups=mesh['y'=8,'zl'=2,'x'=4,'zh'=4,'core'=2] {'y'}, dimensions={0}, use_global_device_ids=true | all-gather | bytes 589824 | tf_op jit(solution)/shard_map/all_gather | solution.py:184
  91.7 1.9 %collective-permute-start.4 = (f32[64,2,8,128]{3,2,1,0:T(8,128)}, f32[64,2,8,128]{3,2,1,0:T(8,128)}, u32[]{:S(2)}, u32[]{:S(2)}) collective-permute-start(f32[64,2,8,128]{3,2,1,0:T(8,128)} %bitcast.3.own_ref), channel_id=1, source_target_pairs={{0,1},{1,0},{2,3},{3,2},{4,5},{5,4},{6,7},{7,6},{8,9},{9,8},{10,11... | collective-permute-start | bytes 1572872 | tf_op jit(solution)/shard_map/ppermute | solution.py:185
  93.6 0.0 collective-permute-done.1.b3
  93.6 0.0 collective-permute-done.b1
  93.6 2.0 %slice.6 = f32[32,8,640]{2,1,0:T(8,128)} slice(f32[64,8,640]{2,1,0:T(8,128)} %collective-permute-done.b1), slice={[0:32], [0:8], [0:640]} | slice | bytes 1310720 | tf_op jit(solution)/shard_map/slice | solution.py:190
  95.6 0.9 slice.7
  96.5 2.8 %collective-permute-start.3 = (f32[32,8,640]{2,1,0:T(8,128)}, f32[32,8,640]{2,1,0:T(8,128)}, u32[]{:S(2)}, u32[]{:S(2)}) collective-permute-start(f32[32,8,640]{2,1,0:T(8,128)} %slice.7), channel_id=1, source_target_pairs={{0,24},{8,0},{16,8},{24,16},{1,25},{9,1},{17,9},{25,17},{2,26},{10... | collective-permute-start | bytes 1966088 | tf_op jit(solution)/shard_map/ppermute | solution.py:191
  99.3 4.3 %collective-permute-start.2 = (f32[32,8,640]{2,1,0:T(8,128)}, f32[32,8,640]{2,1,0:T(8,128)}, u32[]{:S(2)}, u32[]{:S(2)}) collective-permute-start(f32[32,8,640]{2,1,0:T(8,128)} %slice.6), channel_id=1, source_target_pairs={{0,8},{8,16},{16,24},{24,0},{1,9},{9,17},{17,25},{25,1},{2,10},{10... | collective-permute-start | bytes 1966088 | tf_op jit(solution)/shard_map/ppermute | solution.py:190
  103.6 0.0 collective-permute-done.4.other_ref
  103.6 0.0 copy-done.5
  103.6 0.1 broadcast_in_dim.4.vir_ref
  103.8 0.0 copy-done.1
  103.8 0.0 copy-done.3
  103.8 0.0 copy-done.4
  103.8 2.5 %shard_map.79 = f32[4,32,256]{2,1,0:T(8,128)S(1)} custom-call(s32[32]{0:T(128)S(1)} %copy-done.3, f32[4,4,64,512]{3,2,1,0:T(8,128)S(1)} %copy-done.1, f32[64,2,8,128]{3,2,1,0:T(8,128)} %bitcast.3.own_ref, f32[64,2,8,128]{3,2,1,0:T(8,128)} %collective-permute-done.4.other_ref, s32[512,128]{1,0:T(8,128)S(1)} %broadcast_in_dim.4.vir_ref, s32[1,128]{1,0:T(1,128)S(1)} %bitcast.16), custom_call_target="tpu_custom_call" | custom-call | flops 402653184 | bytes 3145728 | tf_op jit(solution)/shard_map/pallas_call | solution.py:113
  106.3 1.9 %collective-permute-start.7 = (f32[32,256]{1,0:T(8,128)S(1)}, f32[32,256]{1,0:T(8,128)S(1)}, u32[]{:S(2)}, u32[]{:S(2)}) collective-permute-start(f32[32,256]{1,0:T(8,128)S(1)} %get-tuple-element.16), channel_id=1, source_target_pairs={{0,24},{8,0},{16,8},{24,16},{1,25},{9,1},{17,9},{25,17},{2,26},{10... | collective-permute-start | bytes 98312 | tf_op jit(solution)/shard_map/ppermute | solution.py:199
  108.2 3.4 %collective-permute-start.6 = (f32[32,256]{1,0:T(8,128)S(1)}, f32[32,256]{1,0:T(8,128)S(1)}, u32[]{:S(2)}, u32[]{:S(2)}) collective-permute-start(f32[32,256]{1,0:T(8,128)S(1)} %get-tuple-element.17), channel_id=1, source_target_pairs={{0,16},{8,24},{16,0},{24,8},{1,17},{9,25},{17,1},{25,9},{2,18},{10... | collective-permute-start | bytes 98312 | tf_op jit(solution)/shard_map/ppermute | solution.py:199
  111.6 3.7 %collective-permute-start.5 = (f32[32,256]{1,0:T(8,128)S(1)}, f32[32,256]{1,0:T(8,128)S(1)}, u32[]{:S(2)}, u32[]{:S(2)}) collective-permute-start(f32[32,256]{1,0:T(8,128)S(1)} %get-tuple-element.18), channel_id=1, source_target_pairs={{0,8},{8,16},{16,24},{24,0},{1,9},{9,17},{17,25},{25,1},{2,10},{10... | collective-permute-start | bytes 98312 | tf_op jit(solution)/shard_map/ppermute | solution.py:199
  115.3 2.8 %collective-permute-done.3.far = f32[32,8,640]{2,1,0:T(8,128)} collective-permute-done((f32[32,8,640]{2,1,0:T(8,128)}, f32[32,8,640]{2,1,0:T(8,128)}, u32[]{:S(2)}, u32[]{:S(2)}) %collective-permute-start.3) | collective-permute-done | bytes 655392 | tf_op jit(solution)/shard_map/ppermute | solution.py:191
  118.1 1.2 collective-permute-done.2.near
  119.3 0.0 all-to-all-done.x_ref
  119.3 0.0 copy-start.2
  119.3 1.3 copy-done.2
  120.7 6.9 %shard_map.78 = f32[2,128,640]{2,1,0:T(8,128)} custom-call(f32[16,2,8,2048]{3,2,1,0:T(8,128)} %all-to-all-done.x_ref, f32[64,8,640]{2,1,0:T(8,128)S(1)} %copy-done.2, f32[64,8,640]{2,1,0:T(8,128)} %collective-permute-done.b1, f32[64,8,640]{2,1,0:T(8,128)S(1)} %collective-permute-done.1.b3, f32[32,8,640]{2,1,0:T(8,128)} %collective-permute-done.2.near, ...), custom_call_target="tpu_custom_call" | custom-call | flops 2013265920 | bytes 8388608 | tf_op jit(solution)/shard_map/pallas_call | solution.py:82
  127.6 3.5 %all-to-all-start.2 = ((f32[2,128,640]{2,1,0:T(8,128)}), f32[2,128,640]{2,1,0:T(8,128)S(1)}, u32[]{:S(2)}, u32[]{:S(2)}) async-start(f32[2,128,640]{2,1,0:T(8,128)} %shard_map.78), calls=%async_computation.2 | async-start | bytes 1310720 | tf_op jit(solution)/shard_map/all_to_all | solution.py:172
  131.1 0.0 collective-permute-done.7.c3
  131.1 0.0 collective-permute-done.6.c2
  131.1 0.0 collective-permute-done.5.c1
  131.1 1.8 %all-to-all-done.2.part_ref = f32[2,128,640]{2,1,0:T(8,128)S(1)} async-done(((f32[2,128,640]{2,1,0:T(8,128)}), f32[2,128,640]{2,1,0:T(8,128)S(1)}, u32[]{:S(2)}, u32[]{:S(2)}) %all-to-all-start.2) | async-done | bytes 655392 | tf_op jit(solution)/shard_map/all_to_all | solution.py:172
  132.9 0.2 shard_map.80
  133.1 32.7 %all_to_all.20.p_ref = f32[64,2,896]{2,1,0:T(2,128)S(1)} all-to-all(f32[64,2,896]{2,1,0:T(2,128)S(1)} %shard_map.80), channel_id=1, replica_groups=mesh['y'=8,'zl'=2,'x'=4,'zh'=4,'core'=2] {'y','zl','zh'}, dimensions={0} | all-to-all | bytes 917504 | tf_op jit(solution)/shard_map/all_to_all | solution.py:172
  165.8 5.2 %collective-permute-start.8 = (f32[2,640]{1,0:T(2,128)S(1)}, f32[2,640]{1,0:T(2,128)S(1)}, u32[]{:S(2)}, u32[]{:S(2)}) collective-permute-start(f32[2,640]{1,0:T(2,128)S(1)} %get-tuple-element.14), channel_id=1, source_target_pairs={{0,0},{2,16},{4,32},{6,48},{8,2},{10,18},{12,34},{14,50},{16,4},{1... | collective-permute-start | bytes 15368 | tf_op jit(solution)/shard_map/ppermute | solution.py:211
  171.0 0.1 reshape.23
  171.1 0.6 copy.11
  171.7 3.5 %collective-permute-done.8 = f32[2,640]{1,0:T(2,128)S(1)} collective-permute-done((f32[2,640]{1,0:T(2,128)S(1)}, f32[2,640]{1,0:T(2,128)S(1)}, u32[]{:S(2)}, u32[]{:S(2)}) %collective-permute-start.8) | collective-permute-done | bytes 5152 | tf_op jit(solution)/shard_map/ppermute | solution.py:211
  175.2 0.6 copy.13
  (3 shorter events, 0.1 us)
Async XLA Ops:
  0.6 15.3 %all-to-all-start.1 = ((f32[8,4,8,128]{3,2,1,0:T(8,128)}), f32[8,4,8,128]{3,2,1,0:T(8,128)S(1)}, u32[]{:S(2)}, u32[]{:S(2)}) async-start(f32[8,4,8,128]{3,2,1,0:T(8,128)} %bitcast.18), calls=%async_computation.1 | async-start | bytes 262144 | tf_op jit(solution)/shard_map/all_to_all | solution.py:172
  9.8 1.6 copy-start
  15.9 103.4 %all-to-all-start = ((f32[16,2,8,2048]{3,2,1,0:T(8,128)}), f32[16,2,8,2048]{3,2,1,0:T(8,128)}, u32[]{:S(2)}, u32[]{:S(2)}) async-start(f32[16,2,8,2048]{3,2,1,0:T(8,128)} %shard_map.77), calls=%async_computation | async-start | bytes 4194304 | tf_op jit(solution)/shard_map/all_to_all | solution.py:172
  21.5 82.1 %copy-start.5 = (s32[512]{0:T(512)S(1)}, s32[512]{0:T(512)}, u32[]{:S(2)}) copy-start(s32[512]{0:T(512)} %param.10) | copy-start | bytes 6148
  21.5 82.2 %copy-start.1 = (f32[4,4,64,512]{3,2,1,0:T(8,128)S(1)}, f32[4,4,64,512]{3,2,1,0:T(8,128)}, u32[]{:S(2)}) copy-start(f32[4,4,64,512]{3,2,1,0:T(8,128)} %a_ref.1) | copy-start | bytes 6291460
  21.6 82.2 %copy-start.3 = (s32[32]{0:T(128)S(1)}, s32[32]{0:T(128)}, u32[]{:S(2)}) copy-start(s32[32]{0:T(128)} %occ_ref.1) | copy-start | bytes 388
  21.6 82.2 %copy-start.4 = (s32[128]{0:T(128)S(1)}, s32[128]{0:T(128)}, u32[]{:S(2)}) copy-start(s32[128]{0:T(128)} %param.11) | copy-start | bytes 1540
  21.6 72.0 %collective-permute-start.1 = (f32[64,8,640]{2,1,0:T(8,128)}, f32[64,8,640]{2,1,0:T(8,128)S(1)}, u32[]{:S(2)}, u32[]{:S(2)}) collective-permute-start(f32[64,8,640]{2,1,0:T(8,128)} %b0), channel_id=1, source_target_pairs={{0,24},{8,0},{16,8},{24,16},{1,25},{9,1},{17,9},{25,17},{2,26},{10... | collective-permute-start | bytes 3932168 | tf_op jit(solution)/shard_map/ppermute | solution.py:188
  24.5 69.1 %collective-permute-start = (f32[64,8,640]{2,1,0:T(8,128)}, f32[64,8,640]{2,1,0:T(8,128)}, u32[]{:S(2)}, u32[]{:S(2)}) collective-permute-start(f32[64,8,640]{2,1,0:T(8,128)} %b0), channel_id=1, source_target_pairs={{0,8},{8,16},{16,24},{24,0},{1,9},{9,17},{17,25},{25,1},{2,10},{10... | collective-permute-start | bytes 3932168 | tf_op jit(solution)/shard_map/ppermute | solution.py:187
  91.7 11.9 %collective-permute-start.4 = (f32[64,2,8,128]{3,2,1,0:T(8,128)}, f32[64,2,8,128]{3,2,1,0:T(8,128)}, u32[]{:S(2)}, u32[]{:S(2)}) collective-permute-start(f32[64,2,8,128]{3,2,1,0:T(8,128)} %bitcast.3.own_ref), channel_id=1, source_target_pairs={{0,1},{1,0},{2,3},{3,2},{4,5},{5,4},{6,7},{7,6},{8,9},{9,8},{10,11... | collective-permute-start | bytes 1572872 | tf_op jit(solution)/shard_map/ppermute | solution.py:185
  96.5 21.6 %collective-permute-start.3 = (f32[32,8,640]{2,1,0:T(8,128)}, f32[32,8,640]{2,1,0:T(8,128)}, u32[]{:S(2)}, u32[]{:S(2)}) collective-permute-start(f32[32,8,640]{2,1,0:T(8,128)} %slice.7), channel_id=1, source_target_pairs={{0,24},{8,0},{16,8},{24,16},{1,25},{9,1},{17,9},{25,17},{2,26},{10... | collective-permute-start | bytes 1966088 | tf_op jit(solution)/shard_map/ppermute | solution.py:191
  99.3 20.1 %collective-permute-start.2 = (f32[32,8,640]{2,1,0:T(8,128)}, f32[32,8,640]{2,1,0:T(8,128)}, u32[]{:S(2)}, u32[]{:S(2)}) collective-permute-start(f32[32,8,640]{2,1,0:T(8,128)} %slice.6), channel_id=1, source_target_pairs={{0,8},{8,16},{16,24},{24,0},{1,9},{9,17},{17,25},{25,1},{2,10},{10... | collective-permute-start | bytes 1966088 | tf_op jit(solution)/shard_map/ppermute | solution.py:190
  106.3 24.8 %collective-permute-start.7 = (f32[32,256]{1,0:T(8,128)S(1)}, f32[32,256]{1,0:T(8,128)S(1)}, u32[]{:S(2)}, u32[]{:S(2)}) collective-permute-start(f32[32,256]{1,0:T(8,128)S(1)} %get-tuple-element.16), channel_id=1, source_target_pairs={{0,24},{8,0},{16,8},{24,16},{1,25},{9,1},{17,9},{25,17},{2,26},{10... | collective-permute-start | bytes 98312 | tf_op jit(solution)/shard_map/ppermute | solution.py:199
  108.2 22.9 %collective-permute-start.6 = (f32[32,256]{1,0:T(8,128)S(1)}, f32[32,256]{1,0:T(8,128)S(1)}, u32[]{:S(2)}, u32[]{:S(2)}) collective-permute-start(f32[32,256]{1,0:T(8,128)S(1)} %get-tuple-element.17), channel_id=1, source_target_pairs={{0,16},{8,24},{16,0},{24,8},{1,17},{9,25},{17,1},{25,9},{2,18},{10... | collective-permute-start | bytes 98312 | tf_op jit(solution)/shard_map/ppermute | solution.py:199
  111.6 19.6 %collective-permute-start.5 = (f32[32,256]{1,0:T(8,128)S(1)}, f32[32,256]{1,0:T(8,128)S(1)}, u32[]{:S(2)}, u32[]{:S(2)}) collective-permute-start(f32[32,256]{1,0:T(8,128)S(1)} %get-tuple-element.18), channel_id=1, source_target_pairs={{0,8},{8,16},{16,24},{24,0},{1,9},{9,17},{17,25},{25,1},{2,10},{10... | collective-permute-start | bytes 98312 | tf_op jit(solution)/shard_map/ppermute | solution.py:199
  119.3 1.3 copy-start.2
  127.6 5.3 %all-to-all-start.2 = ((f32[2,128,640]{2,1,0:T(8,128)}), f32[2,128,640]{2,1,0:T(8,128)S(1)}, u32[]{:S(2)}, u32[]{:S(2)}) async-start(f32[2,128,640]{2,1,0:T(8,128)} %shard_map.78), calls=%async_computation.2 | async-start | bytes 1310720 | tf_op jit(solution)/shard_map/all_to_all | solution.py:172
  165.8 9.4 %collective-permute-start.8 = (f32[2,640]{1,0:T(2,128)S(1)}, f32[2,640]{1,0:T(2,128)S(1)}, u32[]{:S(2)}, u32[]{:S(2)}) collective-permute-start(f32[2,640]{1,0:T(2,128)S(1)} %get-tuple-element.14), channel_id=1, source_target_pairs={{0,0},{2,16},{4,32},{6,48},{8,2},{10,18},{12,34},{14,50},{16,4},{1... | collective-permute-start | bytes 15368 | tf_op jit(solution)/shard_map/ppermute | solution.py:211

commit v2 on v1

v2 whole, which is shorter than its diff:
```python
import jax
import jax.numpy as jnp
from jax import lax
from jax.experimental import pallas as pl
from jax.experimental.pallas import tpu as pltpu
from jax.sharding import Mesh, PartitionSpec as P

F32 = jnp.float32
BF16 = jnp.bfloat16
VMEM_LIMIT = 16 * 1024 * 1024


def split(v):
    hi = v.astype(BF16)
    lo = (v - hi.astype(F32)).astype(BF16)
    return hi, lo


def dot3(xh, xl, bh, bl):
    def mm(p, q):
        return jnp.dot(p, q, preferred_element_type=F32)

    return mm(xh, bh) + (mm(xh, bl) + mm(xl, bh))


def regroup_kernel(a_ref, o_ref):
    rows = a_ref.reshape(512, 128)
    lane = lax.broadcasted_iota(jnp.int32, (8, 128), 1)
    low = lane < 64
    even = (lane & 32) == 0

    def swap(keep, p, q, width):
        return (
            jnp.where(keep, p, pltpu.roll(q, width, 1)),
            jnp.where(keep, pltpu.roll(p, 128 - width, 1), q),
        )

    for q in range(16):
        v = [rows[pl.ds(4 * q + c, 8, stride=64), :] for c in range(4)]
        t0, t2 = swap(low, v[0], v[2], 64)
        t1, t3 = swap(low, v[1], v[3], 64)
        o0, o1 = swap(even, t0, t1, 32)
        o2, o3 = swap(even, t2, t3, 32)
        for g, o in enumerate((o0, o1, o2, o3)):
            o_ref[g, :, pl.ds(q * 128, 128)] = o


def regroup(amplitudes):
    a = amplitudes.reshape(4, 2, 2, 64, 512)
    return pl.pallas_call(
        regroup_kernel,
        grid=(4, 2),
        in_specs=[pl.BlockSpec((4, None, 2, 64, 128), lambda b, h: (0, h, 0, 0, b))],
        out_specs=pl.BlockSpec((4, None, 8, 2048), lambda b, h: (b, h, 0, 0)),
        out_shape=jax.ShapeDtypeStruct((16, 2, 8, 2048), F32),
        compiler_params=pltpu.CompilerParams(vmem_limit_bytes=VMEM_LIMIT),
        cost_estimate=pl.CostEstimate(flops=2**20, bytes_accessed=2**22, transcendentals=0),
    )(a)


def ladder_kernel(x_ref, b1, b3, b0, near, far, o_ref, held, sems):
    me = lax.axis_index("x")

    def copies(k):
        part = pl.ds(k * 16, 16)
        across = (near if k < 2 else far).at[pl.ds(k % 2 * 16, 16)]
        return (
            pltpu.make_async_copy(b0.at[part], held.at[me, part], sems.at[0, k]),
            pltpu.make_async_copy(across, held.at[lax.rem(me + 2, 4), part], sems.at[1, k]),
        )

    for k in range(4):
        for copy in copies(k):
            copy.start()
    for k in range(4):
        part = pl.ds(k * 16, 16)
        held[lax.rem(me + 1, 4), part] = b3[part]
        held[lax.rem(me + 3, 4), part] = b1[part]
        span = pl.ds(k * 512, 512)
        x = jnp.concatenate([x_ref[:, h, :, span].reshape(128, 512) for h in range(2)], axis=0)
        xh, xl = split(x)
        for copy in copies(k):
            copy.wait()
        b = [held[o, k * 16 + c] for c in range(16) for o in range(4)]
        bh, bl = split(jnp.concatenate(b, axis=0))
        total = dot3(xh, xl, bh, bl).reshape(2, 128, 640)
        if k == 0:
            o_ref[...] = total
        else:
            o_ref[...] += total


VMEM = pl.BlockSpec(memory_space=pltpu.VMEM)


def small(kernel, out_shape, *args, scratch=()):
    return pl.pallas_call(
        kernel,
        in_specs=[VMEM] * len(args),
        out_specs=VMEM if isinstance(out_shape, tuple) else [VMEM] * len(out_shape),
        out_shape=jax.ShapeDtypeStruct(out_shape, F32)
        if isinstance(out_shape, tuple)
        else [jax.ShapeDtypeStruct(shape, F32) for shape in out_shape],
        scratch_shapes=[pltpu.VMEM(shape, F32) for shape in scratch],
        compiler_params=pltpu.CompilerParams(vmem_limit_bytes=VMEM_LIMIT),
        cost_estimate=pl.CostEstimate(flops=2**18, bytes_accessed=2**20, transcendentals=0),
    )(*args)


def ladder(x, b0, b1, b3, near, far):
    anywhere = pl.BlockSpec(memory_space=pl.ANY)
    return pl.pallas_call(
        ladder_kernel,
        in_specs=[VMEM] * 3 + [anywhere] * 3,
        out_specs=VMEM,
        out_shape=jax.ShapeDtypeStruct((2, 128, 640), F32),
        scratch_shapes=[pltpu.VMEM((4, 64, 8, 640), F32), pltpu.SemaphoreType.DMA((2, 4))],
        compiler_params=pltpu.CompilerParams(vmem_limit_bytes=50 * 1024 * 1024),
        cost_estimate=pl.CostEstimate(
            flops=3 * 2 * 256 * 2048 * 640, bytes_accessed=8 * 2**20, transcendentals=0
        ),
    )(x, b1, b3, b0, near, far)


def cores_kernel(p_ref, o_ref, total):
    total[...] = p_ref[0] + p_ref[1]
    for y in range(8):
        for d in range(8):
            o_ref[d, y] = total[pl.ds(16 * y + 2 * d, 2), :]


def depth_kernel(p_ref, o_ref):
    for y in range(8):
        p = [p_ref[s, y] for s in range(8)]
        o_ref[y] = ((p[0] + p[1]) + (p[2] + p[3])) + ((p[4] + p[5]) + (p[6] + p[7]))


def pack_kernel(l_ref, c_ref, o_ref):
    for y in range(8):
        p = [c_ref[s, y] for s in range(8)]
        o_ref[y, :, pl.ds(0, 640)] = l_ref[y]
        o_ref[y, :, pl.ds(640, 256)] = ((p[0] + p[1]) + (p[2] + p[3])) + (
            (p[4] + p[5]) + (p[6] + p[7])
        )


def finish_kernel(p_ref, ladder_ref, cycle_ref):
    p = [p_ref[y, :, pl.ds(0, 640)] for y in range(8)]
    ladder_ref[...] = ((p[0] + p[1]) + (p[2] + p[3])) + ((p[4] + p[5]) + (p[6] + p[7]))
    cycle_ref[...] = p_ref[:, :, pl.ds(640, 256)]


def cycle_kernel(occ_ref, a_ref, w_ref, vir_ref, pair_ref, o_ref, turned):
    first = (lax.axis_index("zl") * 4 + lax.axis_index("x")) * 4
    total = jnp.zeros((256, 128), F32)
    for k in range(4):
        allowed = jnp.bitwise_xor(vir_ref[...], occ_ref[first + k]) == pair_ref[...]
        w = jnp.where(allowed, w_ref[:, k].reshape(512, 128), 0.0)
        ah, al = split(a_ref[:, k].reshape(256, 512))
        wh, wl = split(w)
        total = total + dot3(ah, al, wh, wl)
    turned[...] = total.T
    for col in range(8):
        for y in range(8):
            o_ref[col, y] = turned[pl.ds(16 * y + 2 * col, 2), :]


def cycle(occ, amplitudes, w, vir, pair):
    return pl.pallas_call(
        cycle_kernel,
        in_specs=[pl.BlockSpec(memory_space=pltpu.SMEM)] + [VMEM] * 4,
        out_specs=VMEM,
        out_shape=jax.ShapeDtypeStruct((8, 8, 2, 256), F32),
        scratch_shapes=[pltpu.VMEM((128, 256), F32)],
        compiler_params=pltpu.CompilerParams(vmem_limit_bytes=VMEM_LIMIT),
        cost_estimate=pl.CostEstimate(
            flops=3 * 2 * 256 * 2048 * 128, bytes_accessed=3 * 2**20, transcendentals=0
        ),
    )(occ, amplitudes, w, vir, pair)


def exchange(v, axes):
    return lax.all_to_all(v, axes, split_axis=0, concat_axis=0, tiled=True)


def body(amplitudes, ladder_ints, cycle_ints, occ_irrep, vir_irrep, pair_irrep):
    w = exchange(cycle_ints.reshape(8, 4, 8, 128), ("zl", "x"))

    ring = [[(i, (i + s) % 4) for i in range(4)] for s in range(4)]
    sent = regroup(amplitudes)
    x = exchange(sent, ("y", "zl"))
    w = lax.all_gather(w, "y", axis=0, tiled=True)
    _, ladder_ints, vir_irrep = lax.optimization_barrier((sent, ladder_ints, vir_irrep))
    b1 = lax.ppermute(ladder_ints, "x", ring[1])
    b3 = lax.ppermute(ladder_ints, "x", ring[3])
    near = lax.ppermute(b1[:32], "x", ring[1])
    far = lax.ppermute(b3[32:], "x", ring[3])
    part = exchange(ladder(x, ladder_ints, b1, b3, near, far), ("core",))
    part = small(cores_kernel, (8, 8, 2, 640), part, scratch=[(128, 640)])

    vir = jnp.broadcast_to(vir_irrep[:, None], (512, 128))
    _, late = lax.optimization_barrier((part, w))
    cycle_part = cycle(occ_irrep, amplitudes, late, vir, pair_irrep[None])
    part = small(depth_kernel, (8, 2, 640), exchange(part, ("zl", "zh")))
    _, cycle_part = lax.optimization_barrier((part, cycle_part))
    move = [
        ((s * 4 + a) * 4 + hi * 2 + lo, (hi * 4 + lo * 2 + s) * 4 + a)
        for s in range(2)
        for a in range(4)
        for hi in range(2)
        for lo in range(2)
    ]
    part = lax.ppermute(part, ("zl", "x", "zh"), move)
    cycle_part = exchange(cycle_part, ("zl", "x"))
    both = exchange(small(pack_kernel, (8, 2, 896), part, cycle_part), ("y",))
    ladder_resid, cycle_part = small(finish_kernel, [(2, 640), (8, 2, 256)], both)
    cycle_resid = cycle_part.reshape(8, 2, 4, 64).transpose(0, 2, 3, 1).reshape(32, 64, 2)
    return ladder_resid, cycle_resid


def solution(mesh):
    fine = Mesh(mesh.devices.reshape(8, 2, 4, 4, 2), ("y", "zl", "x", "zh", "core"))
    col, depth = ("zl", "x"), ("zh", "core")
    in_specs = (
        P("y", col, depth, None),
        P(depth, ("y", "zl", "x"), None),
        P(None, ("y", "zl", "x"), None),
        P(),
        P(),
        P(),
    )
    out_specs = (P(("y", "zl", "x", "zh", "core"), None), P(None, depth, ("y", "zl", "x")))
    return jax.shard_map(body, mesh=fine, in_specs=in_specs, out_specs=out_specs, check_vma=False)
```

time: 177 us -> 158 us (0.89)
  blocking collectives: 95.5 us -> 17 us
  waiting for transfers between devices: 9.32 us -> 58.1 us
  between operations: 0.91 us -> 14.2 us
  starting transfers between devices: 48.6 us -> 46.7 us
  local copies, waits for them, and re-layouts: 7.3 us -> 5.5 us
    all_gather x1 -> x0, blocking collectives: 62.9 us -> none  [body(): w = lax.all_gather(w, 'y', axis=0, tiled=True)]
    ppermute x1, waiting for transfers between devices: 0.01 us -> 25.9 us  [body(): b1 = lax.ppermute(ladder_ints, 'x', ring[1])]
    ppermute x7 -> x3, waiting for transfers between devices: 7.52 us -> 23.8 us  [the longest x1 9.7 us: body(): near = lax.ppermute(b1[:32], 'x', ring[1])]
    all_to_all x1 -> x2, blocking collectives: 32.7 us -> 17 us  [exchange(): return lax.all_to_all(v, axes, split_axis=0, concat_axis=0, tiled=True)]
    ppermute x7 -> x3, starting transfers between devices: 23.2 us -> 7.75 us  [the longest x1 3.68 us: body(): near = lax.ppermute(b1[:32], 'x', ring[1])]
    all_to_all x3 -> x4, starting transfers between devices: 18.3 us -> 33 us  [exchange(): return lax.all_to_all(v, axes, split_axis=0, concat_axis=0, tiled=True)]
    all_to_all x3 -> x4, waiting for transfers between devices: 1.79 us -> 8.43 us  [exchange(): return lax.all_to_all(v, axes, split_axis=0, concat_axis=0, tiled=True)]
    slice x2, local copies, waits for them, and re-layouts: 2.89 us -> 0.09 us  [the longest x1 0.04 us: body(): far = lax.ppermute(b3[32:], 'x', ring[3])]
  transfers between devices with their start and end apart: 12 -> 10, of which waited for: 4 -> 6; matrix products, arithmetic and copies ran while one was open for 2% -> 0% of each run, Pallas kernels for 8% -> 9%
where the time goes in v2:
time: 158 us; the launch traced here: 157 us
  waiting for transfers between devices  58.1 us (37%)
  starting transfers between devices  46.7 us (30%)
  blocking collectives  17 us (11%)
  Pallas kernels  15.1 us (10%)
  between operations  14.2 us (9%)
  local copies, waits for them, and re-layouts  5.5 us (3%)
    all_to_all x4, starting transfers between devices, exchange(): return lax.all_to_all(v, axes, split_axis=0, concat_axis=0, tiled=True)  33 us
    ppermute x1, waiting for transfers between devices, body(): b1 = lax.ppermute(ladder_ints, 'x', ring[1])  25.9 us
    all_to_all x2, blocking collectives, exchange(): return lax.all_to_all(v, axes, split_axis=0, concat_axis=0, tiled=True)  17 us
    ppermute x1, waiting for transfers between devices, body(): near = lax.ppermute(b1[:32], 'x', ring[1])  9.7 us
    all_to_all x4, waiting for transfers between devices, exchange(): return lax.all_to_all(v, axes, split_axis=0, concat_axis=0, tiled=True)  8.43 us
    ppermute x1, waiting for transfers between devices, body(): part = lax.ppermute(part, ('zl', 'x', 'zh'), move)  8.31 us
    pallas_call x1, Pallas kernels, ladder(): pl.pallas_call(ladder_kernel, in_specs=[VMEM] * 3 + [anywhere] * 3, out_s...  6.61 us
    ppermute x1, waiting for transfers between devices, body(): far = lax.ppermute(b3[32:], 'x', ring[3])  5.76 us
  transfers between devices with their start and end apart: 10, of which 6 were waited for; matrix products, arithmetic and copies ran while one was open for 0% of the time, Pallas kernels for 9%

profile of v2, /device:TPU:6, one launch (start us, length us, event | category | flops | bytes accessed | tf_op | source)
XLA Modules:
  0.0 156.7 jit_solution(817765652400705670)
XLA Ops:
  7.2 9.1 %all-to-all-start.3 = ((f32[8,4,8,128]{3,2,1,0:T(8,128)}), f32[8,4,8,128]{3,2,1,0:T(8,128)S(1)}, u32[]{:S(2)}, u32[]{:S(2)}) async-start(f32[8,4,8,128]{3,2,1,0:T(8,128)} %bitcast.7), calls=%async_computation.3 | async-start | bytes 262144 | tf_op jit(solution)/shard_map/all_to_all | solution.py:183
  16.3 0.0 copy-start
  16.3 1.6 %copy-done = f32[4,4,64,512]{3,2,1,0:T(8,128)S(1)} copy-done((f32[4,4,64,512]{3,2,1,0:T(8,128)S(1)}, f32[4,4,64,512]{3,2,1,0:T(8,128)}, u32[]{:S(2)}) %copy-start) | copy-done | bytes 2097176
  17.9 4.6 %shard_map.77 = f32[16,2,8,2048]{3,2,1,0:T(8,128)} custom-call(f32[4,2,2,64,512]{4,3,2,1,0:T(8,128)S(1)} %bitcast.5), custom_call_target="tpu_custom_call" | custom-call | flops 1048576 | bytes 4194304 | tf_op jit(solution)/shard_map/pallas_call | solution.py:50
  22.5 0.0 all-to-all-done.3
  22.5 0.0 copy-start.6
  22.5 0.7 copy-done.6
  23.1 5.6 %all-to-all-start = ((f32[16,2,8,2048]{3,2,1,0:T(8,128)}), f32[16,2,8,2048]{3,2,1,0:T(8,128)}, u32[]{:S(2)}, u32[]{:S(2)}) async-start(f32[16,2,8,2048]{3,2,1,0:T(8,128)} %shard_map.77), calls=%async_computation | async-start | bytes 4194304 | tf_op jit(solution)/shard_map/all_to_all | solution.py:183
  28.8 0.0 all-gather.2.cloned.1.call-start
  28.8 2.5 %collective-permute-start = (f32[64,8,640]{2,1,0:T(8,128)}, f32[64,8,640]{2,1,0:T(8,128)S(1)}, u32[]{:S(2)}, u32[]{:S(2)}) collective-permute-start(f32[64,8,640]{2,1,0:T(8,128)} %b0), channel_id=1, source_target_pairs={{0,8},{8,16},{16,24},{24,0},{1,9},{9,17},{17,25},{25,1},{2,10},{10... | collective-permute-start | bytes 3932168 | tf_op jit(solution)/shard_map/ppermute | solution.py:194
  31.3 3.4 %collective-permute-start.1 = (f32[64,8,640]{2,1,0:T(8,128)}, f32[64,8,640]{2,1,0:T(8,128)S(1)}, u32[]{:S(2)}, u32[]{:S(2)}) collective-permute-start(f32[64,8,640]{2,1,0:T(8,128)} %b0), channel_id=1, source_target_pairs={{0,24},{8,0},{16,8},{24,16},{1,25},{9,1},{17,9},{25,17},{2,26},{10... | collective-permute-start | bytes 3932168 | tf_op jit(solution)/shard_map/ppermute | solution.py:195
  34.7 0.0 all-gather.2.cloned.1.call-update
  34.7 25.9 %collective-permute-done.b1 = f32[64,8,640]{2,1,0:T(8,128)S(1)} collective-permute-done((f32[64,8,640]{2,1,0:T(8,128)}, f32[64,8,640]{2,1,0:T(8,128)S(1)}, u32[]{:S(2)}, u32[]{:S(2)}) %collective-permute-start) | collective-permute-done | bytes 1310752 | tf_op jit(solution)/shard_map/ppermute | solution.py:194
  60.6 3.7 %collective-permute-start.2 = (f32[32,8,640]{2,1,0:T(8,128)S(1)}, f32[32,8,640]{2,1,0:T(8,128)S(1)}, u32[]{:S(2)}, u32[]{:S(2)}) collective-permute-start(f32[32,8,640]{2,1,0:T(8,128)S(1)} %slice.8), channel_id=1, source_target_pairs={{0,8},{8,16},{16,24},{24,0},{1,9},{9,17},{17,25},{25,1},{2,10},{10... | collective-permute-start | bytes 1966088 | tf_op jit(solution)/shard_map/ppermute | solution.py:196
  64.3 0.0 collective-permute-done.1.b3
  64.3 0.0 copy-start.5
  64.3 1.1 copy-done.5
  65.5 2.2 %collective-permute-start.3 = (f32[32,8,640]{2,1,0:T(8,128)S(1)}, f32[32,8,640]{2,1,0:T(8,128)S(1)}, u32[]{:S(2)}, u32[]{:S(2)}) collective-permute-start(f32[32,8,640]{2,1,0:T(8,128)S(1)} %slice.9), channel_id=1, source_target_pairs={{0,24},{8,0},{16,8},{24,16},{1,25},{9,1},{17,9},{25,17},{2,26},{10... | collective-permute-start | bytes 1966088 | tf_op jit(solution)/shard_map/ppermute | solution.py:197
  67.6 9.7 %collective-permute-done.2.near = f32[32,8,640]{2,1,0:T(8,128)S(1)} collective-permute-done((f32[32,8,640]{2,1,0:T(8,128)S(1)}, f32[32,8,640]{2,1,0:T(8,128)S(1)}, u32[]{:S(2)}, u32[]{:S(2)}) %collective-permute-start.2) | collective-permute-done | bytes 655392 | tf_op jit(solution)/shard_map/ppermute | solution.py:196
  77.3 5.8 %collective-permute-done.3.far = f32[32,8,640]{2,1,0:T(8,128)S(1)} collective-permute-done((f32[32,8,640]{2,1,0:T(8,128)S(1)}, f32[32,8,640]{2,1,0:T(8,128)S(1)}, u32[]{:S(2)}, u32[]{:S(2)}) %collective-permute-start.3) | collective-permute-done | bytes 655392 | tf_op jit(solution)/shard_map/ppermute | solution.py:197
  83.1 1.4 all-to-all-done.x_ref
  84.5 6.6 %shard_map.78 = f32[2,128,640]{2,1,0:T(8,128)S(1)} custom-call(f32[16,2,8,2048]{3,2,1,0:T(8,128)} %all-to-all-done.x_ref, f32[64,8,640]{2,1,0:T(8,128)S(1)} %collective-permute-done.b1, f32[64,8,640]{2,1,0:T(8,128)} %copy-done.5, f32[64,8,640]{2,1,0:T(8,128)} %b0, f32[32,8,640]{2,1,0:T(8,128)S(1)} %collective-permute-done.2.near, ...), custom_call_target="tpu_custom_call" | custom-call | flops 2013265920 | bytes 8388608 | tf_op jit(solution)/shard_map/pallas_call | solution.py:112
  91.1 0.0 copy-start.7
  91.1 0.0 copy-start.1
  91.1 0.0 copy-start.3
  91.1 0.0 copy-start.4
  91.1 4.4 %all_to_all.30.p_ref = f32[2,128,640]{2,1,0:T(8,128)S(1)} all-to-all(f32[2,128,640]{2,1,0:T(8,128)S(1)} %shard_map.78), channel_id=1, replica_groups=mesh['y'=8,'zl'=2,'x'=4,'zh'=4,'core'=2] {'core'}, dimensions={0} | all-to-all | bytes 1310720 | tf_op jit(solution)/shard_map/all_to_all | solution.py:183
  95.5 0.9 shard_map.79
  96.4 10.8 %all-to-all-start.2 = ((f32[8,8,2,640]{3,2,1,0:T(2,128)}), f32[8,8,2,640]{3,2,1,0:T(2,128)S(1)}, u32[]{:S(2)}, u32[]{:S(2)}) async-start(f32[8,8,2,640]{3,2,1,0:T(2,128)} %shard_map.79), calls=%async_computation.2 | async-start | bytes 655360 | tf_op jit(solution)/shard_map/all_to_all | solution.py:183
  107.2 0.0 all-gather.2.cloned.1.call-done.w_ref
  107.2 0.0 copy-done.7
  107.2 0.1 broadcast_in_dim.4.vir_ref
  107.3 0.0 copy-done.1
  107.3 0.0 copy-done.3
  107.3 0.0 copy-done.4
  107.4 0.0 copy-start.2
  107.4 1.2 copy-done.2
  108.6 2.4 %shard_map.81 = f32[8,8,2,256]{3,2,1,0:T(2,128)} custom-call(s32[32]{0:T(128)S(1)} %copy-done.3, f32[4,4,64,512]{3,2,1,0:T(8,128)S(1)} %copy-done.1, f32[64,4,8,128]{3,2,1,0:T(8,128)S(1)} %copy-done.2, s32[512,128]{1,0:T(8,128)S(1)} %broadcast_in_dim.4.vir_ref, s32[1,128]{1,0:T(1,128)S(1)} %bitcast.6), custom_call_target="tpu_custom_call" | custom-call | flops 402653184 | bytes 3145728 | tf_op jit(solution)/shard_map/pallas_call | solution.py:169
  111.0 7.1 %all-to-all-done.2.p_ref = f32[8,8,2,640]{3,2,1,0:T(2,128)S(1)} async-done(((f32[8,8,2,640]{3,2,1,0:T(2,128)}), f32[8,8,2,640]{3,2,1,0:T(2,128)S(1)}, u32[]{:S(2)}, u32[]{:S(2)}) %all-to-all-start.2) | async-done | bytes 327712 | tf_op jit(solution)/shard_map/all_to_all | solution.py:183
  118.1 7.5 %all-to-all-start.4 = ((f32[8,8,2,256]{3,2,1,0:T(2,128)}), f32[8,8,2,256]{3,2,1,0:T(2,128)S(1)}, u32[]{:S(2)}, u32[]{:S(2)}) async-start(f32[8,8,2,256]{3,2,1,0:T(2,128)} %shard_map.81), calls=%async_computation.4 | async-start | bytes 262144 | tf_op jit(solution)/shard_map/all_to_all | solution.py:183
  125.6 1.9 %collective-permute-start.4 = (f32[8,2,640]{2,1,0:T(2,128)S(1)}, f32[8,2,640]{2,1,0:T(2,128)S(1)}, u32[]{:S(2)}, u32[]{:S(2)}) collective-permute-start(f32[8,2,640]{2,1,0:T(2,128)S(1)} %shard_map.80), channel_id=1, source_target_pairs={{0,0},{2,16},{4,32},{6,48},{8,2},{10,18},{12,34},{14,50},{16,4},{1... | collective-permute-start | bytes 122888 | tf_op jit(solution)/shard_map/ppermute | solution.py:213
  127.5 8.3 %collective-permute-done.4.l_ref = f32[8,2,640]{2,1,0:T(2,128)S(1)} collective-permute-done((f32[8,2,640]{2,1,0:T(2,128)S(1)}, f32[8,2,640]{2,1,0:T(2,128)S(1)}, u32[]{:S(2)}, u32[]{:S(2)}) %collective-permute-start.4) | collective-permute-done | bytes 40992 | tf_op jit(solution)/shard_map/ppermute | solution.py:213
  135.8 0.0 all-to-all-done.4.c_ref
  135.8 12.6 %all_to_all.31.p_ref = f32[8,2,896]{2,1,0:T(2,128)S(1)} all-to-all(f32[8,2,896]{2,1,0:T(2,128)S(1)} %shard_map.82), channel_id=1, replica_groups=mesh['y'=8,'zl'=2,'x'=4,'zh'=4,'core'=2] {'y'}, dimensions={0} | all-to-all | bytes 114688 | tf_op jit(solution)/shard_map/all_to_all | solution.py:183
  148.5 0.6 shard_map.83
  149.1 0.1 reshape.19
  149.2 0.6 copy.9
  (4 shorter events, 0.1 us)
Async XLA Ops:
  7.2 15.3 %all-to-all-start.3 = ((f32[8,4,8,128]{3,2,1,0:T(8,128)}), f32[8,4,8,128]{3,2,1,0:T(8,128)S(1)}, u32[]{:S(2)}, u32[]{:S(2)}) async-start(f32[8,4,8,128]{3,2,1,0:T(8,128)} %bitcast.7), calls=%async_computation.3 | async-start | bytes 262144 | tf_op jit(solution)/shard_map/all_to_all | solution.py:183
  16.3 1.6 %copy-start = (f32[4,4,64,512]{3,2,1,0:T(8,128)S(1)}, f32[4,4,64,512]{3,2,1,0:T(8,128)}, u32[]{:S(2)}) copy-start(f32[4,4,64,512]{3,2,1,0:T(8,128)} %a_ref.1) | copy-start | bytes 6291460
  22.5 0.7 copy-start.6
  23.1 61.3 %all-to-all-start = ((f32[16,2,8,2048]{3,2,1,0:T(8,128)}), f32[16,2,8,2048]{3,2,1,0:T(8,128)}, u32[]{:S(2)}, u32[]{:S(2)}) async-start(f32[16,2,8,2048]{3,2,1,0:T(8,128)} %shard_map.77), calls=%async_computation | async-start | bytes 4194304 | tf_op jit(solution)/shard_map/all_to_all | solution.py:183
  28.8 78.4 %all-gather.2.cloned.1.call-start = ((), (), s32[]{:S(2)}) async-start(), calls=%async_computation.6 | async-start | bytes 1179648 | tf_op jit(solution)/shard_map/all_gather | solution.py:192
  28.8 31.8 %collective-permute-start = (f32[64,8,640]{2,1,0:T(8,128)}, f32[64,8,640]{2,1,0:T(8,128)S(1)}, u32[]{:S(2)}, u32[]{:S(2)}) collective-permute-start(f32[64,8,640]{2,1,0:T(8,128)} %b0), channel_id=1, source_target_pairs={{0,8},{8,16},{16,24},{24,0},{1,9},{9,17},{17,25},{25,1},{2,10},{10... | collective-permute-start | bytes 3932168 | tf_op jit(solution)/shard_map/ppermute | solution.py:194
  31.3 33.0 %collective-permute-start.1 = (f32[64,8,640]{2,1,0:T(8,128)}, f32[64,8,640]{2,1,0:T(8,128)S(1)}, u32[]{:S(2)}, u32[]{:S(2)}) collective-permute-start(f32[64,8,640]{2,1,0:T(8,128)} %b0), channel_id=1, source_target_pairs={{0,24},{8,0},{16,8},{24,16},{1,25},{9,1},{17,9},{25,17},{2,26},{10... | collective-permute-start | bytes 3932168 | tf_op jit(solution)/shard_map/ppermute | solution.py:195
  60.6 16.7 %collective-permute-start.2 = (f32[32,8,640]{2,1,0:T(8,128)S(1)}, f32[32,8,640]{2,1,0:T(8,128)S(1)}, u32[]{:S(2)}, u32[]{:S(2)}) collective-permute-start(f32[32,8,640]{2,1,0:T(8,128)S(1)} %slice.8), channel_id=1, source_target_pairs={{0,8},{8,16},{16,24},{24,0},{1,9},{9,17},{17,25},{25,1},{2,10},{10... | collective-permute-start | bytes 1966088 | tf_op jit(solution)/shard_map/ppermute | solution.py:196
  64.3 1.1 copy-start.5
  65.5 17.6 %collective-permute-start.3 = (f32[32,8,640]{2,1,0:T(8,128)S(1)}, f32[32,8,640]{2,1,0:T(8,128)S(1)}, u32[]{:S(2)}, u32[]{:S(2)}) collective-permute-start(f32[32,8,640]{2,1,0:T(8,128)S(1)} %slice.9), channel_id=1, source_target_pairs={{0,24},{8,0},{16,8},{24,16},{1,25},{9,1},{17,9},{25,17},{2,26},{10... | collective-permute-start | bytes 1966088 | tf_op jit(solution)/shard_map/ppermute | solution.py:197
  91.1 16.1 %copy-start.7 = (s32[512]{0:T(512)S(1)}, s32[512]{0:T(512)}, u32[]{:S(2)}) copy-start(s32[512]{0:T(512)} %param.10) | copy-start | bytes 6148
  91.1 16.2 %copy-start.1 = (f32[4,4,64,512]{3,2,1,0:T(8,128)S(1)}, f32[4,4,64,512]{3,2,1,0:T(8,128)}, u32[]{:S(2)}) copy-start(f32[4,4,64,512]{3,2,1,0:T(8,128)} %a_ref.1) | copy-start | bytes 6291460
  91.1 16.2 %copy-start.3 = (s32[32]{0:T(128)S(1)}, s32[32]{0:T(128)}, u32[]{:S(2)}) copy-start(s32[32]{0:T(128)} %occ_ref.1) | copy-start | bytes 388
  91.1 16.2 %copy-start.4 = (s32[128]{0:T(128)S(1)}, s32[128]{0:T(128)}, u32[]{:S(2)}) copy-start(s32[128]{0:T(128)} %param.11) | copy-start | bytes 1540
  96.4 21.7 %all-to-all-start.2 = ((f32[8,8,2,640]{3,2,1,0:T(2,128)}), f32[8,8,2,640]{3,2,1,0:T(2,128)S(1)}, u32[]{:S(2)}, u32[]{:S(2)}) async-start(f32[8,8,2,640]{3,2,1,0:T(2,128)} %shard_map.79), calls=%async_computation.2 | async-start | bytes 655360 | tf_op jit(solution)/shard_map/all_to_all | solution.py:183
  107.4 1.2 copy-start.2
  118.1 17.7 %all-to-all-start.4 = ((f32[8,8,2,256]{3,2,1,0:T(2,128)}), f32[8,8,2,256]{3,2,1,0:T(2,128)S(1)}, u32[]{:S(2)}, u32[]{:S(2)}) async-start(f32[8,8,2,256]{3,2,1,0:T(2,128)} %shard_map.81), calls=%async_computation.4 | async-start | bytes 262144 | tf_op jit(solution)/shard_map/all_to_all | solution.py:183
  125.6 10.2 %collective-permute-start.4 = (f32[8,2,640]{2,1,0:T(2,128)S(1)}, f32[8,2,640]{2,1,0:T(2,128)S(1)}, u32[]{:S(2)}, u32[]{:S(2)}) collective-permute-start(f32[8,2,640]{2,1,0:T(2,128)S(1)} %shard_map.80), channel_id=1, source_target_pairs={{0,0},{2,16},{4,32},{6,48},{8,2},{10,18},{12,34},{14,50},{16,4},{1... | collective-permute-start | bytes 122888 | tf_op jit(solution)/shard_map/ppermute | solution.py:213
Sparse Core Ops, SparseCore 0:
  34.8 57.2 all-gather.1

commit v3 on v2

--- a/solution.py
+++ b/solution.py
@@ -8,6 +8,7 @@
 F32 = jnp.float32
 BF16 = jnp.bfloat16
 VMEM_LIMIT = 16 * 1024 * 1024
+LADDER_LIMIT = 50 * 1024 * 1024
 
 
 def split(v):
@@ -115,68 +116,73 @@
         out_specs=VMEM,
         out_shape=jax.ShapeDtypeStruct((2, 128, 640), F32),
         scratch_shapes=[pltpu.VMEM((4, 64, 8, 640), F32), pltpu.SemaphoreType.DMA((2, 4))],
-        compiler_params=pltpu.CompilerParams(vmem_limit_bytes=50 * 1024 * 1024),
+        compiler_params=pltpu.CompilerParams(vmem_limit_bytes=LADDER_LIMIT),
         cost_estimate=pl.CostEstimate(
             flops=3 * 2 * 256 * 2048 * 640, bytes_accessed=8 * 2**20, transcendentals=0
         ),
     )(x, b1, b3, b0, near, far)
 
 
-def cores_kernel(p_ref, o_ref, total):
-    total[...] = p_ref[0] + p_ref[1]
-    for y in range(8):
-        for d in range(8):
-            o_ref[d, y] = total[pl.ds(16 * y + 2 * d, 2), :]
-
-
-def depth_kernel(p_ref, o_ref):
-    for y in range(8):
-        p = [p_ref[s, y] for s in range(8)]
-        o_ref[y] = ((p[0] + p[1]) + (p[2] + p[3])) + ((p[4] + p[5]) + (p[6] + p[7]))
-
-
-def pack_kernel(l_ref, c_ref, o_ref):
-    for y in range(8):
-        p = [c_ref[s, y] for s in range(8)]
-        o_ref[y, :, pl.ds(0, 640)] = l_ref[y]
-        o_ref[y, :, pl.ds(640, 256)] = ((p[0] + p[1]) + (p[2] + p[3])) + (
-            (p[4] + p[5]) + (p[6] + p[7])
-        )
-
-
-def finish_kernel(p_ref, ladder_ref, cycle_ref):
-    p = [p_ref[y, :, pl.ds(0, 640)] for y in range(8)]
-    ladder_ref[...] = ((p[0] + p[1]) + (p[2] + p[3])) + ((p[4] + p[5]) + (p[6] + p[7]))
-    cycle_ref[...] = p_ref[:, :, pl.ds(640, 256)]
-
-
-def cycle_kernel(occ_ref, a_ref, w_ref, vir_ref, pair_ref, o_ref, turned):
-    first = (lax.axis_index("zl") * 4 + lax.axis_index("x")) * 4
-    total = jnp.zeros((256, 128), F32)
-    for k in range(4):
-        allowed = jnp.bitwise_xor(vir_ref[...], occ_ref[first + k]) == pair_ref[...]
-        w = jnp.where(allowed, w_ref[:, k].reshape(512, 128), 0.0)
-        ah, al = split(a_ref[:, k].reshape(256, 512))
-        wh, wl = split(w)
-        total = total + dot3(ah, al, wh, wl)
-    turned[...] = total.T
+def spread_kernel(w_ref, o_ref):
+    core = lax.axis_index("core")
     for col in range(8):
         for y in range(8):
-            o_ref[col, y] = turned[pl.ds(16 * y + 2 * col, 2), :]
-
-
-def cycle(occ, amplitudes, w, vir, pair):
+            o_ref[y * 8 + col] = w_ref[pl.ds(col * 4 + 2 * core, 2)]
+
+
+def pack_kernel(part_ref, c0, c1, c2, c3, o_ref, ladder_sum, cycle_sum):
+    ladder_sum[...] = part_ref[0] + part_ref[1]
+    cycle_sum[...] = (c0[...] + c1[...]) + (c2[...] + c3[...])
+    for d in range(64):
+        o_ref[d, :, pl.ds(0, 640)] = ladder_sum[pl.ds(2 * d, 2), :]
+        o_ref[d, :, pl.ds(640, 256)] = cycle_sum[pl.ds(d // 4 * 2, 2), :]
+
+
+def finish_kernel(p_ref, ladder_ref, cycle_ref):
+    zh = lax.axis_index("zh")
+    total = [p_ref[d, :, pl.ds(0, 640)] for d in range(8)]
+    for d in range(8, 64):
+        total[d % 8] += p_ref[d, :, pl.ds(0, 640)]
+    while len(total) > 1:
+        total = [p + q for p, q in zip(total[::2], total[1::2])]
+    ladder_ref[...] = total[0]
+    for y in range(8):
+        cycle_ref[y] = (
+            p_ref[y * 8 + zh, :, pl.ds(640, 256)] + p_ref[y * 8 + 4 + zh, :, pl.ds(640, 256)]
+        )
+
+
+def cycle_kernel(occ_ref, a_ref, own_ref, other_ref, vir_ref, pair_ref, o_ref, turned):
+    first = (lax.axis_index("zl") * 4 + lax.axis_index("x")) * 4
+    core = lax.axis_index("core")
+    total = jnp.zeros((256, 128), F32)
+    for half, w_ref in ((core, own_ref), (1 - core, other_ref)):
+        for s in range(2):
+            k = 2 * half + s
+            allowed = jnp.bitwise_xor(vir_ref[...], occ_ref[first + k]) == pair_ref[...]
+            w = jnp.where(allowed, w_ref[:, s].reshape(512, 128), 0.0)
+            ah, al = split(a_ref[:, k].reshape(256, 512))
+            wh, wl = split(w)
+            total = total + dot3(ah, al, wh, wl)
+    turned[...] = total.T
+    for x in range(4):
+        to = lax.rem(x + 4 - lax.axis_index("x"), 4)
+        for d in range(16):
+            o_ref[to, pl.ds(2 * d, 2), :] = turned[pl.ds(8 * d + 2 * x, 2), :]
+
+
+def cycle(occ, amplitudes, own, other, vir, pair):
     return pl.pallas_call(
         cycle_kernel,
-        in_specs=[pl.BlockSpec(memory_space=pltpu.SMEM)] + [VMEM] * 4,
+        in_specs=[pl.BlockSpec(memory_space=pltpu.SMEM)] + [VMEM] * 5,
         out_specs=VMEM,
-        out_shape=jax.ShapeDtypeStruct((8, 8, 2, 256), F32),
+        out_shape=jax.ShapeDtypeStruct((4, 32, 256), F32),
         scratch_shapes=[pltpu.VMEM((128, 256), F32)],
         compiler_params=pltpu.CompilerParams(vmem_limit_bytes=VMEM_LIMIT),
         cost_estimate=pl.CostEstimate(
             flops=3 * 2 * 256 * 2048 * 128, bytes_accessed=3 * 2**20, transcendentals=0
         ),
-    )(occ, amplitudes, w, vir, pair)
+    )(occ, amplitudes, own, other, vir, pair)
 
 
 def exchange(v, axes):
@@ -184,25 +190,28 @@
 
 
 def body(amplitudes, ladder_ints, cycle_ints, occ_irrep, vir_irrep, pair_irrep):
-    w = exchange(cycle_ints.reshape(8, 4, 8, 128), ("zl", "x"))
+    own = exchange(small(spread_kernel, (64, 2, 8, 128), cycle_ints), ("y", "zl", "x"))
 
     ring = [[(i, (i + s) % 4) for i in range(4)] for s in range(4)]
     sent = regroup(amplitudes)
+    _, ladder_ints = lax.optimization_barrier((sent, ladder_ints))
+    sent, own = lax.optimization_barrier((sent, own))
     x = exchange(sent, ("y", "zl"))
-    w = lax.all_gather(w, "y", axis=0, tiled=True)
-    _, ladder_ints, vir_irrep = lax.optimization_barrier((sent, ladder_ints, vir_irrep))
+    other = lax.ppermute(own, "core", [(0, 1), (1, 0)])
     b1 = lax.ppermute(ladder_ints, "x", ring[1])
     b3 = lax.ppermute(ladder_ints, "x", ring[3])
     near = lax.ppermute(b1[:32], "x", ring[1])
     far = lax.ppermute(b3[32:], "x", ring[3])
+
+    vir = jnp.broadcast_to(vir_irrep[:, None], (512, 128))
+    parts = cycle(occ_irrep, amplitudes, own, other, vir, pair_irrep[None])
+    parts = [parts[0]] + [lax.ppermute(parts[s], "x", ring[s]) for s in (1, 2, 3)]
+
     part = exchange(ladder(x, ladder_ints, b1, b3, near, far), ("core",))
-    part = small(cores_kernel, (8, 8, 2, 640), part, scratch=[(128, 640)])
-
-    vir = jnp.broadcast_to(vir_irrep[:, None], (512, 128))
-    _, late = lax.optimization_barrier((part, w))
-    cycle_part = cycle(occ_irrep, amplitudes, late, vir, pair_irrep[None])
-    part = small(depth_kernel, (8, 2, 640), exchange(part, ("zl", "zh")))
-    _, cycle_part = lax.optimization_barrier((part, cycle_part))
+    both = small(pack_kernel, (64, 2, 896), part, *parts, scratch=[(128, 640), (32, 256)])
+    both = exchange(both, ("y", "zl", "zh"))
+    part, cycle_part = small(finish_kernel, [(2, 640), (8, 2, 256)], both)
+    cycle_resid = cycle_part.reshape(8, 2, 4, 64).transpose(0, 2, 3, 1).reshape(32, 64, 2)
     move = [
         ((s * 4 + a) * 4 + hi * 2 + lo, (hi * 4 + lo * 2 + s) * 4 + a)
         for s in range(2)
@@ -210,11 +219,7 @@
         for hi in range(2)
         for lo in range(2)
     ]
-    part = lax.ppermute(part, ("zl", "x", "zh"), move)
-    cycle_part = exchange(cycle_part, ("zl", "x"))
-    both = exchange(small(pack_kernel, (8, 2, 896), part, cycle_part), ("y",))
-    ladder_resid, cycle_part = small(finish_kernel, [(2, 640), (8, 2, 256)], both)
-    cycle_resid = cycle_part.reshape(8, 2, 4, 64).transpose(0, 2, 3, 1).reshape(32, 64, 2)
+    ladder_resid = lax.ppermute(part, ("zl", "x", "zh"), move)
     return ladder_resid, cycle_resid
 
 

time: 158 us -> 145 us (0.918)
  waiting for transfers between devices: 58.1 us -> 39.1 us
  blocking collectives: 17 us -> 34.5 us
  between operations: 14.2 us -> 0.91 us
  starting transfers between devices: 46.7 us -> 50.7 us
    ppermute x1, waiting for transfers between devices: 25.9 us -> 0.01 us  [body(): b1 = lax.ppermute(ladder_ints, 'x', ring[1])]
    ppermute x1, waiting for transfers between devices: 0.01 us -> 22.3 us  [body(): b3 = lax.ppermute(ladder_ints, 'x', ring[3])]
    all_to_all x2 -> x1, blocking collectives: 17 us -> 34.5 us  [exchange(): return lax.all_to_all(v, axes, split_axis=0, concat_axis=0, tiled=True)]
    ppermute x1 -> x5, starting transfers between devices: 1.91 us -> 16.1 us  [the longest x3 8.97 us: body(): lax.ppermute(parts[s], 'x', ring[s])]
    all_to_all x4 -> x3, starting transfers between devices: 33 us -> 20.4 us  [exchange(): return lax.all_to_all(v, axes, split_axis=0, concat_axis=0, tiled=True)]
    ppermute x1, waiting for transfers between devices: 9.7 us -> 0.43 us  [body(): near = lax.ppermute(b1[:32], 'x', ring[1])]
    ppermute x1, waiting for transfers between devices: 5.76 us -> 0.01 us  [body(): far = lax.ppermute(b3[32:], 'x', ring[3])]
    ppermute x1 -> x5, waiting for transfers between devices: 8.31 us -> 3.46 us  [the longest x1 3.45 us: body(): ladder_resid = lax.ppermute(part, ('zl', 'x', 'zh'), move)]
  transfers between devices with their start and end apart: 10 -> 12, of which waited for: 6 -> 5; matrix products, arithmetic and copies ran while one was open for 0% -> 1% of each run, Pallas kernels for 9% -> 10%
where the time goes in v3:
time: 145 us; the launch traced here: 144 us
  starting transfers between devices  50.7 us (35%)
  waiting for transfers between devices  39.1 us (27%)
  blocking collectives  34.5 us (24%)
  Pallas kernels  14.8 us (10%)
  local copies, waits for them, and re-layouts  4.05 us (3%)
    all_to_all x1, blocking collectives, exchange(): return lax.all_to_all(v, axes, split_axis=0, concat_axis=0, tiled=True)  34.5 us
    ppermute x1, waiting for transfers between devices, body(): b3 = lax.ppermute(ladder_ints, 'x', ring[3])  22.3 us
    all_to_all x3, starting transfers between devices, exchange(): return lax.all_to_all(v, axes, split_axis=0, concat_axis=0, tiled=True)  20.4 us
    all_to_all x3, waiting for transfers between devices, exchange(): return lax.all_to_all(v, axes, split_axis=0, concat_axis=0, tiled=True)  12.9 us
    ppermute x3, starting transfers between devices, body(): lax.ppermute(parts[s], 'x', ring[s])  8.97 us
    pallas_call x1, Pallas kernels, ladder(): pl.pallas_call(ladder_kernel, in_specs=[VMEM] * 3 + [anywhere] * 3, out_s...  7.45 us
    ppermute x1, starting transfers between devices, body(): ladder_resid = lax.ppermute(part, ('zl', 'x', 'zh'), move)  5.23 us
    ppermute x1, starting transfers between devices, body(): near = lax.ppermute(b1[:32], 'x', ring[1])  5.13 us
  transfers between devices with their start and end apart: 12, of which 5 were waited for; matrix products, arithmetic and copies ran while one was open for 1% of the time, Pallas kernels for 10%

profile of v3, /device:TPU:6, one launch (start us, length us, event | category | flops | bytes accessed | tf_op | source)
XLA Modules:
  0.0 144.1 jit_solution(6798009549391277349)
XLA Ops:
  0.6 0.0 copy-start.2
  0.6 0.9 copy-done.2
  1.5 0.8 shard_map.78
  2.4 12.4 %all-to-all-start = ((f32[64,2,8,128]{3,2,1,0:T(8,128)}), f32[64,2,8,128]{3,2,1,0:T(8,128)S(1)}, u32[]{:S(2)}, u32[]{:S(2)}) async-start(f32[64,2,8,128]{3,2,1,0:T(8,128)} %shard_map.78), calls=%async_computation | async-start | bytes 1048576 | tf_op jit(solution)/shard_map/all_to_all | solution.py:189
  14.8 0.0 copy-start
  14.8 1.6 %copy-done = f32[4,4,64,512]{3,2,1,0:T(8,128)S(1)} copy-done((f32[4,4,64,512]{3,2,1,0:T(8,128)S(1)}, f32[4,4,64,512]{3,2,1,0:T(8,128)}, u32[]{:S(2)}) %copy-start) | copy-done | bytes 2097176
  16.4 4.5 %shard_map.77 = f32[16,2,8,2048]{3,2,1,0:T(8,128)} custom-call(f32[4,2,2,64,512]{4,3,2,1,0:T(8,128)S(1)} %bitcast.12), custom_call_target="tpu_custom_call" | custom-call | flops 1048576 | bytes 4194304 | tf_op jit(solution)/shard_map/pallas_call | solution.py:51
  20.9 11.1 %all-to-all-done.own_ref = f32[64,2,8,128]{3,2,1,0:T(8,128)S(1)} async-done(((f32[64,2,8,128]{3,2,1,0:T(8,128)}), f32[64,2,8,128]{3,2,1,0:T(8,128)S(1)}, u32[]{:S(2)}, u32[]{:S(2)}) %all-to-all-start) | async-done | bytes 524320 | tf_op jit(solution)/shard_map/all_to_all | solution.py:189
  32.0 4.4 %all-to-all-start.1 = ((f32[16,2,8,2048]{3,2,1,0:T(8,128)}), f32[16,2,8,2048]{3,2,1,0:T(8,128)}, u32[]{:S(2)}, u32[]{:S(2)}) async-start(f32[16,2,8,2048]{3,2,1,0:T(8,128)} %shard_map.77), calls=%async_computation.1 | async-start | bytes 4194304 | tf_op jit(solution)/shard_map/all_to_all | solution.py:189
  36.4 0.0 copy-start.6
  36.5 0.0 copy-start.1
  36.5 0.0 copy-start.3
  36.5 0.0 copy-start.4
  36.5 2.4 %collective-permute-start.1 = (f32[64,8,640]{2,1,0:T(8,128)}, f32[64,8,640]{2,1,0:T(8,128)S(1)}, u32[]{:S(2)}, u32[]{:S(2)}) collective-permute-start(f32[64,8,640]{2,1,0:T(8,128)} %b0), channel_id=1, source_target_pairs={{0,24},{8,0},{16,8},{24,16},{1,25},{9,1},{17,9},{25,17},{2,26},{10... | collective-permute-start | bytes 3932168 | tf_op jit(solution)/shard_map/ppermute | solution.py:202
  38.9 4.8 %collective-permute-start = (f32[64,8,640]{2,1,0:T(8,128)}, f32[64,8,640]{2,1,0:T(8,128)S(1)}, u32[]{:S(2)}, u32[]{:S(2)}) collective-permute-start(f32[64,8,640]{2,1,0:T(8,128)} %b0), channel_id=1, source_target_pairs={{0,8},{8,16},{16,24},{24,0},{1,9},{9,17},{17,25},{25,1},{2,10},{10... | collective-permute-start | bytes 3932168 | tf_op jit(solution)/shard_map/ppermute | solution.py:201
  43.7 1.9 %collective-permute-start.4 = (f32[64,2,8,128]{3,2,1,0:T(8,128)S(1)}, f32[64,2,8,128]{3,2,1,0:T(8,128)S(1)}, u32[]{:S(2)}, u32[]{:S(2)}) collective-permute-start(f32[64,2,8,128]{3,2,1,0:T(8,128)S(1)} %all-to-all-done.own_ref), channel_id=1, source_target_pairs={{0,1},{1,0},{2,3},{3,2},{4,5},{5,4},{6,7},{7,6},{8,9},{9,8},{10,11... | collective-permute-start | bytes 1572872 | tf_op jit(solution)/shard_map/ppermute | solution.py:200
  45.6 22.3 %collective-permute-done.1.b3 = f32[64,8,640]{2,1,0:T(8,128)S(1)} collective-permute-done((f32[64,8,640]{2,1,0:T(8,128)}, f32[64,8,640]{2,1,0:T(8,128)S(1)}, u32[]{:S(2)}, u32[]{:S(2)}) %collective-permute-start.1) | collective-permute-done | bytes 1310752 | tf_op jit(solution)/shard_map/ppermute | solution.py:202
  68.0 0.0 copy-start.5
  68.0 1.9 %collective-permute-start.3 = (f32[32,8,640]{2,1,0:T(8,128)S(1)}, f32[32,8,640]{2,1,0:T(8,128)S(1)}, u32[]{:S(2)}, u32[]{:S(2)}) collective-permute-start(f32[32,8,640]{2,1,0:T(8,128)S(1)} %slice.25), channel_id=1, source_target_pairs={{0,24},{8,0},{16,8},{24,16},{1,25},{9,1},{17,9},{25,17},{2,26},{10... | collective-permute-start | bytes 1966088 | tf_op jit(solution)/shard_map/ppermute | solution.py:204
  69.9 0.0 collective-permute-done.b1
  70.0 5.1 %collective-permute-start.2 = (f32[32,8,640]{2,1,0:T(8,128)S(1)}, f32[32,8,640]{2,1,0:T(8,128)S(1)}, u32[]{:S(2)}, u32[]{:S(2)}) collective-permute-start(f32[32,8,640]{2,1,0:T(8,128)S(1)} %slice.24), channel_id=1, source_target_pairs={{0,8},{8,16},{16,24},{24,0},{1,9},{9,17},{17,25},{25,1},{2,10},{10... | collective-permute-start | bytes 1966088 | tf_op jit(solution)/shard_map/ppermute | solution.py:203
  75.1 0.0 collective-permute-done.4.other_ref
  75.1 0.0 copy-done.5
  75.2 0.0 copy-done.6
  75.2 0.1 broadcast_in_dim.4.vir_ref
  75.3 0.0 copy-done.1
  75.3 0.0 copy-done.3
  75.3 0.0 copy-done.4
  75.3 1.8 %shard_map.80 = f32[4,32,256]{2,1,0:T(8,128)S(1)} custom-call(s32[32]{0:T(128)S(1)} %copy-done.3, f32[4,4,64,512]{3,2,1,0:T(8,128)S(1)} %copy-done.1, f32[64,2,8,128]{3,2,1,0:T(8,128)S(1)} %all-to-all-done.own_ref, f32[64,2,8,128]{3,2,1,0:T(8,128)S(1)} %collective-permute-done.4.other_ref, s32[512,128]{1,0:T(8,128)S(1)} %broadcast_in_dim.4.vir_ref, ...), custom_call_target="tpu_custom_call" | custom-call | flops 402653184 | bytes 3145728 | tf_op jit(solution)/shard_map/pallas_call | solution.py:175
  77.1 1.9 %collective-permute-start.7 = (f32[32,256]{1,0:T(8,128)S(1)}, f32[32,256]{1,0:T(8,128)S(1)}, u32[]{:S(2)}, u32[]{:S(2)}) collective-permute-start(f32[32,256]{1,0:T(8,128)S(1)} %get-tuple-element.12), channel_id=1, source_target_pairs={{0,24},{8,0},{16,8},{24,16},{1,25},{9,1},{17,9},{25,17},{2,26},{10... | collective-permute-start | bytes 98312 | tf_op jit(solution)/shard_map/ppermute | solution.py:208
  79.1 3.4 %collective-permute-start.6 = (f32[32,256]{1,0:T(8,128)S(1)}, f32[32,256]{1,0:T(8,128)S(1)}, u32[]{:S(2)}, u32[]{:S(2)}) collective-permute-start(f32[32,256]{1,0:T(8,128)S(1)} %get-tuple-element.13), channel_id=1, source_target_pairs={{0,16},{8,24},{16,0},{24,8},{1,17},{9,25},{17,1},{25,9},{2,18},{10... | collective-permute-start | bytes 98312 | tf_op jit(solution)/shard_map/ppermute | solution.py:208
  82.5 3.7 %collective-permute-start.5 = (f32[32,256]{1,0:T(8,128)S(1)}, f32[32,256]{1,0:T(8,128)S(1)}, u32[]{:S(2)}, u32[]{:S(2)}) collective-permute-start(f32[32,256]{1,0:T(8,128)S(1)} %get-tuple-element.14), channel_id=1, source_target_pairs={{0,8},{8,16},{16,24},{24,0},{1,9},{9,17},{17,25},{25,1},{2,10},{10... | collective-permute-start | bytes 98312 | tf_op jit(solution)/shard_map/ppermute | solution.py:208
  86.1 0.0 collective-permute-done.3.far
  86.2 0.4 collective-permute-done.2.near
  86.6 0.0 all-to-all-done.1.x_ref
  86.6 7.5 %shard_map.79 = f32[2,128,640]{2,1,0:T(8,128)} custom-call(f32[16,2,8,2048]{3,2,1,0:T(8,128)} %all-to-all-done.1.x_ref, f32[64,8,640]{2,1,0:T(8,128)S(1)} %collective-permute-done.b1, f32[64,8,640]{2,1,0:T(8,128)} %copy-done.5, f32[64,8,640]{2,1,0:T(8,128)} %b0, f32[32,8,640]{2,1,0:T(8,128)S(1)} %collective-permute-done.2.near, ...), custom_call_target="tpu_custom_call" | custom-call | flops 2013265920 | bytes 8388608 | tf_op jit(solution)/shard_map/pallas_call | solution.py:113
  94.0 3.5 %all-to-all-start.2 = ((f32[2,128,640]{2,1,0:T(8,128)}), f32[2,128,640]{2,1,0:T(8,128)S(1)}, u32[]{:S(2)}, u32[]{:S(2)}) async-start(f32[2,128,640]{2,1,0:T(8,128)} %shard_map.79), calls=%async_computation.2 | async-start | bytes 1310720 | tf_op jit(solution)/shard_map/all_to_all | solution.py:189
  97.6 0.0 collective-permute-done.7.c3
  97.6 0.0 collective-permute-done.6.c2
  97.6 0.0 collective-permute-done.5.c1
  97.6 1.8 %all-to-all-done.2.part_ref = f32[2,128,640]{2,1,0:T(8,128)S(1)} async-done(((f32[2,128,640]{2,1,0:T(8,128)}), f32[2,128,640]{2,1,0:T(8,128)S(1)}, u32[]{:S(2)}, u32[]{:S(2)}) %all-to-all-start.2) | async-done | bytes 655392 | tf_op jit(solution)/shard_map/all_to_all | solution.py:189
  99.4 0.2 shard_map.81
  99.6 34.5 %all_to_all.20.p_ref = f32[64,2,896]{2,1,0:T(2,128)S(1)} all-to-all(f32[64,2,896]{2,1,0:T(2,128)S(1)} %shard_map.81), channel_id=1, replica_groups=mesh['y'=8,'zl'=2,'x'=4,'zh'=4,'core'=2] {'y','zl','zh'}, dimensions={0} | all-to-all | bytes 917504 | tf_op jit(solution)/shard_map/all_to_all | solution.py:189
  134.1 5.2 %collective-permute-start.8 = (f32[2,640]{1,0:T(2,128)S(1)}, f32[2,640]{1,0:T(2,128)S(1)}, u32[]{:S(2)}, u32[]{:S(2)}) collective-permute-start(f32[2,640]{1,0:T(2,128)S(1)} %get-tuple-element.10), channel_id=1, source_target_pairs={{0,0},{2,16},{4,32},{6,48},{8,2},{10,18},{12,34},{14,50},{16,4},{1... | collective-permute-start | bytes 15368 | tf_op jit(solution)/shard_map/ppermute | solution.py:222
  139.3 0.1 reshape.15
  139.4 0.6 copy.8
  140.0 3.5 %collective-permute-done.8 = f32[2,640]{1,0:T(2,128)S(1)} collective-permute-done((f32[2,640]{1,0:T(2,128)S(1)}, f32[2,640]{1,0:T(2,128)S(1)}, u32[]{:S(2)}, u32[]{:S(2)}) %collective-permute-start.8) | collective-permute-done | bytes 5152 | tf_op jit(solution)/shard_map/ppermute | solution.py:222
  143.5 0.6 copy.10
  (4 shorter events, 0.1 us)
Async XLA Ops:
  0.6 0.9 copy-start.2
  2.4 29.6 %all-to-all-start = ((f32[64,2,8,128]{3,2,1,0:T(8,128)}), f32[64,2,8,128]{3,2,1,0:T(8,128)S(1)}, u32[]{:S(2)}, u32[]{:S(2)}) async-start(f32[64,2,8,128]{3,2,1,0:T(8,128)} %shard_map.78), calls=%async_computation | async-start | bytes 1048576 | tf_op jit(solution)/shard_map/all_to_all | solution.py:189
  14.8 1.6 %copy-start = (f32[4,4,64,512]{3,2,1,0:T(8,128)S(1)}, f32[4,4,64,512]{3,2,1,0:T(8,128)}, u32[]{:S(2)}) copy-start(f32[4,4,64,512]{3,2,1,0:T(8,128)} %a_ref.1) | copy-start | bytes 6291460
  32.0 54.6 %all-to-all-start.1 = ((f32[16,2,8,2048]{3,2,1,0:T(8,128)}), f32[16,2,8,2048]{3,2,1,0:T(8,128)}, u32[]{:S(2)}, u32[]{:S(2)}) async-start(f32[16,2,8,2048]{3,2,1,0:T(8,128)} %shard_map.77), calls=%async_computation.1 | async-start | bytes 4194304 | tf_op jit(solution)/shard_map/all_to_all | solution.py:189
  36.4 38.7 %copy-start.6 = (s32[512]{0:T(512)S(1)}, s32[512]{0:T(512)}, u32[]{:S(2)}) copy-start(s32[512]{0:T(512)} %param.10) | copy-start | bytes 6148
  36.5 38.8 %copy-start.1 = (f32[4,4,64,512]{3,2,1,0:T(8,128)S(1)}, f32[4,4,64,512]{3,2,1,0:T(8,128)}, u32[]{:S(2)}) copy-start(f32[4,4,64,512]{3,2,1,0:T(8,128)} %a_ref.1) | copy-start | bytes 6291460
  36.5 38.8 %copy-start.3 = (s32[32]{0:T(128)S(1)}, s32[32]{0:T(128)}, u32[]{:S(2)}) copy-start(s32[32]{0:T(128)} %occ_ref.1) | copy-start | bytes 388
  36.5 38.8 %copy-start.4 = (s32[128]{0:T(128)S(1)}, s32[128]{0:T(128)}, u32[]{:S(2)}) copy-start(s32[128]{0:T(128)} %param.11) | copy-start | bytes 1540
  36.5 31.5 %collective-permute-start.1 = (f32[64,8,640]{2,1,0:T(8,128)}, f32[64,8,640]{2,1,0:T(8,128)S(1)}, u32[]{:S(2)}, u32[]{:S(2)}) collective-permute-start(f32[64,8,640]{2,1,0:T(8,128)} %b0), channel_id=1, source_target_pairs={{0,24},{8,0},{16,8},{24,16},{1,25},{9,1},{17,9},{25,17},{2,26},{10... | collective-permute-start | bytes 3932168 | tf_op jit(solution)/shard_map/ppermute | solution.py:202
  38.9 31.0 %collective-permute-start = (f32[64,8,640]{2,1,0:T(8,128)}, f32[64,8,640]{2,1,0:T(8,128)S(1)}, u32[]{:S(2)}, u32[]{:S(2)}) collective-permute-start(f32[64,8,640]{2,1,0:T(8,128)} %b0), channel_id=1, source_target_pairs={{0,8},{8,16},{16,24},{24,0},{1,9},{9,17},{17,25},{25,1},{2,10},{10... | collective-permute-start | bytes 3932168 | tf_op jit(solution)/shard_map/ppermute | solution.py:201
  43.7 31.4 %collective-permute-start.4 = (f32[64,2,8,128]{3,2,1,0:T(8,128)S(1)}, f32[64,2,8,128]{3,2,1,0:T(8,128)S(1)}, u32[]{:S(2)}, u32[]{:S(2)}) collective-permute-start(f32[64,2,8,128]{3,2,1,0:T(8,128)S(1)} %all-to-all-done.own_ref), channel_id=1, source_target_pairs={{0,1},{1,0},{2,3},{3,2},{4,5},{5,4},{6,7},{7,6},{8,9},{9,8},{10,11... | collective-permute-start | bytes 1572872 | tf_op jit(solution)/shard_map/ppermute | solution.py:200
  68.0 7.2 %copy-start.5 = (f32[64,8,640]{2,1,0:T(8,128)}, f32[64,8,640]{2,1,0:T(8,128)S(1)}, u32[]{:S(2)}) copy-start(f32[64,8,640]{2,1,0:T(8,128)S(1)} %collective-permute-done.1.b3) | copy-start | bytes 3932164
  68.0 18.1 %collective-permute-start.3 = (f32[32,8,640]{2,1,0:T(8,128)S(1)}, f32[32,8,640]{2,1,0:T(8,128)S(1)}, u32[]{:S(2)}, u32[]{:S(2)}) collective-permute-start(f32[32,8,640]{2,1,0:T(8,128)S(1)} %slice.25), channel_id=1, source_target_pairs={{0,24},{8,0},{16,8},{24,16},{1,25},{9,1},{17,9},{25,17},{2,26},{10... | collective-permute-start | bytes 1966088 | tf_op jit(solution)/shard_map/ppermute | solution.py:204
  70.0 16.6 %collective-permute-start.2 = (f32[32,8,640]{2,1,0:T(8,128)S(1)}, f32[32,8,640]{2,1,0:T(8,128)S(1)}, u32[]{:S(2)}, u32[]{:S(2)}) collective-permute-start(f32[32,8,640]{2,1,0:T(8,128)S(1)} %slice.24), channel_id=1, source_target_pairs={{0,8},{8,16},{16,24},{24,0},{1,9},{9,17},{17,25},{25,1},{2,10},{10... | collective-permute-start | bytes 1966088 | tf_op jit(solution)/shard_map/ppermute | solution.py:203
  77.1 20.4 %collective-permute-start.7 = (f32[32,256]{1,0:T(8,128)S(1)}, f32[32,256]{1,0:T(8,128)S(1)}, u32[]{:S(2)}, u32[]{:S(2)}) collective-permute-start(f32[32,256]{1,0:T(8,128)S(1)} %get-tuple-element.12), channel_id=1, source_target_pairs={{0,24},{8,0},{16,8},{24,16},{1,25},{9,1},{17,9},{25,17},{2,26},{10... | collective-permute-start | bytes 98312 | tf_op jit(solution)/shard_map/ppermute | solution.py:208
  79.1 18.5 %collective-permute-start.6 = (f32[32,256]{1,0:T(8,128)S(1)}, f32[32,256]{1,0:T(8,128)S(1)}, u32[]{:S(2)}, u32[]{:S(2)}) collective-permute-start(f32[32,256]{1,0:T(8,128)S(1)} %get-tuple-element.13), channel_id=1, source_target_pairs={{0,16},{8,24},{16,0},{24,8},{1,17},{9,25},{17,1},{25,9},{2,18},{10... | collective-permute-start | bytes 98312 | tf_op jit(solution)/shard_map/ppermute | solution.py:208
  82.5 15.1 %collective-permute-start.5 = (f32[32,256]{1,0:T(8,128)S(1)}, f32[32,256]{1,0:T(8,128)S(1)}, u32[]{:S(2)}, u32[]{:S(2)}) collective-permute-start(f32[32,256]{1,0:T(8,128)S(1)} %get-tuple-element.14), channel_id=1, source_target_pairs={{0,8},{8,16},{16,24},{24,0},{1,9},{9,17},{17,25},{25,1},{2,10},{10... | collective-permute-start | bytes 98312 | tf_op jit(solution)/shard_map/ppermute | solution.py:208
  94.0 5.4 %all-to-all-start.2 = ((f32[2,128,640]{2,1,0:T(8,128)}), f32[2,128,640]{2,1,0:T(8,128)S(1)}, u32[]{:S(2)}, u32[]{:S(2)}) async-start(f32[2,128,640]{2,1,0:T(8,128)} %shard_map.79), calls=%async_computation.2 | async-start | bytes 1310720 | tf_op jit(solution)/shard_map/all_to_all | solution.py:189
  134.1 9.4 %collective-permute-start.8 = (f32[2,640]{1,0:T(2,128)S(1)}, f32[2,640]{1,0:T(2,128)S(1)}, u32[]{:S(2)}, u32[]{:S(2)}) collective-permute-start(f32[2,640]{1,0:T(2,128)S(1)} %get-tuple-element.10), channel_id=1, source_target_pairs={{0,0},{2,16},{4,32},{6,48},{8,2},{10,18},{12,34},{14,50},{16,4},{1... | collective-permute-start | bytes 15368 | tf_op jit(solution)/shard_map/ppermute | solution.py:222

commit v4 on v3

--- a/solution.py
+++ b/solution.py
@@ -124,10 +124,10 @@
 
 
 def spread_kernel(w_ref, o_ref):
-    core = lax.axis_index("core")
+    zh = lax.axis_index("zh")
     for col in range(8):
         for y in range(8):
-            o_ref[y * 8 + col] = w_ref[pl.ds(col * 4 + 2 * core, 2)]
+            o_ref[y * 8 + col] = w_ref[col * 4 + zh]
 
 
 def pack_kernel(part_ref, c0, c1, c2, c3, o_ref, ladder_sum, cycle_sum):
@@ -152,18 +152,16 @@
         )
 
 
-def cycle_kernel(occ_ref, a_ref, own_ref, other_ref, vir_ref, pair_ref, o_ref, turned):
+def cycle_kernel(occ_ref, a_ref, w0, w1, w2, w3, vir_ref, pair_ref, o_ref, turned):
     first = (lax.axis_index("zl") * 4 + lax.axis_index("x")) * 4
-    core = lax.axis_index("core")
     total = jnp.zeros((256, 128), F32)
-    for half, w_ref in ((core, own_ref), (1 - core, other_ref)):
-        for s in range(2):
-            k = 2 * half + s
-            allowed = jnp.bitwise_xor(vir_ref[...], occ_ref[first + k]) == pair_ref[...]
-            w = jnp.where(allowed, w_ref[:, s].reshape(512, 128), 0.0)
-            ah, al = split(a_ref[:, k].reshape(256, 512))
-            wh, wl = split(w)
-            total = total + dot3(ah, al, wh, wl)
+    for s, w_ref in enumerate((w0, w1, w2, w3)):
+        k = lax.rem(lax.axis_index("zh") + 4 - s, 4)
+        allowed = jnp.bitwise_xor(vir_ref[...], occ_ref[first + k]) == pair_ref[...]
+        w = jnp.where(allowed, w_ref[...].reshape(512, 128), 0.0)
+        ah, al = split(a_ref[:, k].reshape(256, 512))
+        wh, wl = split(w)
+        total = total + dot3(ah, al, wh, wl)
     turned[...] = total.T
     for x in range(4):
         to = lax.rem(x + 4 - lax.axis_index("x"), 4)
@@ -171,10 +169,10 @@
             o_ref[to, pl.ds(2 * d, 2), :] = turned[pl.ds(8 * d + 2 * x, 2), :]
 
 
-def cycle(occ, amplitudes, own, other, vir, pair):
+def cycle(occ, amplitudes, w, vir, pair):
     return pl.pallas_call(
         cycle_kernel,
-        in_specs=[pl.BlockSpec(memory_space=pltpu.SMEM)] + [VMEM] * 5,
+        in_specs=[pl.BlockSpec(memory_space=pltpu.SMEM)] + [VMEM] * 7,
         out_specs=VMEM,
         out_shape=jax.ShapeDtypeStruct((4, 32, 256), F32),
         scratch_shapes=[pltpu.VMEM((128, 256), F32)],
@@ -182,7 +180,7 @@
         cost_estimate=pl.CostEstimate(
             flops=3 * 2 * 256 * 2048 * 128, bytes_accessed=3 * 2**20, transcendentals=0
         ),
-    )(occ, amplitudes, own, other, vir, pair)
+    )(occ, amplitudes, *w, vir, pair)
 
 
 def exchange(v, axes):
@@ -190,24 +188,26 @@
 
 
 def body(amplitudes, ladder_ints, cycle_ints, occ_irrep, vir_irrep, pair_irrep):
-    own = exchange(small(spread_kernel, (64, 2, 8, 128), cycle_ints), ("y", "zl", "x"))
+    w = exchange(small(spread_kernel, (64, 8, 128), cycle_ints), ("y", "zl", "x"))
 
     ring = [[(i, (i + s) % 4) for i in range(4)] for s in range(4)]
     sent = regroup(amplitudes)
     _, ladder_ints = lax.optimization_barrier((sent, ladder_ints))
-    sent, own = lax.optimization_barrier((sent, own))
+    sent, w = lax.optimization_barrier((sent, w))
     x = exchange(sent, ("y", "zl"))
-    other = lax.ppermute(own, "core", [(0, 1), (1, 0)])
     b1 = lax.ppermute(ladder_ints, "x", ring[1])
     b3 = lax.ppermute(ladder_ints, "x", ring[3])
-    near = lax.ppermute(b1[:32], "x", ring[1])
-    far = lax.ppermute(b3[32:], "x", ring[3])
+    w = [w] + [lax.ppermute(w, "zh", ring[s]) for s in (1, 2, 3)]
+    from_b1, from_b3, *w = lax.optimization_barrier((b1, b3, *w))
+    near = lax.ppermute(from_b1[:32], "x", ring[1])
+    far = lax.ppermute(from_b3[32:], "x", ring[3])
 
     vir = jnp.broadcast_to(vir_irrep[:, None], (512, 128))
-    parts = cycle(occ_irrep, amplitudes, own, other, vir, pair_irrep[None])
+    parts = cycle(occ_irrep, amplitudes, w, vir, pair_irrep[None])
     parts = [parts[0]] + [lax.ppermute(parts[s], "x", ring[s]) for s in (1, 2, 3)]
 
-    part = exchange(ladder(x, ladder_ints, b1, b3, near, far), ("core",))
+    part = ladder(x, ladder_ints, b1, b3, near, far)
+    part = exchange(part, ("core",))
     both = small(pack_kernel, (64, 2, 896), part, *parts, scratch=[(128, 640), (32, 256)])
     both = exchange(both, ("y", "zl", "zh"))
     part, cycle_part = small(finish_kernel, [(2, 640), (8, 2, 256)], both)

time: 145 us -> 167 us (1.15)
  starting transfers between devices: 50.7 us -> 65.6 us
  waiting for transfers between devices: 39.1 us -> 49.4 us
  blocking collectives: 34.5 us -> 32 us
    ppermute x3 -> x5, waiting for transfers between devices: 0.43 us -> 38.1 us  [the longest x3 35.9 us: body(): w = [w] + [lax.ppermute(w, 'zh', ring[s]) for s in (1, 2, 3)]]
    ppermute x1, waiting for transfers between devices: 22.3 us -> 0.01 us  [body(): b3 = lax.ppermute(ladder_ints, 'x', ring[3])]
    ppermute x3 -> x5, starting transfers between devices: 8.97 us -> 23.8 us  [the longest x3 16.8 us: body(): w = [w] + [lax.ppermute(w, 'zh', ring[s]) for s in (1, 2, 3)]]
    all_to_all x3, waiting for transfers between devices: 12.9 us -> 7.83 us  [exchange(): return lax.all_to_all(v, axes, split_axis=0, concat_axis=0, tiled=True)]
    all_to_all x1, blocking collectives: 34.5 us -> 32 us  [exchange(): return lax.all_to_all(v, axes, split_axis=0, concat_axis=0, tiled=True)]
  transfers between devices with their start and end apart: 12 -> 14, of which waited for: 5 -> 7; matrix products, arithmetic and copies ran while one was open for 1% -> 1% of each run, Pallas kernels for 10% -> 8%
where the time goes in v4:
time: 167 us
  starting transfers between devices  65.6 us (39%)
  waiting for transfers between devices  49.4 us (30%)
  blocking collectives  32 us (19%)
  Pallas kernels  14.7 us (9%)
  local copies, waits for them, and re-layouts  4.06 us (2%)
    ppermute x3, waiting for transfers between devices, body(): w = [w] + [lax.ppermute(w, 'zh', ring[s]) for s in (1, 2, 3)]  35.9 us
    all_to_all x1, blocking collectives, exchange(): return lax.all_to_all(v, axes, split_axis=0, concat_axis=0, tiled=True)  32 us
    all_to_all x3, starting transfers between devices, exchange(): return lax.all_to_all(v, axes, split_axis=0, concat_axis=0, tiled=True)  20.4 us
    ppermute x3, starting transfers between devices, body(): w = [w] + [lax.ppermute(w, 'zh', ring[s]) for s in (1, 2, 3)]  16.8 us
    ppermute x3, starting transfers between devices, body(): lax.ppermute(parts[s], 'x', ring[s])  8.97 us
    all_to_all x3, waiting for transfers between devices, exchange(): return lax.all_to_all(v, axes, split_axis=0, concat_axis=0, tiled=True)  7.83 us
    pallas_call x1, Pallas kernels, ladder(): pl.pallas_call(ladder_kernel, in_specs=[VMEM] * 3 + [anywhere] * 3, out_s...  7.44 us
    ppermute x1, starting transfers between devices, body(): ladder_resid = lax.ppermute(part, ('zl', 'x', 'zh'), move)  5.27 us
  transfers between devices with their start and end apart: 14, of which 7 were waited for; matrix products, arithmetic and copies ran while one was open for 1% of the time, Pallas kernels for 8%

profile of v4, /device:TPU:6, one launch (start us, length us, event | category | flops | bytes accessed | tf_op | source)
XLA Modules:
  0.0 166.6 jit_solution(16092878598422930160)
XLA Ops:
  0.6 0.0 copy-start.2
  0.6 0.9 copy-done.2
  1.5 0.7 shard_map.78
  2.3 12.4 %all-to-all-start = ((f32[64,8,128]{2,1,0:T(8,128)}), f32[64,8,128]{2,1,0:T(8,128)S(1)}, u32[]{:S(2)}, u32[]{:S(2)}) async-start(f32[64,8,128]{2,1,0:T(8,128)} %shard_map.78), calls=%async_computation | async-start | bytes 524288 | tf_op jit(solution)/shard_map/all_to_all | solution.py:187
  14.7 0.0 copy-start
  14.7 1.6 copy-done
  16.3 4.6 %shard_map.77 = f32[16,2,8,2048]{3,2,1,0:T(8,128)} custom-call(f32[4,2,2,64,512]{4,3,2,1,0:T(8,128)S(1)} %bitcast.12), custom_call_target="tpu_custom_call" | custom-call | flops 1048576 | bytes 4194304 | tf_op jit(solution)/shard_map/pallas_call | solution.py:51
  20.8 0.0 copy-start.6
  20.8 6.0 %all-to-all-done.w0 = f32[64,8,128]{2,1,0:T(8,128)S(1)} async-done(((f32[64,8,128]{2,1,0:T(8,128)}), f32[64,8,128]{2,1,0:T(8,128)S(1)}, u32[]{:S(2)}, u32[]{:S(2)}) %all-to-all-start) | async-done | bytes 262176 | tf_op jit(solution)/shard_map/all_to_all | solution.py:187
  26.9 4.4 %all-to-all-start.1 = ((f32[16,2,8,2048]{3,2,1,0:T(8,128)}), f32[16,2,8,2048]{3,2,1,0:T(8,128)}, u32[]{:S(2)}, u32[]{:S(2)}) async-start(f32[16,2,8,2048]{3,2,1,0:T(8,128)} %shard_map.77), calls=%async_computation.1 | async-start | bytes 4194304 | tf_op jit(solution)/shard_map/all_to_all | solution.py:187
  31.3 0.0 copy-done.6
  31.3 0.0 copy-start.7
  31.3 0.0 copy-start.1
  31.4 0.0 copy-start.3
  31.4 0.0 copy-start.4
  31.4 2.2 %collective-permute-start.1 = (f32[64,8,640]{2,1,0:T(8,128)S(1)}, f32[64,8,640]{2,1,0:T(8,128)S(1)}, u32[]{:S(2)}, u32[]{:S(2)}) collective-permute-start(f32[64,8,640]{2,1,0:T(8,128)S(1)} %copy-done.6), channel_id=1, source_target_pairs={{0,24},{8,0},{16,8},{24,16},{1,25},{9,1},{17,9},{25,17},{2,26},{10... | collective-permute-start | bytes 3932168 | tf_op jit(solution)/shard_map/ppermute | solution.py:199
  33.5 5.0 %collective-permute-start = (f32[64,8,640]{2,1,0:T(8,128)S(1)}, f32[64,8,640]{2,1,0:T(8,128)S(1)}, u32[]{:S(2)}, u32[]{:S(2)}) collective-permute-start(f32[64,8,640]{2,1,0:T(8,128)S(1)} %copy-done.6), channel_id=1, source_target_pairs={{0,8},{8,16},{16,24},{24,0},{1,9},{9,17},{17,25},{25,1},{2,10},{10... | collective-permute-start | bytes 3932168 | tf_op jit(solution)/shard_map/ppermute | solution.py:198
  38.6 10.0 %collective-permute-start.4 = (f32[64,8,128]{2,1,0:T(8,128)S(1)}, f32[64,8,128]{2,1,0:T(8,128)S(1)}, u32[]{:S(2)}, u32[]{:S(2)}) collective-permute-start(f32[64,8,128]{2,1,0:T(8,128)S(1)} %all-to-all-done.w0), channel_id=1, source_target_pairs={{0,6},{2,0},{4,2},{6,4},{1,7},{3,1},{5,3},{7,5},{8,14},{10,8},{12,... | collective-permute-start | bytes 786440 | tf_op jit(solution)/shard_map/ppermute | solution.py:200
  48.6 1.9 %collective-permute-start.3 = (f32[64,8,128]{2,1,0:T(8,128)S(1)}, f32[64,8,128]{2,1,0:T(8,128)S(1)}, u32[]{:S(2)}, u32[]{:S(2)}) collective-permute-start(f32[64,8,128]{2,1,0:T(8,128)S(1)} %all-to-all-done.w0), channel_id=1, source_target_pairs={{0,4},{2,6},{4,0},{6,2},{1,5},{3,7},{5,1},{7,3},{8,12},{10,14},{12... | collective-permute-start | bytes 786440 | tf_op jit(solution)/shard_map/ppermute | solution.py:200
  50.6 4.8 %collective-permute-start.2 = (f32[64,8,128]{2,1,0:T(8,128)S(1)}, f32[64,8,128]{2,1,0:T(8,128)S(1)}, u32[]{:S(2)}, u32[]{:S(2)}) collective-permute-start(f32[64,8,128]{2,1,0:T(8,128)S(1)} %all-to-all-done.w0), channel_id=1, source_target_pairs={{0,2},{2,4},{4,6},{6,0},{1,3},{3,5},{5,7},{7,1},{8,10},{10,12},{12... | collective-permute-start | bytes 786440 | tf_op jit(solution)/shard_map/ppermute | solution.py:200
  55.4 0.0 collective-permute-done.4.w3
  55.4 34.0 %collective-permute-done.3.w2 = f32[64,8,128]{2,1,0:T(8,128)S(1)} collective-permute-done((f32[64,8,128]{2,1,0:T(8,128)S(1)}, f32[64,8,128]{2,1,0:T(8,128)S(1)}, u32[]{:S(2)}, u32[]{:S(2)}) %collective-permute-start.3) | collective-permute-done | bytes 262176 | tf_op jit(solution)/shard_map/ppermute | solution.py:200
  89.4 1.8 %collective-permute-done.2.w1 = f32[64,8,128]{2,1,0:T(8,128)S(1)} collective-permute-done((f32[64,8,128]{2,1,0:T(8,128)S(1)}, f32[64,8,128]{2,1,0:T(8,128)S(1)}, u32[]{:S(2)}, u32[]{:S(2)}) %collective-permute-start.2) | collective-permute-done | bytes 262176 | tf_op jit(solution)/shard_map/ppermute | solution.py:200
  91.2 0.0 collective-permute-done.1.b3
  91.2 0.0 copy-start.5
  91.2 0.0 collective-permute-done.b1
  91.3 1.9 %collective-permute-start.6 = (f32[32,8,640]{2,1,0:T(8,128)S(1)}, f32[32,8,640]{2,1,0:T(8,128)S(1)}, u32[]{:S(2)}, u32[]{:S(2)}) collective-permute-start(f32[32,8,640]{2,1,0:T(8,128)S(1)} %slice.19), channel_id=1, source_target_pairs={{0,24},{8,0},{16,8},{24,16},{1,25},{9,1},{17,9},{25,17},{2,26},{10... | collective-permute-start | bytes 1966088 | tf_op jit(solution)/shard_map/ppermute | solution.py:203
  93.3 5.1 %collective-permute-start.5 = (f32[32,8,640]{2,1,0:T(8,128)S(1)}, f32[32,8,640]{2,1,0:T(8,128)S(1)}, u32[]{:S(2)}, u32[]{:S(2)}) collective-permute-start(f32[32,8,640]{2,1,0:T(8,128)S(1)} %slice.18), channel_id=1, source_target_pairs={{0,8},{8,16},{16,24},{24,0},{1,9},{9,17},{17,25},{25,1},{2,10},{10... | collective-permute-start | bytes 1966088 | tf_op jit(solution)/shard_map/ppermute | solution.py:202
  98.4 0.0 copy-done.5
  98.4 0.0 copy-done.7
  98.4 0.1 broadcast_in_dim.4.vir_ref
  98.6 0.0 copy-done.1
  98.6 0.0 copy-done.3
  98.6 0.0 copy-done.4
  98.6 1.8 %shard_map.80 = f32[4,32,256]{2,1,0:T(8,128)S(1)} custom-call(s32[32]{0:T(128)S(1)} %copy-done.3, f32[4,4,64,512]{3,2,1,0:T(8,128)S(1)} %copy-done.1, f32[64,8,128]{2,1,0:T(8,128)S(1)} %all-to-all-done.w0, f32[64,8,128]{2,1,0:T(8,128)S(1)} %collective-permute-done.2.w1, f32[64,8,128]{2,1,0:T(8,128)S(1)} %collective-permute-done.3.w2, ...), custom_call_target="tpu_custom_call" | custom-call | flops 402653184 | bytes 3145728 | tf_op jit(solution)/shard_map/pallas_call | solution.py:173
  100.4 1.9 %collective-permute-start.9 = (f32[32,256]{1,0:T(8,128)S(1)}, f32[32,256]{1,0:T(8,128)S(1)}, u32[]{:S(2)}, u32[]{:S(2)}) collective-permute-start(f32[32,256]{1,0:T(8,128)S(1)} %get-tuple-element.24), channel_id=1, source_target_pairs={{0,24},{8,0},{16,8},{24,16},{1,25},{9,1},{17,9},{25,17},{2,26},{10... | collective-permute-start | bytes 98312 | tf_op jit(solution)/shard_map/ppermute | solution.py:207
  102.3 3.4 %collective-permute-start.8 = (f32[32,256]{1,0:T(8,128)S(1)}, f32[32,256]{1,0:T(8,128)S(1)}, u32[]{:S(2)}, u32[]{:S(2)}) collective-permute-start(f32[32,256]{1,0:T(8,128)S(1)} %get-tuple-element.25), channel_id=1, source_target_pairs={{0,16},{8,24},{16,0},{24,8},{1,17},{9,25},{17,1},{25,9},{2,18},{10... | collective-permute-start | bytes 98312 | tf_op jit(solution)/shard_map/ppermute | solution.py:207
  105.7 3.7 %collective-permute-start.7 = (f32[32,256]{1,0:T(8,128)S(1)}, f32[32,256]{1,0:T(8,128)S(1)}, u32[]{:S(2)}, u32[]{:S(2)}) collective-permute-start(f32[32,256]{1,0:T(8,128)S(1)} %get-tuple-element.26), channel_id=1, source_target_pairs={{0,8},{8,16},{16,24},{24,0},{1,9},{9,17},{17,25},{25,1},{2,10},{10... | collective-permute-start | bytes 98312 | tf_op jit(solution)/shard_map/ppermute | solution.py:207
  109.4 1.1 collective-permute-done.6.far
  110.5 1.2 collective-permute-done.5.near
  111.7 0.0 all-to-all-done.1.x_ref
  111.7 7.4 %shard_map.79 = f32[2,128,640]{2,1,0:T(8,128)} custom-call(f32[16,2,8,2048]{3,2,1,0:T(8,128)} %all-to-all-done.1.x_ref, f32[64,8,640]{2,1,0:T(8,128)S(1)} %collective-permute-done.b1, f32[64,8,640]{2,1,0:T(8,128)} %copy-done.5, f32[64,8,640]{2,1,0:T(8,128)} %b0, f32[32,8,640]{2,1,0:T(8,128)S(1)} %collective-permute-done.5.near, ...), custom_call_target="tpu_custom_call" | custom-call | flops 2013265920 | bytes 8388608 | tf_op jit(solution)/shard_map/pallas_call | solution.py:113
  119.1 3.5 %all-to-all-start.2 = ((f32[2,128,640]{2,1,0:T(8,128)}), f32[2,128,640]{2,1,0:T(8,128)S(1)}, u32[]{:S(2)}, u32[]{:S(2)}) async-start(f32[2,128,640]{2,1,0:T(8,128)} %shard_map.79), calls=%async_computation.2 | async-start | bytes 1310720 | tf_op jit(solution)/shard_map/all_to_all | solution.py:187
  122.7 0.0 collective-permute-done.9.c3
  122.7 0.0 collective-permute-done.8.c2
  122.7 0.0 collective-permute-done.7.c1
  122.7 1.8 %all-to-all-done.2.part_ref = f32[2,128,640]{2,1,0:T(8,128)S(1)} async-done(((f32[2,128,640]{2,1,0:T(8,128)}), f32[2,128,640]{2,1,0:T(8,128)S(1)}, u32[]{:S(2)}, u32[]{:S(2)}) %all-to-all-start.2) | async-done | bytes 655392 | tf_op jit(solution)/shard_map/all_to_all | solution.py:187
  124.5 0.2 shard_map.81
  124.6 32.0 %all_to_all.20.p_ref = f32[64,2,896]{2,1,0:T(2,128)S(1)} all-to-all(f32[64,2,896]{2,1,0:T(2,128)S(1)} %shard_map.81), channel_id=1, replica_groups=mesh['y'=8,'zl'=2,'x'=4,'zh'=4,'core'=2] {'y','zl','zh'}, dimensions={0} | all-to-all | bytes 917504 | tf_op jit(solution)/shard_map/all_to_all | solution.py:187
  156.6 5.3 %collective-permute-start.10 = (f32[2,640]{1,0:T(2,128)S(1)}, f32[2,640]{1,0:T(2,128)S(1)}, u32[]{:S(2)}, u32[]{:S(2)}) collective-permute-start(f32[2,640]{1,0:T(2,128)S(1)} %get-tuple-element.22), channel_id=1, source_target_pairs={{0,0},{2,16},{4,32},{6,48},{8,2},{10,18},{12,34},{14,50},{16,4},{1... | collective-permute-start | bytes 15368 | tf_op jit(solution)/shard_map/ppermute | solution.py:222
  161.9 0.1 reshape.15
  162.0 0.6 copy.8
  162.6 3.4 %collective-permute-done.10 = f32[2,640]{1,0:T(2,128)S(1)} collective-permute-done((f32[2,640]{1,0:T(2,128)S(1)}, f32[2,640]{1,0:T(2,128)S(1)}, u32[]{:S(2)}, u32[]{:S(2)}) %collective-permute-start.10) | collective-permute-done | bytes 5152 | tf_op jit(solution)/shard_map/ppermute | solution.py:222
  166.1 0.6 copy.10
  (4 shorter events, 0.1 us)
Async XLA Ops:
  0.6 0.9 copy-start.2
  2.3 24.6 %all-to-all-start = ((f32[64,8,128]{2,1,0:T(8,128)}), f32[64,8,128]{2,1,0:T(8,128)S(1)}, u32[]{:S(2)}, u32[]{:S(2)}) async-start(f32[64,8,128]{2,1,0:T(8,128)} %shard_map.78), calls=%async_computation | async-start | bytes 524288 | tf_op jit(solution)/shard_map/all_to_all | solution.py:187
  14.7 1.6 copy-start
  20.8 10.5 %copy-start.6 = (f32[64,8,640]{2,1,0:T(8,128)S(1)}, f32[64,8,640]{2,1,0:T(8,128)}, u32[]{:S(2)}) copy-start(f32[64,8,640]{2,1,0:T(8,128)} %b0) | copy-start | bytes 3932164
  26.9 84.8 %all-to-all-start.1 = ((f32[16,2,8,2048]{3,2,1,0:T(8,128)}), f32[16,2,8,2048]{3,2,1,0:T(8,128)}, u32[]{:S(2)}, u32[]{:S(2)}) async-start(f32[16,2,8,2048]{3,2,1,0:T(8,128)} %shard_map.77), calls=%async_computation.1 | async-start | bytes 4194304 | tf_op jit(solution)/shard_map/all_to_all | solution.py:187
  31.3 67.1 %copy-start.7 = (s32[512]{0:T(512)S(1)}, s32[512]{0:T(512)}, u32[]{:S(2)}) copy-start(s32[512]{0:T(512)} %param.10) | copy-start | bytes 6148
  31.3 67.2 %copy-start.1 = (f32[4,4,64,512]{3,2,1,0:T(8,128)S(1)}, f32[4,4,64,512]{3,2,1,0:T(8,128)}, u32[]{:S(2)}) copy-start(f32[4,4,64,512]{3,2,1,0:T(8,128)} %a_ref.1) | copy-start | bytes 6291460
  31.4 67.2 %copy-start.3 = (s32[32]{0:T(128)S(1)}, s32[32]{0:T(128)}, u32[]{:S(2)}) copy-start(s32[32]{0:T(128)} %occ_ref.1) | copy-start | bytes 388
  31.4 67.2 %copy-start.4 = (s32[128]{0:T(128)S(1)}, s32[128]{0:T(128)}, u32[]{:S(2)}) copy-start(s32[128]{0:T(128)} %param.11) | copy-start | bytes 1540
  31.4 59.8 %collective-permute-start.1 = (f32[64,8,640]{2,1,0:T(8,128)S(1)}, f32[64,8,640]{2,1,0:T(8,128)S(1)}, u32[]{:S(2)}, u32[]{:S(2)}) collective-permute-start(f32[64,8,640]{2,1,0:T(8,128)S(1)} %copy-done.6), channel_id=1, source_target_pairs={{0,24},{8,0},{16,8},{24,16},{1,25},{9,1},{17,9},{25,17},{2,26},{10... | collective-permute-start | bytes 3932168 | tf_op jit(solution)/shard_map/ppermute | solution.py:199
  33.5 57.7 %collective-permute-start = (f32[64,8,640]{2,1,0:T(8,128)S(1)}, f32[64,8,640]{2,1,0:T(8,128)S(1)}, u32[]{:S(2)}, u32[]{:S(2)}) collective-permute-start(f32[64,8,640]{2,1,0:T(8,128)S(1)} %copy-done.6), channel_id=1, source_target_pairs={{0,8},{8,16},{16,24},{24,0},{1,9},{9,17},{17,25},{25,1},{2,10},{10... | collective-permute-start | bytes 3932168 | tf_op jit(solution)/shard_map/ppermute | solution.py:198
  38.6 16.8 %collective-permute-start.4 = (f32[64,8,128]{2,1,0:T(8,128)S(1)}, f32[64,8,128]{2,1,0:T(8,128)S(1)}, u32[]{:S(2)}, u32[]{:S(2)}) collective-permute-start(f32[64,8,128]{2,1,0:T(8,128)S(1)} %all-to-all-done.w0), channel_id=1, source_target_pairs={{0,6},{2,0},{4,2},{6,4},{1,7},{3,1},{5,3},{7,5},{8,14},{10,8},{12,... | collective-permute-start | bytes 786440 | tf_op jit(solution)/shard_map/ppermute | solution.py:200
  48.6 40.8 %collective-permute-start.3 = (f32[64,8,128]{2,1,0:T(8,128)S(1)}, f32[64,8,128]{2,1,0:T(8,128)S(1)}, u32[]{:S(2)}, u32[]{:S(2)}) collective-permute-start(f32[64,8,128]{2,1,0:T(8,128)S(1)} %all-to-all-done.w0), channel_id=1, source_target_pairs={{0,4},{2,6},{4,0},{6,2},{1,5},{3,7},{5,1},{7,3},{8,12},{10,14},{12... | collective-permute-start | bytes 786440 | tf_op jit(solution)/shard_map/ppermute | solution.py:200
  50.6 40.7 %collective-permute-start.2 = (f32[64,8,128]{2,1,0:T(8,128)S(1)}, f32[64,8,128]{2,1,0:T(8,128)S(1)}, u32[]{:S(2)}, u32[]{:S(2)}) collective-permute-start(f32[64,8,128]{2,1,0:T(8,128)S(1)} %all-to-all-done.w0), channel_id=1, source_target_pairs={{0,2},{2,4},{4,6},{6,0},{1,3},{3,5},{5,7},{7,1},{8,10},{10,12},{12... | collective-permute-start | bytes 786440 | tf_op jit(solution)/shard_map/ppermute | solution.py:200
  91.2 7.2 %copy-start.5 = (f32[64,8,640]{2,1,0:T(8,128)}, f32[64,8,640]{2,1,0:T(8,128)S(1)}, u32[]{:S(2)}) copy-start(f32[64,8,640]{2,1,0:T(8,128)S(1)} %collective-permute-done.1.b3) | copy-start | bytes 3932164
  91.3 19.2 %collective-permute-start.6 = (f32[32,8,640]{2,1,0:T(8,128)S(1)}, f32[32,8,640]{2,1,0:T(8,128)S(1)}, u32[]{:S(2)}, u32[]{:S(2)}) collective-permute-start(f32[32,8,640]{2,1,0:T(8,128)S(1)} %slice.19), channel_id=1, source_target_pairs={{0,24},{8,0},{16,8},{24,16},{1,25},{9,1},{17,9},{25,17},{2,26},{10... | collective-permute-start | bytes 1966088 | tf_op jit(solution)/shard_map/ppermute | solution.py:203
  93.3 18.4 %collective-permute-start.5 = (f32[32,8,640]{2,1,0:T(8,128)S(1)}, f32[32,8,640]{2,1,0:T(8,128)S(1)}, u32[]{:S(2)}, u32[]{:S(2)}) collective-permute-start(f32[32,8,640]{2,1,0:T(8,128)S(1)} %slice.18), channel_id=1, source_target_pairs={{0,8},{8,16},{16,24},{24,0},{1,9},{9,17},{17,25},{25,1},{2,10},{10... | collective-permute-start | bytes 1966088 | tf_op jit(solution)/shard_map/ppermute | solution.py:202
  100.4 22.3 %collective-permute-start.9 = (f32[32,256]{1,0:T(8,128)S(1)}, f32[32,256]{1,0:T(8,128)S(1)}, u32[]{:S(2)}, u32[]{:S(2)}) collective-permute-start(f32[32,256]{1,0:T(8,128)S(1)} %get-tuple-element.24), channel_id=1, source_target_pairs={{0,24},{8,0},{16,8},{24,16},{1,25},{9,1},{17,9},{25,17},{2,26},{10... | collective-permute-start | bytes 98312 | tf_op jit(solution)/shard_map/ppermute | solution.py:207
  102.3 20.3 %collective-permute-start.8 = (f32[32,256]{1,0:T(8,128)S(1)}, f32[32,256]{1,0:T(8,128)S(1)}, u32[]{:S(2)}, u32[]{:S(2)}) collective-permute-start(f32[32,256]{1,0:T(8,128)S(1)} %get-tuple-element.25), channel_id=1, source_target_pairs={{0,16},{8,24},{16,0},{24,8},{1,17},{9,25},{17,1},{25,9},{2,18},{10... | collective-permute-start | bytes 98312 | tf_op jit(solution)/shard_map/ppermute | solution.py:207
  105.7 17.0 %collective-permute-start.7 = (f32[32,256]{1,0:T(8,128)S(1)}, f32[32,256]{1,0:T(8,128)S(1)}, u32[]{:S(2)}, u32[]{:S(2)}) collective-permute-start(f32[32,256]{1,0:T(8,128)S(1)} %get-tuple-element.26), channel_id=1, source_target_pairs={{0,8},{8,16},{16,24},{24,0},{1,9},{9,17},{17,25},{25,1},{2,10},{10... | collective-permute-start | bytes 98312 | tf_op jit(solution)/shard_map/ppermute | solution.py:207
  119.1 5.4 %all-to-all-start.2 = ((f32[2,128,640]{2,1,0:T(8,128)}), f32[2,128,640]{2,1,0:T(8,128)S(1)}, u32[]{:S(2)}, u32[]{:S(2)}) async-start(f32[2,128,640]{2,1,0:T(8,128)} %shard_map.79), calls=%async_computation.2 | async-start | bytes 1310720 | tf_op jit(solution)/shard_map/all_to_all | solution.py:187
  156.6 9.4 %collective-permute-start.10 = (f32[2,640]{1,0:T(2,128)S(1)}, f32[2,640]{1,0:T(2,128)S(1)}, u32[]{:S(2)}, u32[]{:S(2)}) collective-permute-start(f32[2,640]{1,0:T(2,128)S(1)} %get-tuple-element.22), channel_id=1, source_target_pairs={{0,0},{2,16},{4,32},{6,48},{8,2},{10,18},{12,34},{14,50},{16,4},{1... | collective-permute-start | bytes 15368 | tf_op jit(solution)/shard_map/ppermute | solution.py:222

commit v5 on v3

--- a/solution.py
+++ b/solution.py
@@ -8,7 +8,7 @@
 F32 = jnp.float32
 BF16 = jnp.bfloat16
 VMEM_LIMIT = 16 * 1024 * 1024
-LADDER_LIMIT = 50 * 1024 * 1024
+LADDER_LIMIT = 51 * 1024 * 1024
 
 
 def split(v):
@@ -59,7 +59,7 @@
     )(a)
 
 
-def ladder_kernel(x_ref, b1, b3, b0, near, far, o_ref, held, sems):
+def ladder_kernel(x_ref, b1, b1_far, b3, b3_far, b0, near, far, o_ref, held, sems):
     me = lax.axis_index("x")
 
     def copies(k):
@@ -74,9 +74,9 @@
         for copy in copies(k):
             copy.start()
     for k in range(4):
-        part = pl.ds(k * 16, 16)
-        held[lax.rem(me + 1, 4), part] = b3[part]
-        held[lax.rem(me + 3, 4), part] = b1[part]
+        part, half = pl.ds(k * 16, 16), pl.ds(k % 2 * 16, 16)
+        held[lax.rem(me + 1, 4), part] = (b3 if k < 2 else b3_far)[half]
+        held[lax.rem(me + 3, 4), part] = (b1 if k < 2 else b1_far)[half]
         span = pl.ds(k * 512, 512)
         x = jnp.concatenate([x_ref[:, h, :, span].reshape(128, 512) for h in range(2)], axis=0)
         xh, xl = split(x)
@@ -108,11 +108,11 @@
     )(*args)
 
 
-def ladder(x, b0, b1, b3, near, far):
+def ladder(x, *blocks):
     anywhere = pl.BlockSpec(memory_space=pl.ANY)
     return pl.pallas_call(
         ladder_kernel,
-        in_specs=[VMEM] * 3 + [anywhere] * 3,
+        in_specs=[VMEM] * 5 + [anywhere] * 3,
         out_specs=VMEM,
         out_shape=jax.ShapeDtypeStruct((2, 128, 640), F32),
         scratch_shapes=[pltpu.VMEM((4, 64, 8, 640), F32), pltpu.SemaphoreType.DMA((2, 4))],
@@ -120,7 +120,7 @@
         cost_estimate=pl.CostEstimate(
             flops=3 * 2 * 256 * 2048 * 640, bytes_accessed=8 * 2**20, transcendentals=0
         ),
-    )(x, b1, b3, b0, near, far)
+    )(x, *blocks)
 
 
 def spread_kernel(w_ref, o_ref):
@@ -198,16 +198,20 @@
     sent, own = lax.optimization_barrier((sent, own))
     x = exchange(sent, ("y", "zl"))
     other = lax.ppermute(own, "core", [(0, 1), (1, 0)])
-    b1 = lax.ppermute(ladder_ints, "x", ring[1])
-    b3 = lax.ppermute(ladder_ints, "x", ring[3])
-    near = lax.ppermute(b1[:32], "x", ring[1])
-    far = lax.ppermute(b3[32:], "x", ring[3])
+    lower, upper = ladder_ints[:32], ladder_ints[32:]
+    b1 = lax.ppermute(lower, "x", ring[1])
+    b3_far = lax.ppermute(upper, "x", ring[3])
+    b1_far = lax.ppermute(upper, "x", ring[1])
+    b3 = lax.ppermute(lower, "x", ring[3])
+    near = lax.ppermute(b1, "x", ring[1])
+    far = lax.ppermute(b3_far, "x", ring[3])
 
     vir = jnp.broadcast_to(vir_irrep[:, None], (512, 128))
     parts = cycle(occ_irrep, amplitudes, own, other, vir, pair_irrep[None])
     parts = [parts[0]] + [lax.ppermute(parts[s], "x", ring[s]) for s in (1, 2, 3)]
 
-    part = exchange(ladder(x, ladder_ints, b1, b3, near, far), ("core",))
+    part = ladder(x, b1, b1_far, b3, b3_far, ladder_ints, near, far)
+    part = exchange(part, ("core",))
     both = small(pack_kernel, (64, 2, 896), part, *parts, scratch=[(128, 640), (32, 256)])
     both = exchange(both, ("y", "zl", "zh"))
     part, cycle_part = small(finish_kernel, [(2, 640), (8, 2, 256)], both)

time: 145 us -> 143 us (0.986)
  waiting for transfers between devices: 39.1 us -> 28.9 us
  starting transfers between devices: 50.7 us -> 57.6 us
    ppermute x4 -> x6, waiting for transfers between devices: 22.8 us -> 12.7 us  [the longest x1 4.52 us: body(): b1_far = lax.ppermute(upper, 'x', ring[1])]
    ppermute x4 -> x6, starting transfers between devices: 14.2 us -> 20.5 us  [the longest x1 5.59 us: body(): near = lax.ppermute(b1, 'x', ring[1])]
    unnamed x15 -> x19, local copies, waits for them, and re-layouts: 3.11 us -> 3.96 us
  transfers between devices with their start and end apart: 12 -> 14, of which waited for: 5 -> 8; matrix products, arithmetic and copies ran while one was open for 1% -> 1% of each run, Pallas kernels for 10% -> 10%
where the time goes in v5:
time: 143 us; the launch traced here: 142 us
  starting transfers between devices  57.6 us (40%)
  blocking collectives  34.8 us (24%)
  waiting for transfers between devices  28.9 us (20%)
  Pallas kernels  14.7 us (10%)
  local copies, waits for them, and re-layouts  4.91 us (3%)
    all_to_all x1, blocking collectives, exchange(): return lax.all_to_all(v, axes, split_axis=0, concat_axis=0, tiled=True)  34.8 us
    all_to_all x3, starting transfers between devices, exchange(): return lax.all_to_all(v, axes, split_axis=0, concat_axis=0, tiled=True)  20.4 us
    all_to_all x3, waiting for transfers between devices, exchange(): return lax.all_to_all(v, axes, split_axis=0, concat_axis=0, tiled=True)  12.8 us
    ppermute x3, starting transfers between devices, body(): lax.ppermute(parts[s], 'x', ring[s])  9.43 us
    pallas_call x1, Pallas kernels, ladder(): pl.pallas_call(ladder_kernel, in_specs=[VMEM] * 5 + [anywhere] * 3, out_s...  7.32 us
    ppermute x1, starting transfers between devices, body(): near = lax.ppermute(b1, 'x', ring[1])  5.59 us
    ppermute x1, starting transfers between devices, body(): ladder_resid = lax.ppermute(part, ('zl', 'x', 'zh'), move)  5.34 us
    ppermute x1, starting transfers between devices, body(): b1 = lax.ppermute(lower, 'x', ring[1])  4.75 us
  transfers between devices with their start and end apart: 14, of which 8 were waited for; matrix products, arithmetic and copies ran while one was open for 1% of the time, Pallas kernels for 10%

profile of v5, /device:TPU:6, one launch (start us, length us, event | category | flops | bytes accessed | tf_op | source)
XLA Modules:
  0.0 141.8 jit_solution(7313399592001601075)
XLA Ops:
  0.6 0.0 copy-start.2
  0.6 0.9 copy-done.2
  1.5 0.8 shard_map.78
  2.4 12.4 %all-to-all-start = ((f32[64,2,8,128]{3,2,1,0:T(8,128)}), f32[64,2,8,128]{3,2,1,0:T(8,128)S(1)}, u32[]{:S(2)}, u32[]{:S(2)}) async-start(f32[64,2,8,128]{3,2,1,0:T(8,128)} %shard_map.78), calls=%async_computation | async-start | bytes 1048576 | tf_op jit(solution)/shard_map/all_to_all | solution.py:189
  14.8 0.0 copy-start
  14.8 1.6 %copy-done = f32[4,4,64,512]{3,2,1,0:T(8,128)S(1)} copy-done((f32[4,4,64,512]{3,2,1,0:T(8,128)S(1)}, f32[4,4,64,512]{3,2,1,0:T(8,128)}, u32[]{:S(2)}) %copy-start) | copy-done | bytes 2097176
  16.4 4.6 %shard_map.77 = f32[16,2,8,2048]{3,2,1,0:T(8,128)} custom-call(f32[4,2,2,64,512]{4,3,2,1,0:T(8,128)S(1)} %bitcast.12), custom_call_target="tpu_custom_call" | custom-call | flops 1048576 | bytes 4194304 | tf_op jit(solution)/shard_map/pallas_call | solution.py:51
  21.0 0.0 copy-start.5
  21.0 11.0 %all-to-all-done.own_ref = f32[64,2,8,128]{3,2,1,0:T(8,128)S(1)} async-done(((f32[64,2,8,128]{3,2,1,0:T(8,128)}), f32[64,2,8,128]{3,2,1,0:T(8,128)S(1)}, u32[]{:S(2)}, u32[]{:S(2)}) %all-to-all-start) | async-done | bytes 524320 | tf_op jit(solution)/shard_map/all_to_all | solution.py:189
  32.0 4.5 %all-to-all-start.1 = ((f32[16,2,8,2048]{3,2,1,0:T(8,128)}), f32[16,2,8,2048]{3,2,1,0:T(8,128)}, u32[]{:S(2)}, u32[]{:S(2)}) async-start(f32[16,2,8,2048]{3,2,1,0:T(8,128)} %shard_map.77), calls=%async_computation.1 | async-start | bytes 4194304 | tf_op jit(solution)/shard_map/all_to_all | solution.py:189
  36.5 0.0 copy-done.5
  36.5 0.0 copy-start.8
  36.5 0.0 copy-start.1
  36.5 0.0 copy-start.3
  36.5 0.0 copy-start.4
  36.5 0.1 fusion
  36.6 2.4 %collective-permute-start.3 = (f32[32,8,640]{2,1,0:T(8,128)S(1)}, f32[32,8,640]{2,1,0:T(8,128)S(1)}, u32[]{:S(2)}, u32[]{:S(2)}) collective-permute-start(f32[32,8,640]{2,1,0:T(8,128)S(1)} %get-tuple-element.12), channel_id=1, source_target_pairs={{0,24},{8,0},{16,8},{24,16},{1,25},{9,1},{17,9},{25,17},{2,26},{10... | collective-permute-start | bytes 1966088 | tf_op jit(solution)/shard_map/ppermute | solution.py:203
  39.1 4.8 %collective-permute-start = (f32[32,8,640]{2,1,0:T(8,128)S(1)}, f32[32,8,640]{2,1,0:T(8,128)S(1)}, u32[]{:S(2)}, u32[]{:S(2)}) collective-permute-start(f32[32,8,640]{2,1,0:T(8,128)S(1)} %get-tuple-element.13), channel_id=1, source_target_pairs={{0,8},{8,16},{16,24},{24,0},{1,9},{9,17},{17,25},{25,1},{2,10},{10... | collective-permute-start | bytes 1966088 | tf_op jit(solution)/shard_map/ppermute | solution.py:202
  43.8 1.9 %collective-permute-start.6 = (f32[64,2,8,128]{3,2,1,0:T(8,128)S(1)}, f32[64,2,8,128]{3,2,1,0:T(8,128)S(1)}, u32[]{:S(2)}, u32[]{:S(2)}) collective-permute-start(f32[64,2,8,128]{3,2,1,0:T(8,128)S(1)} %all-to-all-done.own_ref), channel_id=1, source_target_pairs={{0,1},{1,0},{2,3},{3,2},{4,5},{5,4},{6,7},{7,6},{8,9},{9,8},{10,11... | collective-permute-start | bytes 1572872 | tf_op jit(solution)/shard_map/ppermute | solution.py:200
  45.8 2.0 %collective-permute-start.1 = (f32[32,8,640]{2,1,0:T(8,128)S(1)}, f32[32,8,640]{2,1,0:T(8,128)S(1)}, u32[]{:S(2)}, u32[]{:S(2)}) collective-permute-start(f32[32,8,640]{2,1,0:T(8,128)S(1)} %get-tuple-element.12), channel_id=1, source_target_pairs={{0,8},{8,16},{16,24},{24,0},{1,9},{9,17},{17,25},{25,1},{2,10},{10... | collective-permute-start | bytes 1966088 | tf_op jit(solution)/shard_map/ppermute | solution.py:204
  47.8 3.8 %collective-permute-start.2 = (f32[32,8,640]{2,1,0:T(8,128)S(1)}, f32[32,8,640]{2,1,0:T(8,128)S(1)}, u32[]{:S(2)}, u32[]{:S(2)}) collective-permute-start(f32[32,8,640]{2,1,0:T(8,128)S(1)} %get-tuple-element.13), channel_id=1, source_target_pairs={{0,24},{8,0},{16,8},{24,16},{1,25},{9,1},{17,9},{25,17},{2,26},{10... | collective-permute-start | bytes 1966088 | tf_op jit(solution)/shard_map/ppermute | solution.py:205
  51.6 2.2 %collective-permute-done.3.b3_far = f32[32,8,640]{2,1,0:T(8,128)S(1)} collective-permute-done((f32[32,8,640]{2,1,0:T(8,128)S(1)}, f32[32,8,640]{2,1,0:T(8,128)S(1)}, u32[]{:S(2)}, u32[]{:S(2)}) %collective-permute-start.3) | collective-permute-done | bytes 655392 | tf_op jit(solution)/shard_map/ppermute | solution.py:203
  53.8 0.0 copy-start.6
  53.8 1.9 %collective-permute-start.5 = (f32[32,8,640]{2,1,0:T(8,128)S(1)}, f32[32,8,640]{2,1,0:T(8,128)S(1)}, u32[]{:S(2)}, u32[]{:S(2)}) collective-permute-start(f32[32,8,640]{2,1,0:T(8,128)S(1)} %collective-permute-done.3.b3_far), channel_id=1, source_target_pairs={{0,24},{8,0},{16,8},{24,16},{1,25},{9,1},{17,9},{25,17},{2,26},{10... | collective-permute-start | bytes 1966088 | tf_op jit(solution)/shard_map/ppermute | solution.py:207
  55.7 3.2 %collective-permute-done.b1 = f32[32,8,640]{2,1,0:T(8,128)S(1)} collective-permute-done((f32[32,8,640]{2,1,0:T(8,128)S(1)}, f32[32,8,640]{2,1,0:T(8,128)S(1)}, u32[]{:S(2)}, u32[]{:S(2)}) %collective-permute-start) | collective-permute-done | bytes 655392 | tf_op jit(solution)/shard_map/ppermute | solution.py:202
  59.0 5.6 %collective-permute-start.4 = (f32[32,8,640]{2,1,0:T(8,128)S(1)}, f32[32,8,640]{2,1,0:T(8,128)}, u32[]{:S(2)}, u32[]{:S(2)}) collective-permute-start(f32[32,8,640]{2,1,0:T(8,128)S(1)} %collective-permute-done.b1), channel_id=1, source_target_pairs={{0,8},{8,16},{16,24},{24,0},{1,9},{9,17},{17,25},{25,1},{2,10},{10... | collective-permute-start | bytes 1966088 | tf_op jit(solution)/shard_map/ppermute | solution.py:206
  64.6 0.0 collective-permute-done.6.other_ref
  64.6 0.0 copy-done.8
  64.6 0.1 broadcast_in_dim.4.vir_ref
  64.7 0.0 copy-done.1
  64.8 0.0 copy-done.3
  64.8 0.0 copy-done.4
  64.8 1.8 %shard_map.80 = f32[4,32,256]{2,1,0:T(8,128)S(1)} custom-call(s32[32]{0:T(128)S(1)} %copy-done.3, f32[4,4,64,512]{3,2,1,0:T(8,128)S(1)} %copy-done.1, f32[64,2,8,128]{3,2,1,0:T(8,128)S(1)} %all-to-all-done.own_ref, f32[64,2,8,128]{3,2,1,0:T(8,128)S(1)} %collective-permute-done.6.other_ref, s32[512,128]{1,0:T(8,128)S(1)} %broadcast_in_dim.4.vir_ref, ...), custom_call_target="tpu_custom_call" | custom-call | flops 402653184 | bytes 3145728 | tf_op jit(solution)/shard_map/pallas_call | solution.py:175
  66.6 1.9 %collective-permute-start.9 = (f32[32,256]{1,0:T(8,128)S(1)}, f32[32,256]{1,0:T(8,128)S(1)}, u32[]{:S(2)}, u32[]{:S(2)}) collective-permute-start(f32[32,256]{1,0:T(8,128)S(1)} %get-tuple-element.14), channel_id=1, source_target_pairs={{0,24},{8,0},{16,8},{24,16},{1,25},{9,1},{17,9},{25,17},{2,26},{10... | collective-permute-start | bytes 98312 | tf_op jit(solution)/shard_map/ppermute | solution.py:211
  68.5 4.5 %collective-permute-done.1.b1_far = f32[32,8,640]{2,1,0:T(8,128)S(1)} collective-permute-done((f32[32,8,640]{2,1,0:T(8,128)S(1)}, f32[32,8,640]{2,1,0:T(8,128)S(1)}, u32[]{:S(2)}, u32[]{:S(2)}) %collective-permute-start.1) | collective-permute-done | bytes 655392 | tf_op jit(solution)/shard_map/ppermute | solution.py:204
  73.0 3.9 %collective-permute-start.8 = (f32[32,256]{1,0:T(8,128)S(1)}, f32[32,256]{1,0:T(8,128)S(1)}, u32[]{:S(2)}, u32[]{:S(2)}) collective-permute-start(f32[32,256]{1,0:T(8,128)S(1)} %get-tuple-element.15), channel_id=1, source_target_pairs={{0,16},{8,24},{16,0},{24,8},{1,17},{9,25},{17,1},{25,9},{2,18},{10... | collective-permute-start | bytes 98312 | tf_op jit(solution)/shard_map/ppermute | solution.py:211
  77.0 0.0 collective-permute-done.2.b3
  77.0 3.6 %collective-permute-start.7 = (f32[32,256]{1,0:T(8,128)S(1)}, f32[32,256]{1,0:T(8,128)S(1)}, u32[]{:S(2)}, u32[]{:S(2)}) collective-permute-start(f32[32,256]{1,0:T(8,128)S(1)} %get-tuple-element.16), channel_id=1, source_target_pairs={{0,8},{8,16},{16,24},{24,0},{1,9},{9,17},{17,25},{25,1},{2,10},{10... | collective-permute-start | bytes 98312 | tf_op jit(solution)/shard_map/ppermute | solution.py:211
  80.6 2.1 %collective-permute-done.5.far = f32[32,8,640]{2,1,0:T(8,128)S(1)} collective-permute-done((f32[32,8,640]{2,1,0:T(8,128)S(1)}, f32[32,8,640]{2,1,0:T(8,128)S(1)}, u32[]{:S(2)}, u32[]{:S(2)}) %collective-permute-start.5) | collective-permute-done | bytes 655392 | tf_op jit(solution)/shard_map/ppermute | solution.py:207
  82.7 0.0 copy-start.7
  82.7 0.9 copy-done.7
  83.5 0.6 collective-permute-done.4.near
  84.2 0.0 all-to-all-done.1.x_ref
  84.2 0.0 copy-done.6
  84.2 7.3 %shard_map.79 = f32[2,128,640]{2,1,0:T(8,128)} custom-call(f32[16,2,8,2048]{3,2,1,0:T(8,128)} %all-to-all-done.1.x_ref, f32[32,8,640]{2,1,0:T(8,128)S(1)} %collective-permute-done.b1, f32[32,8,640]{2,1,0:T(8,128)S(1)} %collective-permute-done.1.b1_far, f32[32,8,640]{2,1,0:T(8,128)S(1)} %collective-permute-done.2.b3, f32[32,8,640]{2,1,0:T(8,128)} %copy-done.6, ...), custom_call_target="tpu_custom_call" | custom-call | flops 2013265920 | bytes 8388608 | tf_op jit(solution)/shard_map/pallas_call | solution.py:113
  91.5 3.5 %all-to-all-start.2 = ((f32[2,128,640]{2,1,0:T(8,128)}), f32[2,128,640]{2,1,0:T(8,128)S(1)}, u32[]{:S(2)}, u32[]{:S(2)}) async-start(f32[2,128,640]{2,1,0:T(8,128)} %shard_map.79), calls=%async_computation.2 | async-start | bytes 1310720 | tf_op jit(solution)/shard_map/all_to_all | solution.py:189
  95.0 0.0 collective-permute-done.9.c3
  95.1 0.0 collective-permute-done.8.c2
  95.1 0.0 collective-permute-done.7.c1
  95.1 1.8 %all-to-all-done.2.part_ref = f32[2,128,640]{2,1,0:T(8,128)S(1)} async-done(((f32[2,128,640]{2,1,0:T(8,128)}), f32[2,128,640]{2,1,0:T(8,128)S(1)}, u32[]{:S(2)}, u32[]{:S(2)}) %all-to-all-start.2) | async-done | bytes 655392 | tf_op jit(solution)/shard_map/all_to_all | solution.py:189
  96.9 0.2 shard_map.81
  97.0 34.8 %all_to_all.20.p_ref = f32[64,2,896]{2,1,0:T(2,128)S(1)} all-to-all(f32[64,2,896]{2,1,0:T(2,128)S(1)} %shard_map.81), channel_id=1, replica_groups=mesh['y'=8,'zl'=2,'x'=4,'zh'=4,'core'=2] {'y','zl','zh'}, dimensions={0} | all-to-all | bytes 917504 | tf_op jit(solution)/shard_map/all_to_all | solution.py:189
  131.8 5.3 %collective-permute-start.10 = (f32[2,640]{1,0:T(2,128)S(1)}, f32[2,640]{1,0:T(2,128)S(1)}, u32[]{:S(2)}, u32[]{:S(2)}) collective-permute-start(f32[2,640]{1,0:T(2,128)S(1)} %get-tuple-element.10), channel_id=1, source_target_pairs={{0,0},{2,16},{4,32},{6,48},{8,2},{10,18},{12,34},{14,50},{16,4},{1... | collective-permute-start | bytes 15368 | tf_op jit(solution)/shard_map/ppermute | solution.py:226
  137.2 0.1 reshape.15
  137.3 0.6 copy.8
  137.9 3.3 %collective-permute-done.10 = f32[2,640]{1,0:T(2,128)S(1)} collective-permute-done((f32[2,640]{1,0:T(2,128)S(1)}, f32[2,640]{1,0:T(2,128)S(1)}, u32[]{:S(2)}, u32[]{:S(2)}) %collective-permute-start.10) | collective-permute-done | bytes 5152 | tf_op jit(solution)/shard_map/ppermute | solution.py:226
  141.2 0.6 copy.10
  (2 shorter events, 0.0 us)
Async XLA Ops:
  0.6 0.9 copy-start.2
  2.4 29.6 %all-to-all-start = ((f32[64,2,8,128]{3,2,1,0:T(8,128)}), f32[64,2,8,128]{3,2,1,0:T(8,128)S(1)}, u32[]{:S(2)}, u32[]{:S(2)}) async-start(f32[64,2,8,128]{3,2,1,0:T(8,128)} %shard_map.78), calls=%async_computation | async-start | bytes 1048576 | tf_op jit(solution)/shard_map/all_to_all | solution.py:189
  14.8 1.6 %copy-start = (f32[4,4,64,512]{3,2,1,0:T(8,128)S(1)}, f32[4,4,64,512]{3,2,1,0:T(8,128)}, u32[]{:S(2)}) copy-start(f32[4,4,64,512]{3,2,1,0:T(8,128)} %a_ref.1) | copy-start | bytes 6291460
  21.0 15.5 %copy-start.5 = (f32[64,8,640]{2,1,0:T(8,128)S(1)}, f32[64,8,640]{2,1,0:T(8,128)}, u32[]{:S(2)}) copy-start(f32[64,8,640]{2,1,0:T(8,128)} %b0) | copy-start | bytes 3932164
  32.0 52.2 %all-to-all-start.1 = ((f32[16,2,8,2048]{3,2,1,0:T(8,128)}), f32[16,2,8,2048]{3,2,1,0:T(8,128)}, u32[]{:S(2)}, u32[]{:S(2)}) async-start(f32[16,2,8,2048]{3,2,1,0:T(8,128)} %shard_map.77), calls=%async_computation.1 | async-start | bytes 4194304 | tf_op jit(solution)/shard_map/all_to_all | solution.py:189
  36.5 28.1 %copy-start.8 = (s32[512]{0:T(512)S(1)}, s32[512]{0:T(512)}, u32[]{:S(2)}) copy-start(s32[512]{0:T(512)} %param.10) | copy-start | bytes 6148
  36.5 28.3 %copy-start.1 = (f32[4,4,64,512]{3,2,1,0:T(8,128)S(1)}, f32[4,4,64,512]{3,2,1,0:T(8,128)}, u32[]{:S(2)}) copy-start(f32[4,4,64,512]{3,2,1,0:T(8,128)} %a_ref.1) | copy-start | bytes 6291460
  36.5 28.2 %copy-start.3 = (s32[32]{0:T(128)S(1)}, s32[32]{0:T(128)}, u32[]{:S(2)}) copy-start(s32[32]{0:T(128)} %occ_ref.1) | copy-start | bytes 388
  36.5 28.2 %copy-start.4 = (s32[128]{0:T(128)S(1)}, s32[128]{0:T(128)}, u32[]{:S(2)}) copy-start(s32[128]{0:T(128)} %param.11) | copy-start | bytes 1540
  36.6 17.2 %collective-permute-start.3 = (f32[32,8,640]{2,1,0:T(8,128)S(1)}, f32[32,8,640]{2,1,0:T(8,128)S(1)}, u32[]{:S(2)}, u32[]{:S(2)}) collective-permute-start(f32[32,8,640]{2,1,0:T(8,128)S(1)} %get-tuple-element.12), channel_id=1, source_target_pairs={{0,24},{8,0},{16,8},{24,16},{1,25},{9,1},{17,9},{25,17},{2,26},{10... | collective-permute-start | bytes 1966088 | tf_op jit(solution)/shard_map/ppermute | solution.py:203
  39.1 19.9 %collective-permute-start = (f32[32,8,640]{2,1,0:T(8,128)S(1)}, f32[32,8,640]{2,1,0:T(8,128)S(1)}, u32[]{:S(2)}, u32[]{:S(2)}) collective-permute-start(f32[32,8,640]{2,1,0:T(8,128)S(1)} %get-tuple-element.13), channel_id=1, source_target_pairs={{0,8},{8,16},{16,24},{24,0},{1,9},{9,17},{17,25},{25,1},{2,10},{10... | collective-permute-start | bytes 1966088 | tf_op jit(solution)/shard_map/ppermute | solution.py:202
  43.8 20.8 %collective-permute-start.6 = (f32[64,2,8,128]{3,2,1,0:T(8,128)S(1)}, f32[64,2,8,128]{3,2,1,0:T(8,128)S(1)}, u32[]{:S(2)}, u32[]{:S(2)}) collective-permute-start(f32[64,2,8,128]{3,2,1,0:T(8,128)S(1)} %all-to-all-done.own_ref), channel_id=1, source_target_pairs={{0,1},{1,0},{2,3},{3,2},{4,5},{5,4},{6,7},{7,6},{8,9},{9,8},{10,11... | collective-permute-start | bytes 1572872 | tf_op jit(solution)/shard_map/ppermute | solution.py:200
  45.8 27.3 %collective-permute-start.1 = (f32[32,8,640]{2,1,0:T(8,128)S(1)}, f32[32,8,640]{2,1,0:T(8,128)S(1)}, u32[]{:S(2)}, u32[]{:S(2)}) collective-permute-start(f32[32,8,640]{2,1,0:T(8,128)S(1)} %get-tuple-element.12), channel_id=1, source_target_pairs={{0,8},{8,16},{16,24},{24,0},{1,9},{9,17},{17,25},{25,1},{2,10},{10... | collective-permute-start | bytes 1966088 | tf_op jit(solution)/shard_map/ppermute | solution.py:204
  47.8 29.2 %collective-permute-start.2 = (f32[32,8,640]{2,1,0:T(8,128)S(1)}, f32[32,8,640]{2,1,0:T(8,128)S(1)}, u32[]{:S(2)}, u32[]{:S(2)}) collective-permute-start(f32[32,8,640]{2,1,0:T(8,128)S(1)} %get-tuple-element.13), channel_id=1, source_target_pairs={{0,24},{8,0},{16,8},{24,16},{1,25},{9,1},{17,9},{25,17},{2,26},{10... | collective-permute-start | bytes 1966088 | tf_op jit(solution)/shard_map/ppermute | solution.py:205
  53.8 30.4 %copy-start.6 = (f32[32,8,640]{2,1,0:T(8,128)}, f32[32,8,640]{2,1,0:T(8,128)S(1)}, u32[]{:S(2)}) copy-start(f32[32,8,640]{2,1,0:T(8,128)S(1)} %collective-permute-done.3.b3_far) | copy-start | bytes 1966084
  53.8 28.9 %collective-permute-start.5 = (f32[32,8,640]{2,1,0:T(8,128)S(1)}, f32[32,8,640]{2,1,0:T(8,128)S(1)}, u32[]{:S(2)}, u32[]{:S(2)}) collective-permute-start(f32[32,8,640]{2,1,0:T(8,128)S(1)} %collective-permute-done.3.b3_far), channel_id=1, source_target_pairs={{0,24},{8,0},{16,8},{24,16},{1,25},{9,1},{17,9},{25,17},{2,26},{10... | collective-permute-start | bytes 1966088 | tf_op jit(solution)/shard_map/ppermute | solution.py:207
  59.0 25.2 %collective-permute-start.4 = (f32[32,8,640]{2,1,0:T(8,128)S(1)}, f32[32,8,640]{2,1,0:T(8,128)}, u32[]{:S(2)}, u32[]{:S(2)}) collective-permute-start(f32[32,8,640]{2,1,0:T(8,128)S(1)} %collective-permute-done.b1), channel_id=1, source_target_pairs={{0,8},{8,16},{16,24},{24,0},{1,9},{9,17},{17,25},{25,1},{2,10},{10... | collective-permute-start | bytes 1966088 | tf_op jit(solution)/shard_map/ppermute | solution.py:206
  66.6 28.5 %collective-permute-start.9 = (f32[32,256]{1,0:T(8,128)S(1)}, f32[32,256]{1,0:T(8,128)S(1)}, u32[]{:S(2)}, u32[]{:S(2)}) collective-permute-start(f32[32,256]{1,0:T(8,128)S(1)} %get-tuple-element.14), channel_id=1, source_target_pairs={{0,24},{8,0},{16,8},{24,16},{1,25},{9,1},{17,9},{25,17},{2,26},{10... | collective-permute-start | bytes 98312 | tf_op jit(solution)/shard_map/ppermute | solution.py:211
  73.0 22.0 %collective-permute-start.8 = (f32[32,256]{1,0:T(8,128)S(1)}, f32[32,256]{1,0:T(8,128)S(1)}, u32[]{:S(2)}, u32[]{:S(2)}) collective-permute-start(f32[32,256]{1,0:T(8,128)S(1)} %get-tuple-element.15), channel_id=1, source_target_pairs={{0,16},{8,24},{16,0},{24,8},{1,17},{9,25},{17,1},{25,9},{2,18},{10... | collective-permute-start | bytes 98312 | tf_op jit(solution)/shard_map/ppermute | solution.py:211
  77.0 18.1 %collective-permute-start.7 = (f32[32,256]{1,0:T(8,128)S(1)}, f32[32,256]{1,0:T(8,128)S(1)}, u32[]{:S(2)}, u32[]{:S(2)}) collective-permute-start(f32[32,256]{1,0:T(8,128)S(1)} %get-tuple-element.16), channel_id=1, source_target_pairs={{0,8},{8,16},{16,24},{24,0},{1,9},{9,17},{17,25},{25,1},{2,10},{10... | collective-permute-start | bytes 98312 | tf_op jit(solution)/shard_map/ppermute | solution.py:211
  82.7 0.9 copy-start.7
  91.5 5.4 %all-to-all-start.2 = ((f32[2,128,640]{2,1,0:T(8,128)}), f32[2,128,640]{2,1,0:T(8,128)S(1)}, u32[]{:S(2)}, u32[]{:S(2)}) async-start(f32[2,128,640]{2,1,0:T(8,128)} %shard_map.79), calls=%async_computation.2 | async-start | bytes 1310720 | tf_op jit(solution)/shard_map/all_to_all | solution.py:189
  131.8 9.4 %collective-permute-start.10 = (f32[2,640]{1,0:T(2,128)S(1)}, f32[2,640]{1,0:T(2,128)S(1)}, u32[]{:S(2)}, u32[]{:S(2)}) collective-permute-start(f32[2,640]{1,0:T(2,128)S(1)} %get-tuple-element.10), channel_id=1, source_target_pairs={{0,0},{2,16},{4,32},{6,48},{8,2},{10,18},{12,34},{14,50},{16,4},{1... | collective-permute-start | bytes 15368 | tf_op jit(solution)/shard_map/ppermute | solution.py:226

commit v6 on v5

--- a/solution.py
+++ b/solution.py
@@ -59,30 +59,18 @@
     )(a)
 
 
-def ladder_kernel(x_ref, b1, b1_far, b3, b3_far, b0, near, far, o_ref, held, sems):
+def ladder_kernel(x_ref, b1, b1_far, b3, b3_far, near, far, b0, o_ref, held):
     me = lax.axis_index("x")
-
-    def copies(k):
-        part = pl.ds(k * 16, 16)
-        across = (near if k < 2 else far).at[pl.ds(k % 2 * 16, 16)]
-        return (
-            pltpu.make_async_copy(b0.at[part], held.at[me, part], sems.at[0, k]),
-            pltpu.make_async_copy(across, held.at[lax.rem(me + 2, 4), part], sems.at[1, k]),
-        )
-
     for k in range(4):
-        for copy in copies(k):
-            copy.start()
-    for k in range(4):
-        part, half = pl.ds(k * 16, 16), pl.ds(k % 2 * 16, 16)
-        held[lax.rem(me + 1, 4), part] = (b3 if k < 2 else b3_far)[half]
-        held[lax.rem(me + 3, 4), part] = (b1 if k < 2 else b1_far)[half]
+        half = pl.ds(k % 2 * 16, 16)
+        held[me] = b0[pl.ds(k * 16, 16)]
+        held[lax.rem(me + 1, 4)] = (b3 if k < 2 else b3_far)[half]
+        held[lax.rem(me + 2, 4)] = (near if k < 2 else far)[half]
+        held[lax.rem(me + 3, 4)] = (b1 if k < 2 else b1_far)[half]
         span = pl.ds(k * 512, 512)
         x = jnp.concatenate([x_ref[:, h, :, span].reshape(128, 512) for h in range(2)], axis=0)
         xh, xl = split(x)
-        for copy in copies(k):
-            copy.wait()
-        b = [held[o, k * 16 + c] for c in range(16) for o in range(4)]
+        b = [held[o, c] for c in range(16) for o in range(4)]
         bh, bl = split(jnp.concatenate(b, axis=0))
         total = dot3(xh, xl, bh, bl).reshape(2, 128, 640)
         if k == 0:
@@ -109,13 +97,12 @@
 
 
 def ladder(x, *blocks):
-    anywhere = pl.BlockSpec(memory_space=pl.ANY)
     return pl.pallas_call(
         ladder_kernel,
-        in_specs=[VMEM] * 5 + [anywhere] * 3,
+        in_specs=[VMEM] * 8,
         out_specs=VMEM,
         out_shape=jax.ShapeDtypeStruct((2, 128, 640), F32),
-        scratch_shapes=[pltpu.VMEM((4, 64, 8, 640), F32), pltpu.SemaphoreType.DMA((2, 4))],
+        scratch_shapes=[pltpu.VMEM((4, 16, 8, 640), F32)],
         compiler_params=pltpu.CompilerParams(vmem_limit_bytes=LADDER_LIMIT),
         cost_estimate=pl.CostEstimate(
             flops=3 * 2 * 256 * 2048 * 640, bytes_accessed=8 * 2**20, transcendentals=0
@@ -210,7 +197,7 @@
     parts = cycle(occ_irrep, amplitudes, own, other, vir, pair_irrep[None])
     parts = [parts[0]] + [lax.ppermute(parts[s], "x", ring[s]) for s in (1, 2, 3)]
 
-    part = ladder(x, b1, b1_far, b3, b3_far, ladder_ints, near, far)
+    part = ladder(x, b1, b1_far, b3, b3_far, near, far, ladder_ints)
     part = exchange(part, ("core",))
     both = small(pack_kernel, (64, 2, 896), part, *parts, scratch=[(128, 640), (32, 256)])
     both = exchange(both, ("y", "zl", "zh"))

time: 143 us -> 142 us (level)
  no operation moved by 1% of the time
where the time goes in v6:
time: 142 us
  starting transfers between devices  57.6 us (41%)
  blocking collectives  34.8 us (25%)
  waiting for transfers between devices  28.9 us (20%)
  Pallas kernels  14.6 us (10%)
  local copies, waits for them, and re-layouts  4.91 us (3%)
    all_to_all x1, blocking collectives, exchange(): return lax.all_to_all(v, axes, split_axis=0, concat_axis=0, tiled=True)  34.8 us
    all_to_all x3, starting transfers between devices, exchange(): return lax.all_to_all(v, axes, split_axis=0, concat_axis=0, tiled=True)  20.4 us
    all_to_all x3, waiting for transfers between devices, exchange(): return lax.all_to_all(v, axes, split_axis=0, concat_axis=0, tiled=True)  12.8 us
    ppermute x3, starting transfers between devices, body(): lax.ppermute(parts[s], 'x', ring[s])  9.43 us
    pallas_call x1, Pallas kernels, ladder(): pl.pallas_call(ladder_kernel, in_specs=[VMEM] * 8, out_specs=VMEM, out_sh...  7.17 us
    ppermute x1, starting transfers between devices, body(): near = lax.ppermute(b1, 'x', ring[1])  5.59 us
    ppermute x1, starting transfers between devices, body(): ladder_resid = lax.ppermute(part, ('zl', 'x', 'zh'), move)  5.34 us
    ppermute x1, starting transfers between devices, body(): b1 = lax.ppermute(lower, 'x', ring[1])  4.75 us
  transfers between devices with their start and end apart: 14, of which 8 were waited for; matrix products, arithmetic and copies ran while one was open for 1% of the time, Pallas kernels for 10%

profile of v6, /device:TPU:6, one launch (start us, length us, event | category | flops | bytes accessed | tf_op | source)
XLA Modules:
  0.0 141.7 jit_solution(16676802826413328486)
XLA Ops:
  0.6 0.0 copy-start.2
  0.6 0.9 copy-done.2
  1.5 0.8 shard_map.78
  2.4 12.4 %all-to-all-start = ((f32[64,2,8,128]{3,2,1,0:T(8,128)}), f32[64,2,8,128]{3,2,1,0:T(8,128)S(1)}, u32[]{:S(2)}, u32[]{:S(2)}) async-start(f32[64,2,8,128]{3,2,1,0:T(8,128)} %shard_map.78), calls=%async_computation | async-start | bytes 1048576 | tf_op jit(solution)/shard_map/all_to_all | solution.py:176
  14.8 0.0 copy-start
  14.8 1.6 %copy-done = f32[4,4,64,512]{3,2,1,0:T(8,128)S(1)} copy-done((f32[4,4,64,512]{3,2,1,0:T(8,128)S(1)}, f32[4,4,64,512]{3,2,1,0:T(8,128)}, u32[]{:S(2)}) %copy-start) | copy-done | bytes 2097176
  16.4 4.6 %shard_map.77 = f32[16,2,8,2048]{3,2,1,0:T(8,128)} custom-call(f32[4,2,2,64,512]{4,3,2,1,0:T(8,128)S(1)} %bitcast.12), custom_call_target="tpu_custom_call" | custom-call | flops 1048576 | bytes 4194304 | tf_op jit(solution)/shard_map/pallas_call | solution.py:51
  21.0 0.0 copy-start.5
  21.0 11.0 %all-to-all-done.own_ref = f32[64,2,8,128]{3,2,1,0:T(8,128)S(1)} async-done(((f32[64,2,8,128]{3,2,1,0:T(8,128)}), f32[64,2,8,128]{3,2,1,0:T(8,128)S(1)}, u32[]{:S(2)}, u32[]{:S(2)}) %all-to-all-start) | async-done | bytes 524320 | tf_op jit(solution)/shard_map/all_to_all | solution.py:176
  32.0 4.5 %all-to-all-start.1 = ((f32[16,2,8,2048]{3,2,1,0:T(8,128)}), f32[16,2,8,2048]{3,2,1,0:T(8,128)}, u32[]{:S(2)}, u32[]{:S(2)}) async-start(f32[16,2,8,2048]{3,2,1,0:T(8,128)} %shard_map.77), calls=%async_computation.1 | async-start | bytes 4194304 | tf_op jit(solution)/shard_map/all_to_all | solution.py:176
  36.5 0.0 copy-done.5
  36.5 0.0 copy-start.8
  36.5 0.0 copy-start.1
  36.5 0.0 copy-start.3
  36.5 0.0 copy-start.4
  36.5 0.1 fusion
  36.6 2.4 %collective-permute-start.3 = (f32[32,8,640]{2,1,0:T(8,128)S(1)}, f32[32,8,640]{2,1,0:T(8,128)S(1)}, u32[]{:S(2)}, u32[]{:S(2)}) collective-permute-start(f32[32,8,640]{2,1,0:T(8,128)S(1)} %get-tuple-element.12), channel_id=1, source_target_pairs={{0,24},{8,0},{16,8},{24,16},{1,25},{9,1},{17,9},{25,17},{2,26},{10... | collective-permute-start | bytes 1966088 | tf_op jit(solution)/shard_map/ppermute | solution.py:190
  39.1 4.8 %collective-permute-start = (f32[32,8,640]{2,1,0:T(8,128)S(1)}, f32[32,8,640]{2,1,0:T(8,128)S(1)}, u32[]{:S(2)}, u32[]{:S(2)}) collective-permute-start(f32[32,8,640]{2,1,0:T(8,128)S(1)} %get-tuple-element.13), channel_id=1, source_target_pairs={{0,8},{8,16},{16,24},{24,0},{1,9},{9,17},{17,25},{25,1},{2,10},{10... | collective-permute-start | bytes 1966088 | tf_op jit(solution)/shard_map/ppermute | solution.py:189
  43.8 1.9 %collective-permute-start.6 = (f32[64,2,8,128]{3,2,1,0:T(8,128)S(1)}, f32[64,2,8,128]{3,2,1,0:T(8,128)S(1)}, u32[]{:S(2)}, u32[]{:S(2)}) collective-permute-start(f32[64,2,8,128]{3,2,1,0:T(8,128)S(1)} %all-to-all-done.own_ref), channel_id=1, source_target_pairs={{0,1},{1,0},{2,3},{3,2},{4,5},{5,4},{6,7},{7,6},{8,9},{9,8},{10,11... | collective-permute-start | bytes 1572872 | tf_op jit(solution)/shard_map/ppermute | solution.py:187
  45.8 2.0 %collective-permute-start.1 = (f32[32,8,640]{2,1,0:T(8,128)S(1)}, f32[32,8,640]{2,1,0:T(8,128)S(1)}, u32[]{:S(2)}, u32[]{:S(2)}) collective-permute-start(f32[32,8,640]{2,1,0:T(8,128)S(1)} %get-tuple-element.12), channel_id=1, source_target_pairs={{0,8},{8,16},{16,24},{24,0},{1,9},{9,17},{17,25},{25,1},{2,10},{10... | collective-permute-start | bytes 1966088 | tf_op jit(solution)/shard_map/ppermute | solution.py:191
  47.8 3.8 %collective-permute-start.2 = (f32[32,8,640]{2,1,0:T(8,128)S(1)}, f32[32,8,640]{2,1,0:T(8,128)S(1)}, u32[]{:S(2)}, u32[]{:S(2)}) collective-permute-start(f32[32,8,640]{2,1,0:T(8,128)S(1)} %get-tuple-element.13), channel_id=1, source_target_pairs={{0,24},{8,0},{16,8},{24,16},{1,25},{9,1},{17,9},{25,17},{2,26},{10... | collective-permute-start | bytes 1966088 | tf_op jit(solution)/shard_map/ppermute | solution.py:192
  51.6 2.2 %collective-permute-done.3.b3_far = f32[32,8,640]{2,1,0:T(8,128)S(1)} collective-permute-done((f32[32,8,640]{2,1,0:T(8,128)S(1)}, f32[32,8,640]{2,1,0:T(8,128)S(1)}, u32[]{:S(2)}, u32[]{:S(2)}) %collective-permute-start.3) | collective-permute-done | bytes 655392 | tf_op jit(solution)/shard_map/ppermute | solution.py:190
  53.8 0.0 copy-start.6
  53.8 1.9 %collective-permute-start.5 = (f32[32,8,640]{2,1,0:T(8,128)S(1)}, f32[32,8,640]{2,1,0:T(8,128)S(1)}, u32[]{:S(2)}, u32[]{:S(2)}) collective-permute-start(f32[32,8,640]{2,1,0:T(8,128)S(1)} %collective-permute-done.3.b3_far), channel_id=1, source_target_pairs={{0,24},{8,0},{16,8},{24,16},{1,25},{9,1},{17,9},{25,17},{2,26},{10... | collective-permute-start | bytes 1966088 | tf_op jit(solution)/shard_map/ppermute | solution.py:194
  55.7 3.2 %collective-permute-done.b1 = f32[32,8,640]{2,1,0:T(8,128)S(1)} collective-permute-done((f32[32,8,640]{2,1,0:T(8,128)S(1)}, f32[32,8,640]{2,1,0:T(8,128)S(1)}, u32[]{:S(2)}, u32[]{:S(2)}) %collective-permute-start) | collective-permute-done | bytes 655392 | tf_op jit(solution)/shard_map/ppermute | solution.py:189
  59.0 5.6 %collective-permute-start.4 = (f32[32,8,640]{2,1,0:T(8,128)S(1)}, f32[32,8,640]{2,1,0:T(8,128)}, u32[]{:S(2)}, u32[]{:S(2)}) collective-permute-start(f32[32,8,640]{2,1,0:T(8,128)S(1)} %collective-permute-done.b1), channel_id=1, source_target_pairs={{0,8},{8,16},{16,24},{24,0},{1,9},{9,17},{17,25},{25,1},{2,10},{10... | collective-permute-start | bytes 1966088 | tf_op jit(solution)/shard_map/ppermute | solution.py:193
  64.6 0.0 collective-permute-done.6.other_ref
  64.6 0.0 copy-done.8
  64.6 0.1 broadcast_in_dim.4.vir_ref
  64.7 0.0 copy-done.1
  64.8 0.0 copy-done.3
  64.8 0.0 copy-done.4
  64.8 1.8 %shard_map.80 = f32[4,32,256]{2,1,0:T(8,128)S(1)} custom-call(s32[32]{0:T(128)S(1)} %copy-done.3, f32[4,4,64,512]{3,2,1,0:T(8,128)S(1)} %copy-done.1, f32[64,2,8,128]{3,2,1,0:T(8,128)S(1)} %all-to-all-done.own_ref, f32[64,2,8,128]{3,2,1,0:T(8,128)S(1)} %collective-permute-done.6.other_ref, s32[512,128]{1,0:T(8,128)S(1)} %broadcast_in_dim.4.vir_ref, ...), custom_call_target="tpu_custom_call" | custom-call | flops 402653184 | bytes 3145728 | tf_op jit(solution)/shard_map/pallas_call | solution.py:162
  66.6 1.9 %collective-permute-start.9 = (f32[32,256]{1,0:T(8,128)S(1)}, f32[32,256]{1,0:T(8,128)S(1)}, u32[]{:S(2)}, u32[]{:S(2)}) collective-permute-start(f32[32,256]{1,0:T(8,128)S(1)} %get-tuple-element.14), channel_id=1, source_target_pairs={{0,24},{8,0},{16,8},{24,16},{1,25},{9,1},{17,9},{25,17},{2,26},{10... | collective-permute-start | bytes 98312 | tf_op jit(solution)/shard_map/ppermute | solution.py:198
  68.5 4.5 %collective-permute-done.1.b1_far = f32[32,8,640]{2,1,0:T(8,128)S(1)} collective-permute-done((f32[32,8,640]{2,1,0:T(8,128)S(1)}, f32[32,8,640]{2,1,0:T(8,128)S(1)}, u32[]{:S(2)}, u32[]{:S(2)}) %collective-permute-start.1) | collective-permute-done | bytes 655392 | tf_op jit(solution)/shard_map/ppermute | solution.py:191
  73.0 3.9 %collective-permute-start.8 = (f32[32,256]{1,0:T(8,128)S(1)}, f32[32,256]{1,0:T(8,128)S(1)}, u32[]{:S(2)}, u32[]{:S(2)}) collective-permute-start(f32[32,256]{1,0:T(8,128)S(1)} %get-tuple-element.15), channel_id=1, source_target_pairs={{0,16},{8,24},{16,0},{24,8},{1,17},{9,25},{17,1},{25,9},{2,18},{10... | collective-permute-start | bytes 98312 | tf_op jit(solution)/shard_map/ppermute | solution.py:198
  77.0 0.0 collective-permute-done.2.b3
  77.0 3.6 %collective-permute-start.7 = (f32[32,256]{1,0:T(8,128)S(1)}, f32[32,256]{1,0:T(8,128)S(1)}, u32[]{:S(2)}, u32[]{:S(2)}) collective-permute-start(f32[32,256]{1,0:T(8,128)S(1)} %get-tuple-element.16), channel_id=1, source_target_pairs={{0,8},{8,16},{16,24},{24,0},{1,9},{9,17},{17,25},{25,1},{2,10},{10... | collective-permute-start | bytes 98312 | tf_op jit(solution)/shard_map/ppermute | solution.py:198
  80.6 2.1 %collective-permute-done.5.far = f32[32,8,640]{2,1,0:T(8,128)S(1)} collective-permute-done((f32[32,8,640]{2,1,0:T(8,128)S(1)}, f32[32,8,640]{2,1,0:T(8,128)S(1)}, u32[]{:S(2)}, u32[]{:S(2)}) %collective-permute-start.5) | collective-permute-done | bytes 655392 | tf_op jit(solution)/shard_map/ppermute | solution.py:194
  82.7 0.0 copy-start.7
  82.7 0.9 copy-done.7
  83.5 0.6 collective-permute-done.4.near
  84.2 0.0 all-to-all-done.1.x_ref
  84.2 0.0 copy-done.6
  84.2 7.2 %shard_map.79 = f32[2,128,640]{2,1,0:T(8,128)} custom-call(f32[16,2,8,2048]{3,2,1,0:T(8,128)} %all-to-all-done.1.x_ref, f32[32,8,640]{2,1,0:T(8,128)S(1)} %collective-permute-done.b1, f32[32,8,640]{2,1,0:T(8,128)S(1)} %collective-permute-done.1.b1_far, f32[32,8,640]{2,1,0:T(8,128)S(1)} %collective-permute-done.2.b3, f32[32,8,640]{2,1,0:T(8,128)} %copy-done.6, ...), custom_call_target="tpu_custom_call" | custom-call | flops 2013265920 | bytes 8388608 | tf_op jit(solution)/shard_map/pallas_call | solution.py:100
  91.4 3.5 %all-to-all-start.2 = ((f32[2,128,640]{2,1,0:T(8,128)}), f32[2,128,640]{2,1,0:T(8,128)S(1)}, u32[]{:S(2)}, u32[]{:S(2)}) async-start(f32[2,128,640]{2,1,0:T(8,128)} %shard_map.79), calls=%async_computation.2 | async-start | bytes 1310720 | tf_op jit(solution)/shard_map/all_to_all | solution.py:176
  94.9 0.0 collective-permute-done.9.c3
  94.9 0.0 collective-permute-done.8.c2
  94.9 0.0 collective-permute-done.7.c1
  94.9 1.8 %all-to-all-done.2.part_ref = f32[2,128,640]{2,1,0:T(8,128)S(1)} async-done(((f32[2,128,640]{2,1,0:T(8,128)}), f32[2,128,640]{2,1,0:T(8,128)S(1)}, u32[]{:S(2)}, u32[]{:S(2)}) %all-to-all-start.2) | async-done | bytes 655392 | tf_op jit(solution)/shard_map/all_to_all | solution.py:176
  96.7 0.2 shard_map.81
  96.9 34.8 %all_to_all.20.p_ref = f32[64,2,896]{2,1,0:T(2,128)S(1)} all-to-all(f32[64,2,896]{2,1,0:T(2,128)S(1)} %shard_map.81), channel_id=1, replica_groups=mesh['y'=8,'zl'=2,'x'=4,'zh'=4,'core'=2] {'y','zl','zh'}, dimensions={0} | all-to-all | bytes 917504 | tf_op jit(solution)/shard_map/all_to_all | solution.py:176
  131.6 5.3 %collective-permute-start.10 = (f32[2,640]{1,0:T(2,128)S(1)}, f32[2,640]{1,0:T(2,128)S(1)}, u32[]{:S(2)}, u32[]{:S(2)}) collective-permute-start(f32[2,640]{1,0:T(2,128)S(1)} %get-tuple-element.10), channel_id=1, source_target_pairs={{0,0},{2,16},{4,32},{6,48},{8,2},{10,18},{12,34},{14,50},{16,4},{1... | collective-permute-start | bytes 15368 | tf_op jit(solution)/shard_map/ppermute | solution.py:213
  137.0 0.1 reshape.15
  137.1 0.6 copy.8
  137.7 3.3 %collective-permute-done.10 = f32[2,640]{1,0:T(2,128)S(1)} collective-permute-done((f32[2,640]{1,0:T(2,128)S(1)}, f32[2,640]{1,0:T(2,128)S(1)}, u32[]{:S(2)}, u32[]{:S(2)}) %collective-permute-start.10) | collective-permute-done | bytes 5152 | tf_op jit(solution)/shard_map/ppermute | solution.py:213
  141.1 0.6 copy.10
  (2 shorter events, 0.0 us)
Async XLA Ops:
  0.6 0.9 copy-start.2
  2.4 29.6 %all-to-all-start = ((f32[64,2,8,128]{3,2,1,0:T(8,128)}), f32[64,2,8,128]{3,2,1,0:T(8,128)S(1)}, u32[]{:S(2)}, u32[]{:S(2)}) async-start(f32[64,2,8,128]{3,2,1,0:T(8,128)} %shard_map.78), calls=%async_computation | async-start | bytes 1048576 | tf_op jit(solution)/shard_map/all_to_all | solution.py:176
  14.8 1.6 %copy-start = (f32[4,4,64,512]{3,2,1,0:T(8,128)S(1)}, f32[4,4,64,512]{3,2,1,0:T(8,128)}, u32[]{:S(2)}) copy-start(f32[4,4,64,512]{3,2,1,0:T(8,128)} %a_ref.1) | copy-start | bytes 6291460
  21.0 15.5 %copy-start.5 = (f32[64,8,640]{2,1,0:T(8,128)S(1)}, f32[64,8,640]{2,1,0:T(8,128)}, u32[]{:S(2)}) copy-start(f32[64,8,640]{2,1,0:T(8,128)} %b0) | copy-start | bytes 3932164
  32.0 52.2 %all-to-all-start.1 = ((f32[16,2,8,2048]{3,2,1,0:T(8,128)}), f32[16,2,8,2048]{3,2,1,0:T(8,128)}, u32[]{:S(2)}, u32[]{:S(2)}) async-start(f32[16,2,8,2048]{3,2,1,0:T(8,128)} %shard_map.77), calls=%async_computation.1 | async-start | bytes 4194304 | tf_op jit(solution)/shard_map/all_to_all | solution.py:176
  36.5 28.1 %copy-start.8 = (s32[512]{0:T(512)S(1)}, s32[512]{0:T(512)}, u32[]{:S(2)}) copy-start(s32[512]{0:T(512)} %param.10) | copy-start | bytes 6148
  36.5 28.3 %copy-start.1 = (f32[4,4,64,512]{3,2,1,0:T(8,128)S(1)}, f32[4,4,64,512]{3,2,1,0:T(8,128)}, u32[]{:S(2)}) copy-start(f32[4,4,64,512]{3,2,1,0:T(8,128)} %a_ref.1) | copy-start | bytes 6291460
  36.5 28.2 %copy-start.3 = (s32[32]{0:T(128)S(1)}, s32[32]{0:T(128)}, u32[]{:S(2)}) copy-start(s32[32]{0:T(128)} %occ_ref.1) | copy-start | bytes 388
  36.5 28.2 %copy-start.4 = (s32[128]{0:T(128)S(1)}, s32[128]{0:T(128)}, u32[]{:S(2)}) copy-start(s32[128]{0:T(128)} %param.11) | copy-start | bytes 1540
  36.6 17.2 %collective-permute-start.3 = (f32[32,8,640]{2,1,0:T(8,128)S(1)}, f32[32,8,640]{2,1,0:T(8,128)S(1)}, u32[]{:S(2)}, u32[]{:S(2)}) collective-permute-start(f32[32,8,640]{2,1,0:T(8,128)S(1)} %get-tuple-element.12), channel_id=1, source_target_pairs={{0,24},{8,0},{16,8},{24,16},{1,25},{9,1},{17,9},{25,17},{2,26},{10... | collective-permute-start | bytes 1966088 | tf_op jit(solution)/shard_map/ppermute | solution.py:190
  39.1 19.9 %collective-permute-start = (f32[32,8,640]{2,1,0:T(8,128)S(1)}, f32[32,8,640]{2,1,0:T(8,128)S(1)}, u32[]{:S(2)}, u32[]{:S(2)}) collective-permute-start(f32[32,8,640]{2,1,0:T(8,128)S(1)} %get-tuple-element.13), channel_id=1, source_target_pairs={{0,8},{8,16},{16,24},{24,0},{1,9},{9,17},{17,25},{25,1},{2,10},{10... | collective-permute-start | bytes 1966088 | tf_op jit(solution)/shard_map/ppermute | solution.py:189
  43.8 20.8 %collective-permute-start.6 = (f32[64,2,8,128]{3,2,1,0:T(8,128)S(1)}, f32[64,2,8,128]{3,2,1,0:T(8,128)S(1)}, u32[]{:S(2)}, u32[]{:S(2)}) collective-permute-start(f32[64,2,8,128]{3,2,1,0:T(8,128)S(1)} %all-to-all-done.own_ref), channel_id=1, source_target_pairs={{0,1},{1,0},{2,3},{3,2},{4,5},{5,4},{6,7},{7,6},{8,9},{9,8},{10,11... | collective-permute-start | bytes 1572872 | tf_op jit(solution)/shard_map/ppermute | solution.py:187
  45.8 27.3 %collective-permute-start.1 = (f32[32,8,640]{2,1,0:T(8,128)S(1)}, f32[32,8,640]{2,1,0:T(8,128)S(1)}, u32[]{:S(2)}, u32[]{:S(2)}) collective-permute-start(f32[32,8,640]{2,1,0:T(8,128)S(1)} %get-tuple-element.12), channel_id=1, source_target_pairs={{0,8},{8,16},{16,24},{24,0},{1,9},{9,17},{17,25},{25,1},{2,10},{10... | collective-permute-start | bytes 1966088 | tf_op jit(solution)/shard_map/ppermute | solution.py:191
  47.8 29.2 %collective-permute-start.2 = (f32[32,8,640]{2,1,0:T(8,128)S(1)}, f32[32,8,640]{2,1,0:T(8,128)S(1)}, u32[]{:S(2)}, u32[]{:S(2)}) collective-permute-start(f32[32,8,640]{2,1,0:T(8,128)S(1)} %get-tuple-element.13), channel_id=1, source_target_pairs={{0,24},{8,0},{16,8},{24,16},{1,25},{9,1},{17,9},{25,17},{2,26},{10... | collective-permute-start | bytes 1966088 | tf_op jit(solution)/shard_map/ppermute | solution.py:192
  53.8 30.4 %copy-start.6 = (f32[32,8,640]{2,1,0:T(8,128)}, f32[32,8,640]{2,1,0:T(8,128)S(1)}, u32[]{:S(2)}) copy-start(f32[32,8,640]{2,1,0:T(8,128)S(1)} %collective-permute-done.3.b3_far) | copy-start | bytes 1966084
  53.8 28.9 %collective-permute-start.5 = (f32[32,8,640]{2,1,0:T(8,128)S(1)}, f32[32,8,640]{2,1,0:T(8,128)S(1)}, u32[]{:S(2)}, u32[]{:S(2)}) collective-permute-start(f32[32,8,640]{2,1,0:T(8,128)S(1)} %collective-permute-done.3.b3_far), channel_id=1, source_target_pairs={{0,24},{8,0},{16,8},{24,16},{1,25},{9,1},{17,9},{25,17},{2,26},{10... | collective-permute-start | bytes 1966088 | tf_op jit(solution)/shard_map/ppermute | solution.py:194
  59.0 25.2 %collective-permute-start.4 = (f32[32,8,640]{2,1,0:T(8,128)S(1)}, f32[32,8,640]{2,1,0:T(8,128)}, u32[]{:S(2)}, u32[]{:S(2)}) collective-permute-start(f32[32,8,640]{2,1,0:T(8,128)S(1)} %collective-permute-done.b1), channel_id=1, source_target_pairs={{0,8},{8,16},{16,24},{24,0},{1,9},{9,17},{17,25},{25,1},{2,10},{10... | collective-permute-start | bytes 1966088 | tf_op jit(solution)/shard_map/ppermute | solution.py:193
  66.6 28.3 %collective-permute-start.9 = (f32[32,256]{1,0:T(8,128)S(1)}, f32[32,256]{1,0:T(8,128)S(1)}, u32[]{:S(2)}, u32[]{:S(2)}) collective-permute-start(f32[32,256]{1,0:T(8,128)S(1)} %get-tuple-element.14), channel_id=1, source_target_pairs={{0,24},{8,0},{16,8},{24,16},{1,25},{9,1},{17,9},{25,17},{2,26},{10... | collective-permute-start | bytes 98312 | tf_op jit(solution)/shard_map/ppermute | solution.py:198
  73.0 21.9 %collective-permute-start.8 = (f32[32,256]{1,0:T(8,128)S(1)}, f32[32,256]{1,0:T(8,128)S(1)}, u32[]{:S(2)}, u32[]{:S(2)}) collective-permute-start(f32[32,256]{1,0:T(8,128)S(1)} %get-tuple-element.15), channel_id=1, source_target_pairs={{0,16},{8,24},{16,0},{24,8},{1,17},{9,25},{17,1},{25,9},{2,18},{10... | collective-permute-start | bytes 98312 | tf_op jit(solution)/shard_map/ppermute | solution.py:198
  77.0 17.9 %collective-permute-start.7 = (f32[32,256]{1,0:T(8,128)S(1)}, f32[32,256]{1,0:T(8,128)S(1)}, u32[]{:S(2)}, u32[]{:S(2)}) collective-permute-start(f32[32,256]{1,0:T(8,128)S(1)} %get-tuple-element.16), channel_id=1, source_target_pairs={{0,8},{8,16},{16,24},{24,0},{1,9},{9,17},{17,25},{25,1},{2,10},{10... | collective-permute-start | bytes 98312 | tf_op jit(solution)/shard_map/ppermute | solution.py:198
  82.7 0.9 copy-start.7
  91.4 5.3 %all-to-all-start.2 = ((f32[2,128,640]{2,1,0:T(8,128)}), f32[2,128,640]{2,1,0:T(8,128)S(1)}, u32[]{:S(2)}, u32[]{:S(2)}) async-start(f32[2,128,640]{2,1,0:T(8,128)} %shard_map.79), calls=%async_computation.2 | async-start | bytes 1310720 | tf_op jit(solution)/shard_map/all_to_all | solution.py:176
  131.6 9.4 %collective-permute-start.10 = (f32[2,640]{1,0:T(2,128)S(1)}, f32[2,640]{1,0:T(2,128)S(1)}, u32[]{:S(2)}, u32[]{:S(2)}) collective-permute-start(f32[2,640]{1,0:T(2,128)S(1)} %get-tuple-element.10), channel_id=1, source_target_pairs={{0,0},{2,16},{4,32},{6,48},{8,2},{10,18},{12,34},{14,50},{16,4},{1... | collective-permute-start | bytes 15368 | tf_op jit(solution)/shard_map/ppermute | solution.py:213

commit v7 on v5

--- a/solution.py
+++ b/solution.py
@@ -9,6 +9,7 @@
 BF16 = jnp.bfloat16
 VMEM_LIMIT = 16 * 1024 * 1024
 LADDER_LIMIT = 51 * 1024 * 1024
+SPREAD_LIMIT = 60 * 1024 * 1024
 
 
 def split(v):
@@ -59,24 +60,28 @@
     )(a)
 
 
-def ladder_kernel(x_ref, b1, b1_far, b3, b3_far, b0, near, far, o_ref, held, sems):
+def ladder_kernel(x_ref, b1, b1_far, b3, near, b0, b3_far, far, o_ref, held, sems):
     me = lax.axis_index("x")
 
     def copies(k):
-        part = pl.ds(k * 16, 16)
-        across = (near if k < 2 else far).at[pl.ds(k % 2 * 16, 16)]
-        return (
-            pltpu.make_async_copy(b0.at[part], held.at[me, part], sems.at[0, k]),
-            pltpu.make_async_copy(across, held.at[lax.rem(me + 2, 4), part], sems.at[1, k]),
-        )
+        part, half = pl.ds(k * 16, 16), pl.ds(k % 2 * 16, 16)
+        found = [(0, b0.at[part])]
+        if k >= 2:
+            found += [(1, b3_far.at[half]), (2, far.at[half])]
+        return [
+            pltpu.make_async_copy(b, held.at[lax.rem(me + s, 4), part], sems.at[s, k])
+            for s, b in found
+        ]
 
     for k in range(4):
         for copy in copies(k):
             copy.start()
     for k in range(4):
         part, half = pl.ds(k * 16, 16), pl.ds(k % 2 * 16, 16)
-        held[lax.rem(me + 1, 4), part] = (b3 if k < 2 else b3_far)[half]
         held[lax.rem(me + 3, 4), part] = (b1 if k < 2 else b1_far)[half]
+        if k < 2:
+            held[lax.rem(me + 1, 4), part] = b3[half]
+            held[lax.rem(me + 2, 4), part] = near[half]
         span = pl.ds(k * 512, 512)
         x = jnp.concatenate([x_ref[:, h, :, span].reshape(128, 512) for h in range(2)], axis=0)
         xh, xl = split(x)
@@ -115,7 +120,7 @@
         in_specs=[VMEM] * 5 + [anywhere] * 3,
         out_specs=VMEM,
         out_shape=jax.ShapeDtypeStruct((2, 128, 640), F32),
-        scratch_shapes=[pltpu.VMEM((4, 64, 8, 640), F32), pltpu.SemaphoreType.DMA((2, 4))],
+        scratch_shapes=[pltpu.VMEM((4, 64, 8, 640), F32), pltpu.SemaphoreType.DMA((3, 4))],
         compiler_params=pltpu.CompilerParams(vmem_limit_bytes=LADDER_LIMIT),
         cost_estimate=pl.CostEstimate(
             flops=3 * 2 * 256 * 2048 * 640, bytes_accessed=8 * 2**20, transcendentals=0
@@ -123,11 +128,24 @@
     )(x, *blocks)
 
 
-def spread_kernel(w_ref, o_ref):
-    core = lax.axis_index("core")
-    for col in range(8):
-        for y in range(8):
-            o_ref[y * 8 + col] = w_ref[pl.ds(col * 4 + 2 * core, 2)]
+def spread_kernel(w_hbm, o_ref, held, sem):
+    copy = pltpu.make_async_copy(w_hbm.at[:, pl.ds(2 * lax.axis_index("core"), 2)], held, sem)
+    copy.start()
+    copy.wait()
+    for y in range(8):
+        o_ref[pl.ds(y * 8, 8)] = held[...]
+
+
+def spread(w):
+    return pl.pallas_call(
+        spread_kernel,
+        in_specs=[pl.BlockSpec(memory_space=pl.ANY)],
+        out_specs=VMEM,
+        out_shape=jax.ShapeDtypeStruct((64, 2, 8, 128), F32),
+        scratch_shapes=[pltpu.VMEM((8, 2, 8, 128), F32), pltpu.SemaphoreType.DMA],
+        compiler_params=pltpu.CompilerParams(vmem_limit_bytes=SPREAD_LIMIT),
+        cost_estimate=pl.CostEstimate(flops=0, bytes_accessed=2**20, transcendentals=0),
+    )(w.reshape(8, 4, 8, 128))
 
 
 def pack_kernel(part_ref, c0, c1, c2, c3, o_ref, ladder_sum, cycle_sum):
@@ -190,7 +208,7 @@
 
 
 def body(amplitudes, ladder_ints, cycle_ints, occ_irrep, vir_irrep, pair_irrep):
-    own = exchange(small(spread_kernel, (64, 2, 8, 128), cycle_ints), ("y", "zl", "x"))
+    own = exchange(spread(cycle_ints), ("y", "zl", "x"))
 
     ring = [[(i, (i + s) % 4) for i in range(4)] for s in range(4)]
     sent = regroup(amplitudes)
@@ -210,7 +228,7 @@
     parts = cycle(occ_irrep, amplitudes, own, other, vir, pair_irrep[None])
     parts = [parts[0]] + [lax.ppermute(parts[s], "x", ring[s]) for s in (1, 2, 3)]
 
-    part = ladder(x, b1, b1_far, b3, b3_far, ladder_ints, near, far)
+    part = ladder(x, b1, b1_far, b3, near, ladder_ints, b3_far, far)
     part = exchange(part, ("core",))
     both = small(pack_kernel, (64, 2, 896), part, *parts, scratch=[(128, 640), (32, 256)])
     both = exchange(both, ("y", "zl", "zh"))

time: 143 us -> 143 us (level)
    pallas_call x0 -> x1, Pallas kernels: none -> 1.7 us  [spread(): pl.pallas_call(spread_kernel, in_specs=[pl.BlockSpec(memory_space=pl.ANY)...]
    unnamed x19 -> x17, local copies, waits for them, and re-layouts: 3.96 us -> 3.07 us
where the time goes in v7:
time: 143 us; the launch traced here: 142 us
  starting transfers between devices  57.6 us (40%)
  blocking collectives  34.8 us (24%)
  waiting for transfers between devices  29 us (20%)
  Pallas kernels  15.5 us (11%)
  local copies, waits for them, and re-layouts  4.01 us (3%)
    all_to_all x1, blocking collectives, exchange(): return lax.all_to_all(v, axes, split_axis=0, concat_axis=0, tiled=True)  34.8 us
    all_to_all x3, starting transfers between devices, exchange(): return lax.all_to_all(v, axes, split_axis=0, concat_axis=0, tiled=True)  20.4 us
    all_to_all x3, waiting for transfers between devices, exchange(): return lax.all_to_all(v, axes, split_axis=0, concat_axis=0, tiled=True)  12.9 us
    ppermute x3, starting transfers between devices, body(): lax.ppermute(parts[s], 'x', ring[s])  9.43 us
    pallas_call x1, Pallas kernels, ladder(): pl.pallas_call(ladder_kernel, in_specs=[VMEM] * 5 + [anywhere] * 3, out_s...  7.25 us
    ppermute x1, starting transfers between devices, body(): near = lax.ppermute(b1, 'x', ring[1])  5.59 us
    ppermute x1, starting transfers between devices, body(): ladder_resid = lax.ppermute(part, ('zl', 'x', 'zh'), move)  5.32 us
    ppermute x1, starting transfers between devices, body(): b1 = lax.ppermute(lower, 'x', ring[1])  4.75 us
  transfers between devices with their start and end apart: 14, of which 8 were waited for; matrix products, arithmetic and copies ran while one was open for 1% of the time, Pallas kernels for 10%

profile of v7, /device:TPU:6, one launch (start us, length us, event | category | flops | bytes accessed | tf_op | source)
XLA Modules:
  0.0 141.7 jit_solution(10052348109005166708)
XLA Ops:
  0.6 1.7 %shard_map.78 = f32[64,2,8,128]{3,2,1,0:T(8,128)} custom-call(f32[8,4,8,128]{3,2,1,0:T(8,128)} %bitcast.15), custom_call_target="tpu_custom_call" | custom-call | bytes 1048576 | tf_op jit(solution)/shard_map/pallas_call | solution.py:140
  2.3 12.4 %all-to-all-start = ((f32[64,2,8,128]{3,2,1,0:T(8,128)}), f32[64,2,8,128]{3,2,1,0:T(8,128)S(1)}, u32[]{:S(2)}, u32[]{:S(2)}) async-start(f32[64,2,8,128]{3,2,1,0:T(8,128)} %shard_map.78), calls=%async_computation | async-start | bytes 1048576 | tf_op jit(solution)/shard_map/all_to_all | solution.py:207
  14.8 0.0 copy-start
  14.8 1.6 %copy-done = f32[4,4,64,512]{3,2,1,0:T(8,128)S(1)} copy-done((f32[4,4,64,512]{3,2,1,0:T(8,128)S(1)}, f32[4,4,64,512]{3,2,1,0:T(8,128)}, u32[]{:S(2)}) %copy-start) | copy-done | bytes 2097176
  16.4 4.5 %shard_map.77 = f32[16,2,8,2048]{3,2,1,0:T(8,128)} custom-call(f32[4,2,2,64,512]{4,3,2,1,0:T(8,128)S(1)} %bitcast.13), custom_call_target="tpu_custom_call" | custom-call | flops 1048576 | bytes 4194304 | tf_op jit(solution)/shard_map/pallas_call | solution.py:52
  20.9 0.0 copy-start.4
  20.9 11.1 %all-to-all-done.own_ref = f32[64,2,8,128]{3,2,1,0:T(8,128)S(1)} async-done(((f32[64,2,8,128]{3,2,1,0:T(8,128)}), f32[64,2,8,128]{3,2,1,0:T(8,128)S(1)}, u32[]{:S(2)}, u32[]{:S(2)}) %all-to-all-start) | async-done | bytes 524320 | tf_op jit(solution)/shard_map/all_to_all | solution.py:207
  32.0 4.4 %all-to-all-start.1 = ((f32[16,2,8,2048]{3,2,1,0:T(8,128)}), f32[16,2,8,2048]{3,2,1,0:T(8,128)}, u32[]{:S(2)}, u32[]{:S(2)}) async-start(f32[16,2,8,2048]{3,2,1,0:T(8,128)} %shard_map.77), calls=%async_computation.1 | async-start | bytes 4194304 | tf_op jit(solution)/shard_map/all_to_all | solution.py:207
  36.4 0.0 copy-done.4
  36.4 0.0 copy-start.7
  36.4 0.0 copy-start.1
  36.5 0.0 copy-start.2
  36.5 0.0 copy-start.3
  36.5 0.1 fusion
  36.6 2.4 %collective-permute-start.4 = (f32[32,8,640]{2,1,0:T(8,128)S(1)}, f32[32,8,640]{2,1,0:T(8,128)S(1)}, u32[]{:S(2)}, u32[]{:S(2)}) collective-permute-start(f32[32,8,640]{2,1,0:T(8,128)S(1)} %get-tuple-element.12), channel_id=1, source_target_pairs={{0,24},{8,0},{16,8},{24,16},{1,25},{9,1},{17,9},{25,17},{2,26},{10... | collective-permute-start | bytes 1966088 | tf_op jit(solution)/shard_map/ppermute | solution.py:221
  39.0 4.8 %collective-permute-start = (f32[32,8,640]{2,1,0:T(8,128)S(1)}, f32[32,8,640]{2,1,0:T(8,128)S(1)}, u32[]{:S(2)}, u32[]{:S(2)}) collective-permute-start(f32[32,8,640]{2,1,0:T(8,128)S(1)} %get-tuple-element.13), channel_id=1, source_target_pairs={{0,8},{8,16},{16,24},{24,0},{1,9},{9,17},{17,25},{25,1},{2,10},{10... | collective-permute-start | bytes 1966088 | tf_op jit(solution)/shard_map/ppermute | solution.py:220
  43.8 1.9 %collective-permute-start.6 = (f32[64,2,8,128]{3,2,1,0:T(8,128)S(1)}, f32[64,2,8,128]{3,2,1,0:T(8,128)S(1)}, u32[]{:S(2)}, u32[]{:S(2)}) collective-permute-start(f32[64,2,8,128]{3,2,1,0:T(8,128)S(1)} %all-to-all-done.own_ref), channel_id=1, source_target_pairs={{0,1},{1,0},{2,3},{3,2},{4,5},{5,4},{6,7},{7,6},{8,9},{9,8},{10,11... | collective-permute-start | bytes 1572872 | tf_op jit(solution)/shard_map/ppermute | solution.py:218
  45.7 2.0 %collective-permute-start.1 = (f32[32,8,640]{2,1,0:T(8,128)S(1)}, f32[32,8,640]{2,1,0:T(8,128)S(1)}, u32[]{:S(2)}, u32[]{:S(2)}) collective-permute-start(f32[32,8,640]{2,1,0:T(8,128)S(1)} %get-tuple-element.12), channel_id=1, source_target_pairs={{0,8},{8,16},{16,24},{24,0},{1,9},{9,17},{17,25},{25,1},{2,10},{10... | collective-permute-start | bytes 1966088 | tf_op jit(solution)/shard_map/ppermute | solution.py:222
  47.7 3.8 %collective-permute-start.2 = (f32[32,8,640]{2,1,0:T(8,128)S(1)}, f32[32,8,640]{2,1,0:T(8,128)S(1)}, u32[]{:S(2)}, u32[]{:S(2)}) collective-permute-start(f32[32,8,640]{2,1,0:T(8,128)S(1)} %get-tuple-element.13), channel_id=1, source_target_pairs={{0,24},{8,0},{16,8},{24,16},{1,25},{9,1},{17,9},{25,17},{2,26},{10... | collective-permute-start | bytes 1966088 | tf_op jit(solution)/shard_map/ppermute | solution.py:223
  51.6 2.2 %collective-permute-done.4.b3_far = f32[32,8,640]{2,1,0:T(8,128)S(1)} collective-permute-done((f32[32,8,640]{2,1,0:T(8,128)S(1)}, f32[32,8,640]{2,1,0:T(8,128)S(1)}, u32[]{:S(2)}, u32[]{:S(2)}) %collective-permute-start.4) | collective-permute-done | bytes 655392 | tf_op jit(solution)/shard_map/ppermute | solution.py:221
  53.8 0.0 copy-start.5
  53.8 1.9 %collective-permute-start.5 = (f32[32,8,640]{2,1,0:T(8,128)S(1)}, f32[32,8,640]{2,1,0:T(8,128)S(1)}, u32[]{:S(2)}, u32[]{:S(2)}) collective-permute-start(f32[32,8,640]{2,1,0:T(8,128)S(1)} %collective-permute-done.4.b3_far), channel_id=1, source_target_pairs={{0,24},{8,0},{16,8},{24,16},{1,25},{9,1},{17,9},{25,17},{2,26},{10... | collective-permute-start | bytes 1966088 | tf_op jit(solution)/shard_map/ppermute | solution.py:225
  55.7 3.2 %collective-permute-done.b1 = f32[32,8,640]{2,1,0:T(8,128)S(1)} collective-permute-done((f32[32,8,640]{2,1,0:T(8,128)S(1)}, f32[32,8,640]{2,1,0:T(8,128)S(1)}, u32[]{:S(2)}, u32[]{:S(2)}) %collective-permute-start) | collective-permute-done | bytes 655392 | tf_op jit(solution)/shard_map/ppermute | solution.py:220
  58.9 5.6 %collective-permute-start.3 = (f32[32,8,640]{2,1,0:T(8,128)S(1)}, f32[32,8,640]{2,1,0:T(8,128)}, u32[]{:S(2)}, u32[]{:S(2)}) collective-permute-start(f32[32,8,640]{2,1,0:T(8,128)S(1)} %collective-permute-done.b1), channel_id=1, source_target_pairs={{0,8},{8,16},{16,24},{24,0},{1,9},{9,17},{17,25},{25,1},{2,10},{10... | collective-permute-start | bytes 1966088 | tf_op jit(solution)/shard_map/ppermute | solution.py:224
  64.5 0.0 collective-permute-done.6.other_ref
  64.6 0.0 copy-done.7
  64.6 0.1 broadcast_in_dim.4.vir_ref
  64.7 0.0 copy-done.1
  64.7 0.0 copy-done.2
  64.7 0.0 copy-done.3
  64.7 1.8 %shard_map.80 = f32[4,32,256]{2,1,0:T(8,128)S(1)} custom-call(s32[32]{0:T(128)S(1)} %copy-done.2, f32[4,4,64,512]{3,2,1,0:T(8,128)S(1)} %copy-done.1, f32[64,2,8,128]{3,2,1,0:T(8,128)S(1)} %all-to-all-done.own_ref, f32[64,2,8,128]{3,2,1,0:T(8,128)S(1)} %collective-permute-done.6.other_ref, s32[512,128]{1,0:T(8,128)S(1)} %broadcast_in_dim.4.vir_ref, ...), custom_call_target="tpu_custom_call" | custom-call | flops 402653184 | bytes 3145728 | tf_op jit(solution)/shard_map/pallas_call | solution.py:193
  66.5 1.9 %collective-permute-start.9 = (f32[32,256]{1,0:T(8,128)S(1)}, f32[32,256]{1,0:T(8,128)S(1)}, u32[]{:S(2)}, u32[]{:S(2)}) collective-permute-start(f32[32,256]{1,0:T(8,128)S(1)} %get-tuple-element.14), channel_id=1, source_target_pairs={{0,24},{8,0},{16,8},{24,16},{1,25},{9,1},{17,9},{25,17},{2,26},{10... | collective-permute-start | bytes 98312 | tf_op jit(solution)/shard_map/ppermute | solution.py:229
  68.5 4.5 %collective-permute-done.1.b1_far = f32[32,8,640]{2,1,0:T(8,128)S(1)} collective-permute-done((f32[32,8,640]{2,1,0:T(8,128)S(1)}, f32[32,8,640]{2,1,0:T(8,128)S(1)}, u32[]{:S(2)}, u32[]{:S(2)}) %collective-permute-start.1) | collective-permute-done | bytes 655392 | tf_op jit(solution)/shard_map/ppermute | solution.py:222
  73.0 3.9 %collective-permute-start.8 = (f32[32,256]{1,0:T(8,128)S(1)}, f32[32,256]{1,0:T(8,128)S(1)}, u32[]{:S(2)}, u32[]{:S(2)}) collective-permute-start(f32[32,256]{1,0:T(8,128)S(1)} %get-tuple-element.15), channel_id=1, source_target_pairs={{0,16},{8,24},{16,0},{24,8},{1,17},{9,25},{17,1},{25,9},{2,18},{10... | collective-permute-start | bytes 98312 | tf_op jit(solution)/shard_map/ppermute | solution.py:229
  76.9 0.0 collective-permute-done.2.b3
  76.9 3.6 %collective-permute-start.7 = (f32[32,256]{1,0:T(8,128)S(1)}, f32[32,256]{1,0:T(8,128)S(1)}, u32[]{:S(2)}, u32[]{:S(2)}) collective-permute-start(f32[32,256]{1,0:T(8,128)S(1)} %get-tuple-element.16), channel_id=1, source_target_pairs={{0,8},{8,16},{16,24},{24,0},{1,9},{9,17},{17,25},{25,1},{2,10},{10... | collective-permute-start | bytes 98312 | tf_op jit(solution)/shard_map/ppermute | solution.py:229
  80.5 2.1 %collective-permute-done.5.far = f32[32,8,640]{2,1,0:T(8,128)S(1)} collective-permute-done((f32[32,8,640]{2,1,0:T(8,128)S(1)}, f32[32,8,640]{2,1,0:T(8,128)S(1)}, u32[]{:S(2)}, u32[]{:S(2)}) %collective-permute-start.5) | collective-permute-done | bytes 655392 | tf_op jit(solution)/shard_map/ppermute | solution.py:225
  82.6 0.0 copy-start.6
  82.6 0.9 copy-done.6
  83.5 0.6 collective-permute-done.3.near
  84.1 0.0 all-to-all-done.1.x_ref
  84.1 0.0 copy-done.5
  84.1 7.3 %shard_map.79 = f32[2,128,640]{2,1,0:T(8,128)} custom-call(f32[16,2,8,2048]{3,2,1,0:T(8,128)} %all-to-all-done.1.x_ref, f32[32,8,640]{2,1,0:T(8,128)S(1)} %collective-permute-done.b1, f32[32,8,640]{2,1,0:T(8,128)S(1)} %collective-permute-done.1.b1_far, f32[32,8,640]{2,1,0:T(8,128)S(1)} %collective-permute-done.2.b3, ...), custom_call_target="tpu_custom_call" | custom-call | flops 2013265920 | bytes 8388608 | tf_op jit(solution)/shard_map/pallas_call | solution.py:118
  91.4 3.5 %all-to-all-start.2 = ((f32[2,128,640]{2,1,0:T(8,128)}), f32[2,128,640]{2,1,0:T(8,128)S(1)}, u32[]{:S(2)}, u32[]{:S(2)}) async-start(f32[2,128,640]{2,1,0:T(8,128)} %shard_map.79), calls=%async_computation.2 | async-start | bytes 1310720 | tf_op jit(solution)/shard_map/all_to_all | solution.py:207
  94.9 0.0 collective-permute-done.9.c3
  94.9 0.0 collective-permute-done.8.c2
  95.0 0.0 collective-permute-done.7.c1
  95.0 1.8 %all-to-all-done.2.part_ref = f32[2,128,640]{2,1,0:T(8,128)S(1)} async-done(((f32[2,128,640]{2,1,0:T(8,128)}), f32[2,128,640]{2,1,0:T(8,128)S(1)}, u32[]{:S(2)}, u32[]{:S(2)}) %all-to-all-start.2) | async-done | bytes 655392 | tf_op jit(solution)/shard_map/all_to_all | solution.py:207
  96.8 0.2 shard_map.81
  96.9 34.8 %all_to_all.20.p_ref = f32[64,2,896]{2,1,0:T(2,128)S(1)} all-to-all(f32[64,2,896]{2,1,0:T(2,128)S(1)} %shard_map.81), channel_id=1, replica_groups=mesh['y'=8,'zl'=2,'x'=4,'zh'=4,'core'=2] {'y','zl','zh'}, dimensions={0} | all-to-all | bytes 917504 | tf_op jit(solution)/shard_map/all_to_all | solution.py:207
  131.7 5.3 %collective-permute-start.10 = (f32[2,640]{1,0:T(2,128)S(1)}, f32[2,640]{1,0:T(2,128)S(1)}, u32[]{:S(2)}, u32[]{:S(2)}) collective-permute-start(f32[2,640]{1,0:T(2,128)S(1)} %get-tuple-element.10), channel_id=1, source_target_pairs={{0,0},{2,16},{4,32},{6,48},{8,2},{10,18},{12,34},{14,50},{16,4},{1... | collective-permute-start | bytes 15368 | tf_op jit(solution)/shard_map/ppermute | solution.py:244
  137.0 0.1 reshape.19
  137.1 0.6 copy.8
  137.8 3.4 %collective-permute-done.10 = f32[2,640]{1,0:T(2,128)S(1)} collective-permute-done((f32[2,640]{1,0:T(2,128)S(1)}, f32[2,640]{1,0:T(2,128)S(1)}, u32[]{:S(2)}, u32[]{:S(2)}) %collective-permute-start.10) | collective-permute-done | bytes 5152 | tf_op jit(solution)/shard_map/ppermute | solution.py:244
  141.1 0.6 copy.10
  (2 shorter events, 0.0 us)
Async XLA Ops:
  2.3 29.6 %all-to-all-start = ((f32[64,2,8,128]{3,2,1,0:T(8,128)}), f32[64,2,8,128]{3,2,1,0:T(8,128)S(1)}, u32[]{:S(2)}, u32[]{:S(2)}) async-start(f32[64,2,8,128]{3,2,1,0:T(8,128)} %shard_map.78), calls=%async_computation | async-start | bytes 1048576 | tf_op jit(solution)/shard_map/all_to_all | solution.py:207
  14.8 1.6 %copy-start = (f32[4,4,64,512]{3,2,1,0:T(8,128)S(1)}, f32[4,4,64,512]{3,2,1,0:T(8,128)}, u32[]{:S(2)}) copy-start(f32[4,4,64,512]{3,2,1,0:T(8,128)} %a_ref.1) | copy-start | bytes 6291460
  20.9 15.5 %copy-start.4 = (f32[64,8,640]{2,1,0:T(8,128)S(1)}, f32[64,8,640]{2,1,0:T(8,128)}, u32[]{:S(2)}) copy-start(f32[64,8,640]{2,1,0:T(8,128)} %b0) | copy-start | bytes 3932164
  32.0 52.2 %all-to-all-start.1 = ((f32[16,2,8,2048]{3,2,1,0:T(8,128)}), f32[16,2,8,2048]{3,2,1,0:T(8,128)}, u32[]{:S(2)}, u32[]{:S(2)}) async-start(f32[16,2,8,2048]{3,2,1,0:T(8,128)} %shard_map.77), calls=%async_computation.1 | async-start | bytes 4194304 | tf_op jit(solution)/shard_map/all_to_all | solution.py:207
  36.4 28.1 %copy-start.7 = (s32[512]{0:T(512)S(1)}, s32[512]{0:T(512)}, u32[]{:S(2)}) copy-start(s32[512]{0:T(512)} %param.10) | copy-start | bytes 6148
  36.4 28.3 %copy-start.1 = (f32[4,4,64,512]{3,2,1,0:T(8,128)S(1)}, f32[4,4,64,512]{3,2,1,0:T(8,128)}, u32[]{:S(2)}) copy-start(f32[4,4,64,512]{3,2,1,0:T(8,128)} %a_ref.1) | copy-start | bytes 6291460
  36.5 28.2 %copy-start.2 = (s32[32]{0:T(128)S(1)}, s32[32]{0:T(128)}, u32[]{:S(2)}) copy-start(s32[32]{0:T(128)} %occ_ref.1) | copy-start | bytes 388
  36.5 28.2 %copy-start.3 = (s32[128]{0:T(128)S(1)}, s32[128]{0:T(128)}, u32[]{:S(2)}) copy-start(s32[128]{0:T(128)} %param.11) | copy-start | bytes 1540
  36.6 17.2 %collective-permute-start.4 = (f32[32,8,640]{2,1,0:T(8,128)S(1)}, f32[32,8,640]{2,1,0:T(8,128)S(1)}, u32[]{:S(2)}, u32[]{:S(2)}) collective-permute-start(f32[32,8,640]{2,1,0:T(8,128)S(1)} %get-tuple-element.12), channel_id=1, source_target_pairs={{0,24},{8,0},{16,8},{24,16},{1,25},{9,1},{17,9},{25,17},{2,26},{10... | collective-permute-start | bytes 1966088 | tf_op jit(solution)/shard_map/ppermute | solution.py:221
  39.0 19.9 %collective-permute-start = (f32[32,8,640]{2,1,0:T(8,128)S(1)}, f32[32,8,640]{2,1,0:T(8,128)S(1)}, u32[]{:S(2)}, u32[]{:S(2)}) collective-permute-start(f32[32,8,640]{2,1,0:T(8,128)S(1)} %get-tuple-element.13), channel_id=1, source_target_pairs={{0,8},{8,16},{16,24},{24,0},{1,9},{9,17},{17,25},{25,1},{2,10},{10... | collective-permute-start | bytes 1966088 | tf_op jit(solution)/shard_map/ppermute | solution.py:220
  43.8 20.8 %collective-permute-start.6 = (f32[64,2,8,128]{3,2,1,0:T(8,128)S(1)}, f32[64,2,8,128]{3,2,1,0:T(8,128)S(1)}, u32[]{:S(2)}, u32[]{:S(2)}) collective-permute-start(f32[64,2,8,128]{3,2,1,0:T(8,128)S(1)} %all-to-all-done.own_ref), channel_id=1, source_target_pairs={{0,1},{1,0},{2,3},{3,2},{4,5},{5,4},{6,7},{7,6},{8,9},{9,8},{10,11... | collective-permute-start | bytes 1572872 | tf_op jit(solution)/shard_map/ppermute | solution.py:218
  45.7 27.3 %collective-permute-start.1 = (f32[32,8,640]{2,1,0:T(8,128)S(1)}, f32[32,8,640]{2,1,0:T(8,128)S(1)}, u32[]{:S(2)}, u32[]{:S(2)}) collective-permute-start(f32[32,8,640]{2,1,0:T(8,128)S(1)} %get-tuple-element.12), channel_id=1, source_target_pairs={{0,8},{8,16},{16,24},{24,0},{1,9},{9,17},{17,25},{25,1},{2,10},{10... | collective-permute-start | bytes 1966088 | tf_op jit(solution)/shard_map/ppermute | solution.py:222
  47.7 29.2 %collective-permute-start.2 = (f32[32,8,640]{2,1,0:T(8,128)S(1)}, f32[32,8,640]{2,1,0:T(8,128)S(1)}, u32[]{:S(2)}, u32[]{:S(2)}) collective-permute-start(f32[32,8,640]{2,1,0:T(8,128)S(1)} %get-tuple-element.13), channel_id=1, source_target_pairs={{0,24},{8,0},{16,8},{24,16},{1,25},{9,1},{17,9},{25,17},{2,26},{10... | collective-permute-start | bytes 1966088 | tf_op jit(solution)/shard_map/ppermute | solution.py:223
  53.8 30.4 %copy-start.5 = (f32[32,8,640]{2,1,0:T(8,128)}, f32[32,8,640]{2,1,0:T(8,128)S(1)}, u32[]{:S(2)}) copy-start(f32[32,8,640]{2,1,0:T(8,128)S(1)} %collective-permute-done.4.b3_far) | copy-start | bytes 1966084
  53.8 28.9 %collective-permute-start.5 = (f32[32,8,640]{2,1,0:T(8,128)S(1)}, f32[32,8,640]{2,1,0:T(8,128)S(1)}, u32[]{:S(2)}, u32[]{:S(2)}) collective-permute-start(f32[32,8,640]{2,1,0:T(8,128)S(1)} %collective-permute-done.4.b3_far), channel_id=1, source_target_pairs={{0,24},{8,0},{16,8},{24,16},{1,25},{9,1},{17,9},{25,17},{2,26},{10... | collective-permute-start | bytes 1966088 | tf_op jit(solution)/shard_map/ppermute | solution.py:225
  58.9 25.2 %collective-permute-start.3 = (f32[32,8,640]{2,1,0:T(8,128)S(1)}, f32[32,8,640]{2,1,0:T(8,128)}, u32[]{:S(2)}, u32[]{:S(2)}) collective-permute-start(f32[32,8,640]{2,1,0:T(8,128)S(1)} %collective-permute-done.b1), channel_id=1, source_target_pairs={{0,8},{8,16},{16,24},{24,0},{1,9},{9,17},{17,25},{25,1},{2,10},{10... | collective-permute-start | bytes 1966088 | tf_op jit(solution)/shard_map/ppermute | solution.py:224
  66.5 28.4 %collective-permute-start.9 = (f32[32,256]{1,0:T(8,128)S(1)}, f32[32,256]{1,0:T(8,128)S(1)}, u32[]{:S(2)}, u32[]{:S(2)}) collective-permute-start(f32[32,256]{1,0:T(8,128)S(1)} %get-tuple-element.14), channel_id=1, source_target_pairs={{0,24},{8,0},{16,8},{24,16},{1,25},{9,1},{17,9},{25,17},{2,26},{10... | collective-permute-start | bytes 98312 | tf_op jit(solution)/shard_map/ppermute | solution.py:229
  73.0 22.0 %collective-permute-start.8 = (f32[32,256]{1,0:T(8,128)S(1)}, f32[32,256]{1,0:T(8,128)S(1)}, u32[]{:S(2)}, u32[]{:S(2)}) collective-permute-start(f32[32,256]{1,0:T(8,128)S(1)} %get-tuple-element.15), channel_id=1, source_target_pairs={{0,16},{8,24},{16,0},{24,8},{1,17},{9,25},{17,1},{25,9},{2,18},{10... | collective-permute-start | bytes 98312 | tf_op jit(solution)/shard_map/ppermute | solution.py:229
  76.9 18.0 %collective-permute-start.7 = (f32[32,256]{1,0:T(8,128)S(1)}, f32[32,256]{1,0:T(8,128)S(1)}, u32[]{:S(2)}, u32[]{:S(2)}) collective-permute-start(f32[32,256]{1,0:T(8,128)S(1)} %get-tuple-element.16), channel_id=1, source_target_pairs={{0,8},{8,16},{16,24},{24,0},{1,9},{9,17},{17,25},{25,1},{2,10},{10... | collective-permute-start | bytes 98312 | tf_op jit(solution)/shard_map/ppermute | solution.py:229
  82.6 0.9 copy-start.6
  91.4 5.4 %all-to-all-start.2 = ((f32[2,128,640]{2,1,0:T(8,128)}), f32[2,128,640]{2,1,0:T(8,128)S(1)}, u32[]{:S(2)}, u32[]{:S(2)}) async-start(f32[2,128,640]{2,1,0:T(8,128)} %shard_map.79), calls=%async_computation.2 | async-start | bytes 1310720 | tf_op jit(solution)/shard_map/all_to_all | solution.py:207
  131.7 9.4 %collective-permute-start.10 = (f32[2,640]{1,0:T(2,128)S(1)}, f32[2,640]{1,0:T(2,128)S(1)}, u32[]{:S(2)}, u32[]{:S(2)}) collective-permute-start(f32[2,640]{1,0:T(2,128)S(1)} %get-tuple-element.10), channel_id=1, source_target_pairs={{0,0},{2,16},{4,32},{6,48},{8,2},{10,18},{12,34},{14,50},{16,4},{1... | collective-permute-start | bytes 15368 | tf_op jit(solution)/shard_map/ppermute | solution.py:244

commit v8 on v7

--- a/solution.py
+++ b/solution.py
@@ -148,26 +148,36 @@
     )(w.reshape(8, 4, 8, 128))
 
 
-def pack_kernel(part_ref, c0, c1, c2, c3, o_ref, ladder_sum, cycle_sum):
-    ladder_sum[...] = part_ref[0] + part_ref[1]
-    cycle_sum[...] = (c0[...] + c1[...]) + (c2[...] + c3[...])
-    for d in range(64):
-        o_ref[d, :, pl.ds(0, 640)] = ladder_sum[pl.ds(2 * d, 2), :]
-        o_ref[d, :, pl.ds(640, 256)] = cycle_sum[pl.ds(d // 4 * 2, 2), :]
+def cores_kernel(p_ref, o_ref, total):
+    total[...] = p_ref[0] + p_ref[1]
+    for y in range(8):
+        for d in range(8):
+            o_ref[d, y] = total[pl.ds(16 * y + 2 * d, 2), :]
+
+
+def depth_kernel(p_ref, o_ref):
+    for y in range(8):
+        p = [p_ref[s, y] for s in range(8)]
+        o_ref[y] = ((p[0] + p[1]) + (p[2] + p[3])) + ((p[4] + p[5]) + (p[6] + p[7]))
+
+
+def fold_kernel(c0, c1, c2, c3, keep_ref, give_ref):
+    zl = lax.axis_index("zl")
+    keep_ref[...] = (c0[zl] + c1[zl]) + (c2[zl] + c3[zl])
+    give_ref[...] = (c0[1 - zl] + c1[1 - zl]) + (c2[1 - zl] + c3[1 - zl])
+
+
+def pack_kernel(l_ref, keep_ref, got_ref, o_ref):
+    for y in range(8):
+        rows = pl.ds(2 * y, 2)
+        o_ref[y, :, pl.ds(0, 640)] = l_ref[y]
+        o_ref[y, :, pl.ds(640, 256)] = keep_ref[rows, :] + got_ref[rows, :]
 
 
 def finish_kernel(p_ref, ladder_ref, cycle_ref):
-    zh = lax.axis_index("zh")
-    total = [p_ref[d, :, pl.ds(0, 640)] for d in range(8)]
-    for d in range(8, 64):
-        total[d % 8] += p_ref[d, :, pl.ds(0, 640)]
-    while len(total) > 1:
-        total = [p + q for p, q in zip(total[::2], total[1::2])]
-    ladder_ref[...] = total[0]
-    for y in range(8):
-        cycle_ref[y] = (
-            p_ref[y * 8 + zh, :, pl.ds(640, 256)] + p_ref[y * 8 + 4 + zh, :, pl.ds(640, 256)]
-        )
+    p = [p_ref[y, :, pl.ds(0, 640)] for y in range(8)]
+    ladder_ref[...] = ((p[0] + p[1]) + (p[2] + p[3])) + ((p[4] + p[5]) + (p[6] + p[7]))
+    cycle_ref[...] = p_ref[:, :, pl.ds(640, 256)]
 
 
 def cycle_kernel(occ_ref, a_ref, own_ref, other_ref, vir_ref, pair_ref, o_ref, turned):
@@ -185,8 +195,10 @@
     turned[...] = total.T
     for x in range(4):
         to = lax.rem(x + 4 - lax.axis_index("x"), 4)
-        for d in range(16):
-            o_ref[to, pl.ds(2 * d, 2), :] = turned[pl.ds(8 * d + 2 * x, 2), :]
+        for zl in range(2):
+            for y in range(8):
+                rows = turned[pl.ds(16 * y + 8 * zl + 2 * x, 2), :]
+                o_ref[to, zl, pl.ds(2 * y, 2), :] = rows
 
 
 def cycle(occ, amplitudes, own, other, vir, pair):
@@ -194,7 +206,7 @@
         cycle_kernel,
         in_specs=[pl.BlockSpec(memory_space=pltpu.SMEM)] + [VMEM] * 5,
         out_specs=VMEM,
-        out_shape=jax.ShapeDtypeStruct((4, 32, 256), F32),
+        out_shape=jax.ShapeDtypeStruct((4, 2, 16, 256), F32),
         scratch_shapes=[pltpu.VMEM((128, 256), F32)],
         compiler_params=pltpu.CompilerParams(vmem_limit_bytes=VMEM_LIMIT),
         cost_estimate=pl.CostEstimate(
@@ -229,11 +241,13 @@
     parts = [parts[0]] + [lax.ppermute(parts[s], "x", ring[s]) for s in (1, 2, 3)]
 
     part = ladder(x, b1, b1_far, b3, near, ladder_ints, b3_far, far)
-    part = exchange(part, ("core",))
-    both = small(pack_kernel, (64, 2, 896), part, *parts, scratch=[(128, 640), (32, 256)])
-    both = exchange(both, ("y", "zl", "zh"))
-    part, cycle_part = small(finish_kernel, [(2, 640), (8, 2, 256)], both)
-    cycle_resid = cycle_part.reshape(8, 2, 4, 64).transpose(0, 2, 3, 1).reshape(32, 64, 2)
+    _, *parts = lax.optimization_barrier((part, *parts))
+    keep, give = small(fold_kernel, [(16, 256), (16, 256)], *parts)
+    got = lax.ppermute(give, "zl", [(0, 1), (1, 0)])
+    part, keep = lax.optimization_barrier((exchange(part, ("core",)), keep))
+    part = small(cores_kernel, (8, 8, 2, 640), part, scratch=[(128, 640)])
+    part, got = lax.optimization_barrier((exchange(part, ("zl", "zh")), got))
+    part = small(depth_kernel, (8, 2, 640), part)
     move = [
         ((s * 4 + a) * 4 + hi * 2 + lo, (hi * 4 + lo * 2 + s) * 4 + a)
         for s in range(2)
@@ -241,7 +255,10 @@
         for hi in range(2)
         for lo in range(2)
     ]
-    ladder_resid = lax.ppermute(part, ("zl", "x", "zh"), move)
+    part = lax.ppermute(part, ("zl", "x", "zh"), move)
+    both = exchange(small(pack_kernel, (8, 2, 896), part, keep, got), ("y",))
+    ladder_resid, cycle_part = small(finish_kernel, [(2, 640), (8, 2, 256)], both)
+    cycle_resid = cycle_part.reshape(8, 2, 4, 64).transpose(0, 2, 3, 1).reshape(32, 64, 2)
     return ladder_resid, cycle_resid
 
 

time: 143 us -> 148 us (1.035)
  the two profiles are of different devices: /device:TPU:6 before, /device:TPU:64 now
where the time goes in v8:
time: 148 us; the launch traced here: 147 us
  starting transfers between devices  64.4 us (44%)
  waiting for transfers between devices  47 us (32%)
  Pallas kernels  16.8 us (11%)
  blocking collectives  14.5 us (10%)
  local copies, waits for them, and re-layouts  3.42 us (2%)
    all_to_all x4, starting transfers between devices, exchange(): return lax.all_to_all(v, axes, split_axis=0, concat_axis=0, tiled=True)  30.1 us
    all_to_all x4, waiting for transfers between devices, exchange(): return lax.all_to_all(v, axes, split_axis=0, concat_axis=0, tiled=True)  17.9 us
    all_to_all x1, blocking collectives, exchange(): return lax.all_to_all(v, axes, split_axis=0, concat_axis=0, tiled=True)  14.5 us
    ppermute x3, starting transfers between devices, body(): lax.ppermute(parts[s], 'x', ring[s])  9.34 us
    pallas_call x1, Pallas kernels, ladder(): pl.pallas_call(ladder_kernel, in_specs=[VMEM] * 5 + [anywhere] * 3, out_s...  7.24 us
    ppermute x1, waiting for transfers between devices, body(): part = lax.ppermute(part, ('zl', 'x', 'zh'), move)  6.98 us
    ppermute x1, waiting for transfers between devices, body(): got = lax.ppermute(give, 'zl', [(0, 1), (1, 0)])  5.64 us
    ppermute x1, waiting for transfers between devices, body(): b1_far = lax.ppermute(upper, 'x', ring[1])  4.98 us
  transfers between devices with their start and end apart: 16, of which 10 were waited for; matrix products, arithmetic and copies ran while one was open for 0% of the time, Pallas kernels for 9%

profile of v8, /device:TPU:64, one launch (start us, length us, event | category | flops | bytes accessed | tf_op | source)
XLA Modules:
  0.0 147.1 jit_solution(12479467679701552365)
XLA Ops:
  0.6 1.7 %shard_map.78 = f32[64,2,8,128]{3,2,1,0:T(8,128)} custom-call(f32[8,4,8,128]{3,2,1,0:T(8,128)} %bitcast.15), custom_call_target="tpu_custom_call" | custom-call | bytes 1048576 | tf_op jit(solution)/shard_map/pallas_call | solution.py:140
  2.3 11.6 %all-to-all-start = ((f32[64,2,8,128]{3,2,1,0:T(8,128)}), f32[64,2,8,128]{3,2,1,0:T(8,128)S(1)}, u32[]{:S(2)}, u32[]{:S(2)}) async-start(f32[64,2,8,128]{3,2,1,0:T(8,128)} %shard_map.78), calls=%async_computation | async-start | bytes 1048576 | tf_op jit(solution)/shard_map/all_to_all | solution.py:219
  13.9 0.0 copy-start
  13.9 1.6 %copy-done = f32[4,4,64,512]{3,2,1,0:T(8,128)S(1)} copy-done((f32[4,4,64,512]{3,2,1,0:T(8,128)S(1)}, f32[4,4,64,512]{3,2,1,0:T(8,128)}, u32[]{:S(2)}) %copy-start) | copy-done | bytes 2097176
  15.5 4.6 %shard_map.77 = f32[16,2,8,2048]{3,2,1,0:T(8,128)} custom-call(f32[4,2,2,64,512]{4,3,2,1,0:T(8,128)S(1)} %bitcast.13), custom_call_target="tpu_custom_call" | custom-call | flops 1048576 | bytes 4194304 | tf_op jit(solution)/shard_map/pallas_call | solution.py:52
  20.1 0.0 copy-start.4
  20.1 11.5 %all-to-all-done.own_ref = f32[64,2,8,128]{3,2,1,0:T(8,128)S(1)} async-done(((f32[64,2,8,128]{3,2,1,0:T(8,128)}), f32[64,2,8,128]{3,2,1,0:T(8,128)S(1)}, u32[]{:S(2)}, u32[]{:S(2)}) %all-to-all-start) | async-done | bytes 524320 | tf_op jit(solution)/shard_map/all_to_all | solution.py:219
  31.6 5.0 %all-to-all-start.1 = ((f32[16,2,8,2048]{3,2,1,0:T(8,128)}), f32[16,2,8,2048]{3,2,1,0:T(8,128)}, u32[]{:S(2)}, u32[]{:S(2)}) async-start(f32[16,2,8,2048]{3,2,1,0:T(8,128)} %shard_map.77), calls=%async_computation.1 | async-start | bytes 4194304 | tf_op jit(solution)/shard_map/all_to_all | solution.py:219
  36.6 0.0 copy-done.4
  36.7 0.0 copy-start.7
  36.7 0.0 copy-start.1
  36.7 0.0 copy-start.2
  36.7 0.0 copy-start.3
  36.7 0.1 fusion
  36.8 3.9 %collective-permute-start.4 = (f32[32,8,640]{2,1,0:T(8,128)S(1)}, f32[32,8,640]{2,1,0:T(8,128)S(1)}, u32[]{:S(2)}, u32[]{:S(2)}) collective-permute-start(f32[32,8,640]{2,1,0:T(8,128)S(1)} %get-tuple-element.32), channel_id=1, source_target_pairs={{0,24},{8,0},{16,8},{24,16},{1,25},{9,1},{17,9},{25,17},{2,26},{10... | collective-permute-start | bytes 1966088 | tf_op jit(solution)/shard_map/ppermute | solution.py:233
  40.8 2.0 %collective-permute-start = (f32[32,8,640]{2,1,0:T(8,128)S(1)}, f32[32,8,640]{2,1,0:T(8,128)S(1)}, u32[]{:S(2)}, u32[]{:S(2)}) collective-permute-start(f32[32,8,640]{2,1,0:T(8,128)S(1)} %get-tuple-element.33), channel_id=1, source_target_pairs={{0,8},{8,16},{16,24},{24,0},{1,9},{9,17},{17,25},{25,1},{2,10},{10... | collective-permute-start | bytes 1966088 | tf_op jit(solution)/shard_map/ppermute | solution.py:232
  42.8 1.9 %collective-permute-start.6 = (f32[64,2,8,128]{3,2,1,0:T(8,128)S(1)}, f32[64,2,8,128]{3,2,1,0:T(8,128)S(1)}, u32[]{:S(2)}, u32[]{:S(2)}) collective-permute-start(f32[64,2,8,128]{3,2,1,0:T(8,128)S(1)} %all-to-all-done.own_ref), channel_id=1, source_target_pairs={{0,1},{1,0},{2,3},{3,2},{4,5},{5,4},{6,7},{7,6},{8,9},{9,8},{10,11... | collective-permute-start | bytes 1572872 | tf_op jit(solution)/shard_map/ppermute | solution.py:230
  44.7 2.4 %collective-permute-start.1 = (f32[32,8,640]{2,1,0:T(8,128)S(1)}, f32[32,8,640]{2,1,0:T(8,128)S(1)}, u32[]{:S(2)}, u32[]{:S(2)}) collective-permute-start(f32[32,8,640]{2,1,0:T(8,128)S(1)} %get-tuple-element.32), channel_id=1, source_target_pairs={{0,8},{8,16},{16,24},{24,0},{1,9},{9,17},{17,25},{25,1},{2,10},{10... | collective-permute-start | bytes 1966088 | tf_op jit(solution)/shard_map/ppermute | solution.py:234
  47.2 4.6 %collective-permute-start.2 = (f32[32,8,640]{2,1,0:T(8,128)S(1)}, f32[32,8,640]{2,1,0:T(8,128)S(1)}, u32[]{:S(2)}, u32[]{:S(2)}) collective-permute-start(f32[32,8,640]{2,1,0:T(8,128)S(1)} %get-tuple-element.33), channel_id=1, source_target_pairs={{0,24},{8,0},{16,8},{24,16},{1,25},{9,1},{17,9},{25,17},{2,26},{10... | collective-permute-start | bytes 1966088 | tf_op jit(solution)/shard_map/ppermute | solution.py:235
  51.8 1.7 %collective-permute-done.4.b3_far = f32[32,8,640]{2,1,0:T(8,128)S(1)} collective-permute-done((f32[32,8,640]{2,1,0:T(8,128)S(1)}, f32[32,8,640]{2,1,0:T(8,128)S(1)}, u32[]{:S(2)}, u32[]{:S(2)}) %collective-permute-start.4) | collective-permute-done | bytes 655392 | tf_op jit(solution)/shard_map/ppermute | solution.py:233
  53.5 0.0 copy-start.5
  53.5 4.3 %collective-permute-start.5 = (f32[32,8,640]{2,1,0:T(8,128)S(1)}, f32[32,8,640]{2,1,0:T(8,128)S(1)}, u32[]{:S(2)}, u32[]{:S(2)}) collective-permute-start(f32[32,8,640]{2,1,0:T(8,128)S(1)} %collective-permute-done.4.b3_far), channel_id=1, source_target_pairs={{0,24},{8,0},{16,8},{24,16},{1,25},{9,1},{17,9},{25,17},{2,26},{10... | collective-permute-start | bytes 1966088 | tf_op jit(solution)/shard_map/ppermute | solution.py:237
  57.8 3.8 %collective-permute-done.b1 = f32[32,8,640]{2,1,0:T(8,128)S(1)} collective-permute-done((f32[32,8,640]{2,1,0:T(8,128)S(1)}, f32[32,8,640]{2,1,0:T(8,128)S(1)}, u32[]{:S(2)}, u32[]{:S(2)}) %collective-permute-start) | collective-permute-done | bytes 655392 | tf_op jit(solution)/shard_map/ppermute | solution.py:232
  61.5 1.9 %collective-permute-start.3 = (f32[32,8,640]{2,1,0:T(8,128)S(1)}, f32[32,8,640]{2,1,0:T(8,128)}, u32[]{:S(2)}, u32[]{:S(2)}) collective-permute-start(f32[32,8,640]{2,1,0:T(8,128)S(1)} %collective-permute-done.b1), channel_id=1, source_target_pairs={{0,8},{8,16},{16,24},{24,0},{1,9},{9,17},{17,25},{25,1},{2,10},{10... | collective-permute-start | bytes 1966088 | tf_op jit(solution)/shard_map/ppermute | solution.py:236
  63.4 0.0 collective-permute-done.6.other_ref
  63.5 0.0 copy-done.7
  63.5 0.1 broadcast_in_dim.4.vir_ref
  63.6 0.0 copy-done.1
  63.6 0.0 copy-done.2
  63.6 0.0 copy-done.3
  63.6 1.8 %shard_map.80 = f32[4,2,16,256]{3,2,1,0:T(8,128)S(1)} custom-call(s32[32]{0:T(128)S(1)} %copy-done.2, f32[4,4,64,512]{3,2,1,0:T(8,128)S(1)} %copy-done.1, f32[64,2,8,128]{3,2,1,0:T(8,128)S(1)} %all-to-all-done.own_ref, f32[64,2,8,128]{3,2,1,0:T(8,128)S(1)} %collective-permute-done.6.other_ref, s32[512,128]{1,0:T(8,128)S(1)} %broadcast_in_dim.4.vir_ref, ...), custom_call_target="tpu_custom_call" | custom-call | flops 402653184 | bytes 3145728 | tf_op jit(solution)/shard_map/pallas_call | solution.py:205
  65.4 5.1 %collective-permute-start.9 = (f32[2,16,256]{2,1,0:T(8,128)S(1)}, f32[2,16,256]{2,1,0:T(8,128)S(1)}, u32[]{:S(2)}, u32[]{:S(2)}) collective-permute-start(f32[2,16,256]{2,1,0:T(8,128)S(1)} %get-tuple-element.34), channel_id=1, source_target_pairs={{0,24},{8,0},{16,8},{24,16},{1,25},{9,1},{17,9},{25,17},{2,26},{10... | collective-permute-start | bytes 98312 | tf_op jit(solution)/shard_map/ppermute | solution.py:241
  70.6 5.0 %collective-permute-done.1.b1_far = f32[32,8,640]{2,1,0:T(8,128)S(1)} collective-permute-done((f32[32,8,640]{2,1,0:T(8,128)S(1)}, f32[32,8,640]{2,1,0:T(8,128)S(1)}, u32[]{:S(2)}, u32[]{:S(2)}) %collective-permute-start.1) | collective-permute-done | bytes 655392 | tf_op jit(solution)/shard_map/ppermute | solution.py:234
  75.6 1.9 %collective-permute-start.8 = (f32[2,16,256]{2,1,0:T(8,128)S(1)}, f32[2,16,256]{2,1,0:T(8,128)S(1)}, u32[]{:S(2)}, u32[]{:S(2)}) collective-permute-start(f32[2,16,256]{2,1,0:T(8,128)S(1)} %get-tuple-element.35), channel_id=1, source_target_pairs={{0,16},{8,24},{16,0},{24,8},{1,17},{9,25},{17,1},{25,9},{2,18},{10... | collective-permute-start | bytes 98312 | tf_op jit(solution)/shard_map/ppermute | solution.py:241
  77.5 0.0 collective-permute-done.2.b3
  77.5 2.3 %collective-permute-start.7 = (f32[2,16,256]{2,1,0:T(8,128)S(1)}, f32[2,16,256]{2,1,0:T(8,128)S(1)}, u32[]{:S(2)}, u32[]{:S(2)}) collective-permute-start(f32[2,16,256]{2,1,0:T(8,128)S(1)} %get-tuple-element.36), channel_id=1, source_target_pairs={{0,8},{8,16},{16,24},{24,0},{1,9},{9,17},{17,25},{25,1},{2,10},{10... | collective-permute-start | bytes 98312 | tf_op jit(solution)/shard_map/ppermute | solution.py:241
  79.8 1.7 %collective-permute-done.5.far = f32[32,8,640]{2,1,0:T(8,128)S(1)} collective-permute-done((f32[32,8,640]{2,1,0:T(8,128)S(1)}, f32[32,8,640]{2,1,0:T(8,128)S(1)}, u32[]{:S(2)}, u32[]{:S(2)}) %collective-permute-start.5) | collective-permute-done | bytes 655392 | tf_op jit(solution)/shard_map/ppermute | solution.py:237
  81.5 0.0 copy-start.6
  81.5 0.9 copy-done.6
  82.4 4.4 %collective-permute-done.3.near = f32[32,8,640]{2,1,0:T(8,128)} collective-permute-done((f32[32,8,640]{2,1,0:T(8,128)S(1)}, f32[32,8,640]{2,1,0:T(8,128)}, u32[]{:S(2)}, u32[]{:S(2)}) %collective-permute-start.3) | collective-permute-done | bytes 655392 | tf_op jit(solution)/shard_map/ppermute | solution.py:236
  86.8 0.0 all-to-all-done.1.x_ref
  86.8 0.0 copy-done.5
  86.8 7.2 %shard_map.79 = f32[2,128,640]{2,1,0:T(8,128)} custom-call(f32[16,2,8,2048]{3,2,1,0:T(8,128)} %all-to-all-done.1.x_ref, f32[32,8,640]{2,1,0:T(8,128)S(1)} %collective-permute-done.b1, f32[32,8,640]{2,1,0:T(8,128)S(1)} %collective-permute-done.1.b1_far, f32[32,8,640]{2,1,0:T(8,128)S(1)} %collective-permute-done.2.b3, ...), custom_call_target="tpu_custom_call" | custom-call | flops 2013265920 | bytes 8388608 | tf_op jit(solution)/shard_map/pallas_call | solution.py:118
  94.0 3.5 %all-to-all-start.2 = ((f32[2,128,640]{2,1,0:T(8,128)}), f32[2,128,640]{2,1,0:T(8,128)S(1)}, u32[]{:S(2)}, u32[]{:S(2)}) async-start(f32[2,128,640]{2,1,0:T(8,128)} %shard_map.79), calls=%async_computation.2 | async-start | bytes 1310720 | tf_op jit(solution)/shard_map/all_to_all | solution.py:219
  97.5 0.0 collective-permute-done.9.c3
  97.5 0.0 collective-permute-done.8.c2
  97.6 0.0 collective-permute-done.7.c1
  97.6 1.8 %all-to-all-done.2.p_ref = f32[2,128,640]{2,1,0:T(8,128)S(1)} async-done(((f32[2,128,640]{2,1,0:T(8,128)}), f32[2,128,640]{2,1,0:T(8,128)S(1)}, u32[]{:S(2)}, u32[]{:S(2)}) %all-to-all-start.2) | async-done | bytes 655392 | tf_op jit(solution)/shard_map/all_to_all | solution.py:219
  99.4 0.9 shard_map.82
  100.2 10.0 %all-to-all-start.3 = ((f32[8,8,2,640]{3,2,1,0:T(2,128)}), f32[8,8,2,640]{3,2,1,0:T(2,128)S(1)}, u32[]{:S(2)}, u32[]{:S(2)}) async-start(f32[8,8,2,640]{3,2,1,0:T(2,128)} %shard_map.82), calls=%async_computation.3 | async-start | bytes 655360 | tf_op jit(solution)/shard_map/all_to_all | solution.py:219
  110.2 1.9 %collective-permute-start.10 = (f32[16,256]{1,0:T(8,128)S(1)}, f32[16,256]{1,0:T(8,128)S(1)}, u32[]{:S(2)}, u32[]{:S(2)}) collective-permute-start(f32[16,256]{1,0:T(8,128)S(1)} %get-tuple-element.26), channel_id=1, source_target_pairs={{0,32},{32,0},{1,33},{33,1},{2,34},{34,2},{3,35},{35,3},{4,36},{36... | collective-permute-start | bytes 49160 | tf_op jit(solution)/shard_map/ppermute | solution.py:246
  112.1 5.6 %collective-permute-done.10.got_ref = f32[16,256]{1,0:T(8,128)S(1)} collective-permute-done((f32[16,256]{1,0:T(8,128)S(1)}, f32[16,256]{1,0:T(8,128)S(1)}, u32[]{:S(2)}, u32[]{:S(2)}) %collective-permute-start.10) | collective-permute-done | bytes 16416 | tf_op jit(solution)/shard_map/ppermute | solution.py:246
  117.7 4.6 %all-to-all-done.3.p_ref = f32[8,8,2,640]{3,2,1,0:T(2,128)S(1)} async-done(((f32[8,8,2,640]{3,2,1,0:T(2,128)}), f32[8,8,2,640]{3,2,1,0:T(2,128)S(1)}, u32[]{:S(2)}, u32[]{:S(2)}) %all-to-all-start.3) | async-done | bytes 327712 | tf_op jit(solution)/shard_map/all_to_all | solution.py:219
  122.3 1.9 %collective-permute-start.11 = (f32[8,2,640]{2,1,0:T(2,128)S(1)}, f32[8,2,640]{2,1,0:T(2,128)S(1)}, u32[]{:S(2)}, u32[]{:S(2)}) collective-permute-start(f32[8,2,640]{2,1,0:T(2,128)S(1)} %shard_map.83), channel_id=1, source_target_pairs={{0,0},{2,16},{4,32},{6,48},{8,2},{10,18},{12,34},{14,50},{16,4},{1... | collective-permute-start | bytes 122888 | tf_op jit(solution)/shard_map/ppermute | solution.py:258
  124.3 7.0 %collective-permute-done.11.l_ref = f32[8,2,640]{2,1,0:T(2,128)S(1)} collective-permute-done((f32[8,2,640]{2,1,0:T(2,128)S(1)}, f32[8,2,640]{2,1,0:T(2,128)S(1)}, u32[]{:S(2)}, u32[]{:S(2)}) %collective-permute-start.11) | collective-permute-done | bytes 40992 | tf_op jit(solution)/shard_map/ppermute | solution.py:258
  131.3 14.5 %all_to_all.25.p_ref = f32[8,2,896]{2,1,0:T(2,128)S(1)} all-to-all(f32[8,2,896]{2,1,0:T(2,128)S(1)} %shard_map.84), channel_id=1, replica_groups=mesh['y'=8,'zl'=2,'x'=4,'zh'=4,'core'=2] {'y'}, dimensions={0} | all-to-all | bytes 114688 | tf_op jit(solution)/shard_map/all_to_all | solution.py:219
  145.8 0.6 shard_map.85
  146.4 0.1 reshape.19
  146.5 0.6 copy.8
  (4 shorter events, 0.1 us)
Async XLA Ops:
  2.3 29.3 %all-to-all-start = ((f32[64,2,8,128]{3,2,1,0:T(8,128)}), f32[64,2,8,128]{3,2,1,0:T(8,128)S(1)}, u32[]{:S(2)}, u32[]{:S(2)}) async-start(f32[64,2,8,128]{3,2,1,0:T(8,128)} %shard_map.78), calls=%async_computation | async-start | bytes 1048576 | tf_op jit(solution)/shard_map/all_to_all | solution.py:219
  13.9 1.6 %copy-start = (f32[4,4,64,512]{3,2,1,0:T(8,128)S(1)}, f32[4,4,64,512]{3,2,1,0:T(8,128)}, u32[]{:S(2)}) copy-start(f32[4,4,64,512]{3,2,1,0:T(8,128)} %a_ref.1) | copy-start | bytes 6291460
  20.1 16.6 %copy-start.4 = (f32[64,8,640]{2,1,0:T(8,128)S(1)}, f32[64,8,640]{2,1,0:T(8,128)}, u32[]{:S(2)}) copy-start(f32[64,8,640]{2,1,0:T(8,128)} %b0) | copy-start | bytes 3932164
  31.6 55.1 %all-to-all-start.1 = ((f32[16,2,8,2048]{3,2,1,0:T(8,128)}), f32[16,2,8,2048]{3,2,1,0:T(8,128)}, u32[]{:S(2)}, u32[]{:S(2)}) async-start(f32[16,2,8,2048]{3,2,1,0:T(8,128)} %shard_map.77), calls=%async_computation.1 | async-start | bytes 4194304 | tf_op jit(solution)/shard_map/all_to_all | solution.py:219
  36.7 26.8 %copy-start.7 = (s32[512]{0:T(512)S(1)}, s32[512]{0:T(512)}, u32[]{:S(2)}) copy-start(s32[512]{0:T(512)} %param.10) | copy-start | bytes 6148
  36.7 26.9 %copy-start.1 = (f32[4,4,64,512]{3,2,1,0:T(8,128)S(1)}, f32[4,4,64,512]{3,2,1,0:T(8,128)}, u32[]{:S(2)}) copy-start(f32[4,4,64,512]{3,2,1,0:T(8,128)} %a_ref.1) | copy-start | bytes 6291460
  36.7 26.9 %copy-start.2 = (s32[32]{0:T(128)S(1)}, s32[32]{0:T(128)}, u32[]{:S(2)}) copy-start(s32[32]{0:T(128)} %occ_ref.1) | copy-start | bytes 388
  36.7 26.9 %copy-start.3 = (s32[128]{0:T(128)S(1)}, s32[128]{0:T(128)}, u32[]{:S(2)}) copy-start(s32[128]{0:T(128)} %param.11) | copy-start | bytes 1540
  36.8 16.7 %collective-permute-start.4 = (f32[32,8,640]{2,1,0:T(8,128)S(1)}, f32[32,8,640]{2,1,0:T(8,128)S(1)}, u32[]{:S(2)}, u32[]{:S(2)}) collective-permute-start(f32[32,8,640]{2,1,0:T(8,128)S(1)} %get-tuple-element.32), channel_id=1, source_target_pairs={{0,24},{8,0},{16,8},{24,16},{1,25},{9,1},{17,9},{25,17},{2,26},{10... | collective-permute-start | bytes 1966088 | tf_op jit(solution)/shard_map/ppermute | solution.py:233
  40.8 20.8 %collective-permute-start = (f32[32,8,640]{2,1,0:T(8,128)S(1)}, f32[32,8,640]{2,1,0:T(8,128)S(1)}, u32[]{:S(2)}, u32[]{:S(2)}) collective-permute-start(f32[32,8,640]{2,1,0:T(8,128)S(1)} %get-tuple-element.33), channel_id=1, source_target_pairs={{0,8},{8,16},{16,24},{24,0},{1,9},{9,17},{17,25},{25,1},{2,10},{10... | collective-permute-start | bytes 1966088 | tf_op jit(solution)/shard_map/ppermute | solution.py:232
  42.8 20.7 %collective-permute-start.6 = (f32[64,2,8,128]{3,2,1,0:T(8,128)S(1)}, f32[64,2,8,128]{3,2,1,0:T(8,128)S(1)}, u32[]{:S(2)}, u32[]{:S(2)}) collective-permute-start(f32[64,2,8,128]{3,2,1,0:T(8,128)S(1)} %all-to-all-done.own_ref), channel_id=1, source_target_pairs={{0,1},{1,0},{2,3},{3,2},{4,5},{5,4},{6,7},{7,6},{8,9},{9,8},{10,11... | collective-permute-start | bytes 1572872 | tf_op jit(solution)/shard_map/ppermute | solution.py:230
  44.7 30.9 %collective-permute-start.1 = (f32[32,8,640]{2,1,0:T(8,128)S(1)}, f32[32,8,640]{2,1,0:T(8,128)S(1)}, u32[]{:S(2)}, u32[]{:S(2)}) collective-permute-start(f32[32,8,640]{2,1,0:T(8,128)S(1)} %get-tuple-element.32), channel_id=1, source_target_pairs={{0,8},{8,16},{16,24},{24,0},{1,9},{9,17},{17,25},{25,1},{2,10},{10... | collective-permute-start | bytes 1966088 | tf_op jit(solution)/shard_map/ppermute | solution.py:234
  47.2 30.3 %collective-permute-start.2 = (f32[32,8,640]{2,1,0:T(8,128)S(1)}, f32[32,8,640]{2,1,0:T(8,128)S(1)}, u32[]{:S(2)}, u32[]{:S(2)}) collective-permute-start(f32[32,8,640]{2,1,0:T(8,128)S(1)} %get-tuple-element.33), channel_id=1, source_target_pairs={{0,24},{8,0},{16,8},{24,16},{1,25},{9,1},{17,9},{25,17},{2,26},{10... | collective-permute-start | bytes 1966088 | tf_op jit(solution)/shard_map/ppermute | solution.py:235
  53.5 33.3 %copy-start.5 = (f32[32,8,640]{2,1,0:T(8,128)}, f32[32,8,640]{2,1,0:T(8,128)S(1)}, u32[]{:S(2)}) copy-start(f32[32,8,640]{2,1,0:T(8,128)S(1)} %collective-permute-done.4.b3_far) | copy-start | bytes 1966084
  53.5 28.0 %collective-permute-start.5 = (f32[32,8,640]{2,1,0:T(8,128)S(1)}, f32[32,8,640]{2,1,0:T(8,128)S(1)}, u32[]{:S(2)}, u32[]{:S(2)}) collective-permute-start(f32[32,8,640]{2,1,0:T(8,128)S(1)} %collective-permute-done.4.b3_far), channel_id=1, source_target_pairs={{0,24},{8,0},{16,8},{24,16},{1,25},{9,1},{17,9},{25,17},{2,26},{10... | collective-permute-start | bytes 1966088 | tf_op jit(solution)/shard_map/ppermute | solution.py:237
  61.5 25.2 %collective-permute-start.3 = (f32[32,8,640]{2,1,0:T(8,128)S(1)}, f32[32,8,640]{2,1,0:T(8,128)}, u32[]{:S(2)}, u32[]{:S(2)}) collective-permute-start(f32[32,8,640]{2,1,0:T(8,128)S(1)} %collective-permute-done.b1), channel_id=1, source_target_pairs={{0,8},{8,16},{16,24},{24,0},{1,9},{9,17},{17,25},{25,1},{2,10},{10... | collective-permute-start | bytes 1966088 | tf_op jit(solution)/shard_map/ppermute | solution.py:236
  65.4 32.1 %collective-permute-start.9 = (f32[2,16,256]{2,1,0:T(8,128)S(1)}, f32[2,16,256]{2,1,0:T(8,128)S(1)}, u32[]{:S(2)}, u32[]{:S(2)}) collective-permute-start(f32[2,16,256]{2,1,0:T(8,128)S(1)} %get-tuple-element.34), channel_id=1, source_target_pairs={{0,24},{8,0},{16,8},{24,16},{1,25},{9,1},{17,9},{25,17},{2,26},{10... | collective-permute-start | bytes 98312 | tf_op jit(solution)/shard_map/ppermute | solution.py:241
  75.6 22.0 %collective-permute-start.8 = (f32[2,16,256]{2,1,0:T(8,128)S(1)}, f32[2,16,256]{2,1,0:T(8,128)S(1)}, u32[]{:S(2)}, u32[]{:S(2)}) collective-permute-start(f32[2,16,256]{2,1,0:T(8,128)S(1)} %get-tuple-element.35), channel_id=1, source_target_pairs={{0,16},{8,24},{16,0},{24,8},{1,17},{9,25},{17,1},{25,9},{2,18},{10... | collective-permute-start | bytes 98312 | tf_op jit(solution)/shard_map/ppermute | solution.py:241
  77.5 20.1 %collective-permute-start.7 = (f32[2,16,256]{2,1,0:T(8,128)S(1)}, f32[2,16,256]{2,1,0:T(8,128)S(1)}, u32[]{:S(2)}, u32[]{:S(2)}) collective-permute-start(f32[2,16,256]{2,1,0:T(8,128)S(1)} %get-tuple-element.36), channel_id=1, source_target_pairs={{0,8},{8,16},{16,24},{24,0},{1,9},{9,17},{17,25},{25,1},{2,10},{10... | collective-permute-start | bytes 98312 | tf_op jit(solution)/shard_map/ppermute | solution.py:241
  81.5 0.9 copy-start.6
  94.0 5.4 %all-to-all-start.2 = ((f32[2,128,640]{2,1,0:T(8,128)}), f32[2,128,640]{2,1,0:T(8,128)S(1)}, u32[]{:S(2)}, u32[]{:S(2)}) async-start(f32[2,128,640]{2,1,0:T(8,128)} %shard_map.79), calls=%async_computation.2 | async-start | bytes 1310720 | tf_op jit(solution)/shard_map/all_to_all | solution.py:219
  100.2 22.1 %all-to-all-start.3 = ((f32[8,8,2,640]{3,2,1,0:T(2,128)}), f32[8,8,2,640]{3,2,1,0:T(2,128)S(1)}, u32[]{:S(2)}, u32[]{:S(2)}) async-start(f32[8,8,2,640]{3,2,1,0:T(2,128)} %shard_map.82), calls=%async_computation.3 | async-start | bytes 655360 | tf_op jit(solution)/shard_map/all_to_all | solution.py:219
  110.2 7.6 %collective-permute-start.10 = (f32[16,256]{1,0:T(8,128)S(1)}, f32[16,256]{1,0:T(8,128)S(1)}, u32[]{:S(2)}, u32[]{:S(2)}) collective-permute-start(f32[16,256]{1,0:T(8,128)S(1)} %get-tuple-element.26), channel_id=1, source_target_pairs={{0,32},{32,0},{1,33},{33,1},{2,34},{34,2},{3,35},{35,3},{4,36},{36... | collective-permute-start | bytes 49160 | tf_op jit(solution)/shard_map/ppermute | solution.py:246
  122.3 8.9 %collective-permute-start.11 = (f32[8,2,640]{2,1,0:T(2,128)S(1)}, f32[8,2,640]{2,1,0:T(2,128)S(1)}, u32[]{:S(2)}, u32[]{:S(2)}) collective-permute-start(f32[8,2,640]{2,1,0:T(2,128)S(1)} %shard_map.83), channel_id=1, source_target_pairs={{0,0},{2,16},{4,32},{6,48},{8,2},{10,18},{12,34},{14,50},{16,4},{1... | collective-permute-start | bytes 122888 | tf_op jit(solution)/shard_map/ppermute | solution.py:258

commit v9 on v7

--- a/solution.py
+++ b/solution.py
@@ -60,15 +60,18 @@
     )(a)
 
 
-def ladder_kernel(x_ref, b1, b1_far, b3, near, b0, b3_far, far, o_ref, held, sems):
+def ladder_kernel(b1, b1_far, b3, near, x_hbm, b0, b3_far, far, o_ref, x_ref, held, sems):
     me = lax.axis_index("x")
 
     def copies(k):
         part, half = pl.ds(k * 16, 16), pl.ds(k % 2 * 16, 16)
+        span = pl.ds(k * 512, 512)
         found = [(0, b0.at[part])]
         if k >= 2:
             found += [(1, b3_far.at[half]), (2, far.at[half])]
         return [
+            pltpu.make_async_copy(x_hbm.at[:, :, :, span], x_ref.at[:, :, :, span], sems.at[3, k])
+        ] + [
             pltpu.make_async_copy(b, held.at[lax.rem(me + s, 4), part], sems.at[s, k])
             for s, b in found
         ]
@@ -83,10 +86,10 @@
             held[lax.rem(me + 1, 4), part] = b3[half]
             held[lax.rem(me + 2, 4), part] = near[half]
         span = pl.ds(k * 512, 512)
+        for copy in copies(k):
+            copy.wait()
         x = jnp.concatenate([x_ref[:, h, :, span].reshape(128, 512) for h in range(2)], axis=0)
         xh, xl = split(x)
-        for copy in copies(k):
-            copy.wait()
         b = [held[o, k * 16 + c] for c in range(16) for o in range(4)]
         bh, bl = split(jnp.concatenate(b, axis=0))
         total = dot3(xh, xl, bh, bl).reshape(2, 128, 640)
@@ -113,19 +116,23 @@
     )(*args)
 
 
-def ladder(x, *blocks):
+def ladder(*blocks):
     anywhere = pl.BlockSpec(memory_space=pl.ANY)
     return pl.pallas_call(
         ladder_kernel,
-        in_specs=[VMEM] * 5 + [anywhere] * 3,
+        in_specs=[VMEM] * 4 + [anywhere] * 4,
         out_specs=VMEM,
         out_shape=jax.ShapeDtypeStruct((2, 128, 640), F32),
-        scratch_shapes=[pltpu.VMEM((4, 64, 8, 640), F32), pltpu.SemaphoreType.DMA((3, 4))],
+        scratch_shapes=[
+            pltpu.VMEM((16, 2, 8, 2048), F32),
+            pltpu.VMEM((4, 64, 8, 640), F32),
+            pltpu.SemaphoreType.DMA((4, 4)),
+        ],
         compiler_params=pltpu.CompilerParams(vmem_limit_bytes=LADDER_LIMIT),
         cost_estimate=pl.CostEstimate(
             flops=3 * 2 * 256 * 2048 * 640, bytes_accessed=8 * 2**20, transcendentals=0
         ),
-    )(x, *blocks)
+    )(*blocks)
 
 
 def spread_kernel(w_hbm, o_ref, held, sem):
@@ -228,7 +235,7 @@
     parts = cycle(occ_irrep, amplitudes, own, other, vir, pair_irrep[None])
     parts = [parts[0]] + [lax.ppermute(parts[s], "x", ring[s]) for s in (1, 2, 3)]
 
-    part = ladder(x, b1, b1_far, b3, near, ladder_ints, b3_far, far)
+    part = ladder(b1, b1_far, b3, near, x, ladder_ints, b3_far, far)
     part = exchange(part, ("core",))
     both = small(pack_kernel, (64, 2, 896), part, *parts, scratch=[(128, 640), (32, 256)])
     both = exchange(both, ("y", "zl", "zh"))

time: 143 us -> 142 us (level)
  transfers between devices with their start and end apart: 14 -> 14, of which waited for: 8 -> 8; matrix products, arithmetic and copies ran while one was open for 1% -> 1% of each run, Pallas kernels for 10% -> 9%
where the time goes in v9:
time: 142 us; the launch traced here: 141 us
  starting transfers between devices  57.6 us (41%)
  blocking collectives  34.7 us (24%)
  waiting for transfers between devices  29 us (20%)
  Pallas kernels  14.8 us (10%)
  local copies, waits for them, and re-layouts  4.01 us (3%)
    all_to_all x1, blocking collectives, exchange(): return lax.all_to_all(v, axes, split_axis=0, concat_axis=0, tiled=True)  34.7 us
    all_to_all x3, starting transfers between devices, exchange(): return lax.all_to_all(v, axes, split_axis=0, concat_axis=0, tiled=True)  20.4 us
    all_to_all x3, waiting for transfers between devices, exchange(): return lax.all_to_all(v, axes, split_axis=0, concat_axis=0, tiled=True)  12.9 us
    ppermute x3, starting transfers between devices, body(): lax.ppermute(parts[s], 'x', ring[s])  9.43 us
    pallas_call x1, Pallas kernels, ladder(): pl.pallas_call(ladder_kernel, in_specs=[VMEM] * 4 + [anywhere] * 4, out_s...  6.55 us
    ppermute x1, starting transfers between devices, body(): near = lax.ppermute(b1, 'x', ring[1])  5.59 us
    ppermute x1, starting transfers between devices, body(): ladder_resid = lax.ppermute(part, ('zl', 'x', 'zh'), move)  5.34 us
    ppermute x1, starting transfers between devices, body(): b1 = lax.ppermute(lower, 'x', ring[1])  4.75 us
  transfers between devices with their start and end apart: 14, of which 8 were waited for; matrix products, arithmetic and copies ran while one was open for 1% of the time, Pallas kernels for 9%

profile of v9, /device:TPU:6, one launch (start us, length us, event | category | flops | bytes accessed | tf_op | source)
XLA Modules:
  0.0 141.0 jit_solution(17154168961921928751)
XLA Ops:
  0.6 1.7 %shard_map.78 = f32[64,2,8,128]{3,2,1,0:T(8,128)} custom-call(f32[8,4,8,128]{3,2,1,0:T(8,128)} %bitcast.15), custom_call_target="tpu_custom_call" | custom-call | bytes 1048576 | tf_op jit(solution)/shard_map/pallas_call | solution.py:147
  2.3 12.4 %all-to-all-start = ((f32[64,2,8,128]{3,2,1,0:T(8,128)}), f32[64,2,8,128]{3,2,1,0:T(8,128)S(1)}, u32[]{:S(2)}, u32[]{:S(2)}) async-start(f32[64,2,8,128]{3,2,1,0:T(8,128)} %shard_map.78), calls=%async_computation | async-start | bytes 1048576 | tf_op jit(solution)/shard_map/all_to_all | solution.py:214
  14.8 0.0 copy-start
  14.8 1.6 %copy-done = f32[4,4,64,512]{3,2,1,0:T(8,128)S(1)} copy-done((f32[4,4,64,512]{3,2,1,0:T(8,128)S(1)}, f32[4,4,64,512]{3,2,1,0:T(8,128)}, u32[]{:S(2)}) %copy-start) | copy-done | bytes 2097176
  16.4 4.5 %shard_map.77 = f32[16,2,8,2048]{3,2,1,0:T(8,128)} custom-call(f32[4,2,2,64,512]{4,3,2,1,0:T(8,128)S(1)} %bitcast.13), custom_call_target="tpu_custom_call" | custom-call | flops 1048576 | bytes 4194304 | tf_op jit(solution)/shard_map/pallas_call | solution.py:52
  20.9 0.0 copy-start.4
  20.9 11.1 %all-to-all-done.own_ref = f32[64,2,8,128]{3,2,1,0:T(8,128)S(1)} async-done(((f32[64,2,8,128]{3,2,1,0:T(8,128)}), f32[64,2,8,128]{3,2,1,0:T(8,128)S(1)}, u32[]{:S(2)}, u32[]{:S(2)}) %all-to-all-start) | async-done | bytes 524320 | tf_op jit(solution)/shard_map/all_to_all | solution.py:214
  32.0 4.4 %all-to-all-start.1 = ((f32[16,2,8,2048]{3,2,1,0:T(8,128)}), f32[16,2,8,2048]{3,2,1,0:T(8,128)}, u32[]{:S(2)}, u32[]{:S(2)}) async-start(f32[16,2,8,2048]{3,2,1,0:T(8,128)} %shard_map.77), calls=%async_computation.1 | async-start | bytes 4194304 | tf_op jit(solution)/shard_map/all_to_all | solution.py:214
  36.4 0.0 copy-done.4
  36.4 0.0 copy-start.7
  36.4 0.0 copy-start.1
  36.5 0.0 copy-start.2
  36.5 0.0 copy-start.3
  36.5 0.1 fusion
  36.6 2.4 %collective-permute-start.4 = (f32[32,8,640]{2,1,0:T(8,128)S(1)}, f32[32,8,640]{2,1,0:T(8,128)S(1)}, u32[]{:S(2)}, u32[]{:S(2)}) collective-permute-start(f32[32,8,640]{2,1,0:T(8,128)S(1)} %get-tuple-element.12), channel_id=1, source_target_pairs={{0,24},{8,0},{16,8},{24,16},{1,25},{9,1},{17,9},{25,17},{2,26},{10... | collective-permute-start | bytes 1966088 | tf_op jit(solution)/shard_map/ppermute | solution.py:228
  39.0 4.8 %collective-permute-start = (f32[32,8,640]{2,1,0:T(8,128)S(1)}, f32[32,8,640]{2,1,0:T(8,128)S(1)}, u32[]{:S(2)}, u32[]{:S(2)}) collective-permute-start(f32[32,8,640]{2,1,0:T(8,128)S(1)} %get-tuple-element.13), channel_id=1, source_target_pairs={{0,8},{8,16},{16,24},{24,0},{1,9},{9,17},{17,25},{25,1},{2,10},{10... | collective-permute-start | bytes 1966088 | tf_op jit(solution)/shard_map/ppermute | solution.py:227
  43.8 1.9 %collective-permute-start.6 = (f32[64,2,8,128]{3,2,1,0:T(8,128)S(1)}, f32[64,2,8,128]{3,2,1,0:T(8,128)S(1)}, u32[]{:S(2)}, u32[]{:S(2)}) collective-permute-start(f32[64,2,8,128]{3,2,1,0:T(8,128)S(1)} %all-to-all-done.own_ref), channel_id=1, source_target_pairs={{0,1},{1,0},{2,3},{3,2},{4,5},{5,4},{6,7},{7,6},{8,9},{9,8},{10,11... | collective-permute-start | bytes 1572872 | tf_op jit(solution)/shard_map/ppermute | solution.py:225
  45.7 2.0 %collective-permute-start.1 = (f32[32,8,640]{2,1,0:T(8,128)S(1)}, f32[32,8,640]{2,1,0:T(8,128)S(1)}, u32[]{:S(2)}, u32[]{:S(2)}) collective-permute-start(f32[32,8,640]{2,1,0:T(8,128)S(1)} %get-tuple-element.12), channel_id=1, source_target_pairs={{0,8},{8,16},{16,24},{24,0},{1,9},{9,17},{17,25},{25,1},{2,10},{10... | collective-permute-start | bytes 1966088 | tf_op jit(solution)/shard_map/ppermute | solution.py:229
  47.7 3.8 %collective-permute-start.2 = (f32[32,8,640]{2,1,0:T(8,128)S(1)}, f32[32,8,640]{2,1,0:T(8,128)S(1)}, u32[]{:S(2)}, u32[]{:S(2)}) collective-permute-start(f32[32,8,640]{2,1,0:T(8,128)S(1)} %get-tuple-element.13), channel_id=1, source_target_pairs={{0,24},{8,0},{16,8},{24,16},{1,25},{9,1},{17,9},{25,17},{2,26},{10... | collective-permute-start | bytes 1966088 | tf_op jit(solution)/shard_map/ppermute | solution.py:230
  51.6 2.2 %collective-permute-done.4.b3_far = f32[32,8,640]{2,1,0:T(8,128)S(1)} collective-permute-done((f32[32,8,640]{2,1,0:T(8,128)S(1)}, f32[32,8,640]{2,1,0:T(8,128)S(1)}, u32[]{:S(2)}, u32[]{:S(2)}) %collective-permute-start.4) | collective-permute-done | bytes 655392 | tf_op jit(solution)/shard_map/ppermute | solution.py:228
  53.8 0.0 copy-start.5
  53.8 1.9 %collective-permute-start.5 = (f32[32,8,640]{2,1,0:T(8,128)S(1)}, f32[32,8,640]{2,1,0:T(8,128)S(1)}, u32[]{:S(2)}, u32[]{:S(2)}) collective-permute-start(f32[32,8,640]{2,1,0:T(8,128)S(1)} %collective-permute-done.4.b3_far), channel_id=1, source_target_pairs={{0,24},{8,0},{16,8},{24,16},{1,25},{9,1},{17,9},{25,17},{2,26},{10... | collective-permute-start | bytes 1966088 | tf_op jit(solution)/shard_map/ppermute | solution.py:232
  55.7 3.2 %collective-permute-done.b1 = f32[32,8,640]{2,1,0:T(8,128)S(1)} collective-permute-done((f32[32,8,640]{2,1,0:T(8,128)S(1)}, f32[32,8,640]{2,1,0:T(8,128)S(1)}, u32[]{:S(2)}, u32[]{:S(2)}) %collective-permute-start) | collective-permute-done | bytes 655392 | tf_op jit(solution)/shard_map/ppermute | solution.py:227
  58.9 5.6 %collective-permute-start.3 = (f32[32,8,640]{2,1,0:T(8,128)S(1)}, f32[32,8,640]{2,1,0:T(8,128)}, u32[]{:S(2)}, u32[]{:S(2)}) collective-permute-start(f32[32,8,640]{2,1,0:T(8,128)S(1)} %collective-permute-done.b1), channel_id=1, source_target_pairs={{0,8},{8,16},{16,24},{24,0},{1,9},{9,17},{17,25},{25,1},{2,10},{10... | collective-permute-start | bytes 1966088 | tf_op jit(solution)/shard_map/ppermute | solution.py:231
  64.5 0.0 collective-permute-done.6.other_ref
  64.6 0.0 copy-done.7
  64.6 0.1 broadcast_in_dim.4.vir_ref
  64.7 0.0 copy-done.1
  64.7 0.0 copy-done.2
  64.7 0.0 copy-done.3
  64.7 1.8 %shard_map.80 = f32[4,32,256]{2,1,0:T(8,128)S(1)} custom-call(s32[32]{0:T(128)S(1)} %copy-done.2, f32[4,4,64,512]{3,2,1,0:T(8,128)S(1)} %copy-done.1, f32[64,2,8,128]{3,2,1,0:T(8,128)S(1)} %all-to-all-done.own_ref, f32[64,2,8,128]{3,2,1,0:T(8,128)S(1)} %collective-permute-done.6.other_ref, s32[512,128]{1,0:T(8,128)S(1)} %broadcast_in_dim.4.vir_ref, ...), custom_call_target="tpu_custom_call" | custom-call | flops 402653184 | bytes 3145728 | tf_op jit(solution)/shard_map/pallas_call | solution.py:200
  66.5 1.9 %collective-permute-start.9 = (f32[32,256]{1,0:T(8,128)S(1)}, f32[32,256]{1,0:T(8,128)S(1)}, u32[]{:S(2)}, u32[]{:S(2)}) collective-permute-start(f32[32,256]{1,0:T(8,128)S(1)} %get-tuple-element.14), channel_id=1, source_target_pairs={{0,24},{8,0},{16,8},{24,16},{1,25},{9,1},{17,9},{25,17},{2,26},{10... | collective-permute-start | bytes 98312 | tf_op jit(solution)/shard_map/ppermute | solution.py:236
  68.5 4.5 %collective-permute-done.1.b1_far = f32[32,8,640]{2,1,0:T(8,128)S(1)} collective-permute-done((f32[32,8,640]{2,1,0:T(8,128)S(1)}, f32[32,8,640]{2,1,0:T(8,128)S(1)}, u32[]{:S(2)}, u32[]{:S(2)}) %collective-permute-start.1) | collective-permute-done | bytes 655392 | tf_op jit(solution)/shard_map/ppermute | solution.py:229
  73.0 3.9 %collective-permute-start.8 = (f32[32,256]{1,0:T(8,128)S(1)}, f32[32,256]{1,0:T(8,128)S(1)}, u32[]{:S(2)}, u32[]{:S(2)}) collective-permute-start(f32[32,256]{1,0:T(8,128)S(1)} %get-tuple-element.15), channel_id=1, source_target_pairs={{0,16},{8,24},{16,0},{24,8},{1,17},{9,25},{17,1},{25,9},{2,18},{10... | collective-permute-start | bytes 98312 | tf_op jit(solution)/shard_map/ppermute | solution.py:236
  76.9 0.0 collective-permute-done.2.b3
  76.9 3.6 %collective-permute-start.7 = (f32[32,256]{1,0:T(8,128)S(1)}, f32[32,256]{1,0:T(8,128)S(1)}, u32[]{:S(2)}, u32[]{:S(2)}) collective-permute-start(f32[32,256]{1,0:T(8,128)S(1)} %get-tuple-element.16), channel_id=1, source_target_pairs={{0,8},{8,16},{16,24},{24,0},{1,9},{9,17},{17,25},{25,1},{2,10},{10... | collective-permute-start | bytes 98312 | tf_op jit(solution)/shard_map/ppermute | solution.py:236
  80.5 2.1 %collective-permute-done.5.far = f32[32,8,640]{2,1,0:T(8,128)S(1)} collective-permute-done((f32[32,8,640]{2,1,0:T(8,128)S(1)}, f32[32,8,640]{2,1,0:T(8,128)S(1)}, u32[]{:S(2)}, u32[]{:S(2)}) %collective-permute-start.5) | collective-permute-done | bytes 655392 | tf_op jit(solution)/shard_map/ppermute | solution.py:232
  82.6 0.0 copy-start.6
  82.6 0.9 copy-done.6
  83.5 0.6 collective-permute-done.3.near
  84.1 0.0 all-to-all-done.1.x_hbm
  84.1 0.0 copy-done.5
  84.1 6.5 %shard_map.79 = f32[2,128,640]{2,1,0:T(8,128)} custom-call(f32[32,8,640]{2,1,0:T(8,128)S(1)} %collective-permute-done.b1, f32[32,8,640]{2,1,0:T(8,128)S(1)} %collective-permute-done.1.b1_far, f32[32,8,640]{2,1,0:T(8,128)S(1)} %collective-permute-done.2.b3, f32[32,8,640]{2,1,0:T(8,128)} %collective-permute-done.3.near, ...), custom_call_target="tpu_custom_call" | custom-call | flops 2013265920 | bytes 8388608 | tf_op jit(solution)/shard_map/pallas_call | solution.py:121
  90.7 3.5 %all-to-all-start.2 = ((f32[2,128,640]{2,1,0:T(8,128)}), f32[2,128,640]{2,1,0:T(8,128)S(1)}, u32[]{:S(2)}, u32[]{:S(2)}) async-start(f32[2,128,640]{2,1,0:T(8,128)} %shard_map.79), calls=%async_computation.2 | async-start | bytes 1310720 | tf_op jit(solution)/shard_map/all_to_all | solution.py:214
  94.2 0.0 collective-permute-done.9.c3
  94.2 0.0 collective-permute-done.8.c2
  94.2 0.0 collective-permute-done.7.c1
  94.3 1.8 %all-to-all-done.2.part_ref = f32[2,128,640]{2,1,0:T(8,128)S(1)} async-done(((f32[2,128,640]{2,1,0:T(8,128)}), f32[2,128,640]{2,1,0:T(8,128)S(1)}, u32[]{:S(2)}, u32[]{:S(2)}) %all-to-all-start.2) | async-done | bytes 655392 | tf_op jit(solution)/shard_map/all_to_all | solution.py:214
  96.0 0.2 shard_map.81
  96.2 34.7 %all_to_all.20.p_ref = f32[64,2,896]{2,1,0:T(2,128)S(1)} all-to-all(f32[64,2,896]{2,1,0:T(2,128)S(1)} %shard_map.81), channel_id=1, replica_groups=mesh['y'=8,'zl'=2,'x'=4,'zh'=4,'core'=2] {'y','zl','zh'}, dimensions={0} | all-to-all | bytes 917504 | tf_op jit(solution)/shard_map/all_to_all | solution.py:214
  131.0 5.3 %collective-permute-start.10 = (f32[2,640]{1,0:T(2,128)S(1)}, f32[2,640]{1,0:T(2,128)S(1)}, u32[]{:S(2)}, u32[]{:S(2)}) collective-permute-start(f32[2,640]{1,0:T(2,128)S(1)} %get-tuple-element.10), channel_id=1, source_target_pairs={{0,0},{2,16},{4,32},{6,48},{8,2},{10,18},{12,34},{14,50},{16,4},{1... | collective-permute-start | bytes 15368 | tf_op jit(solution)/shard_map/ppermute | solution.py:251
  136.3 0.1 reshape.19
  136.4 0.6 copy.8
  137.1 3.3 %collective-permute-done.10 = f32[2,640]{1,0:T(2,128)S(1)} collective-permute-done((f32[2,640]{1,0:T(2,128)S(1)}, f32[2,640]{1,0:T(2,128)S(1)}, u32[]{:S(2)}, u32[]{:S(2)}) %collective-permute-start.10) | collective-permute-done | bytes 5152 | tf_op jit(solution)/shard_map/ppermute | solution.py:251
  140.4 0.6 copy.10
  (2 shorter events, 0.0 us)
Async XLA Ops:
  2.3 29.6 %all-to-all-start = ((f32[64,2,8,128]{3,2,1,0:T(8,128)}), f32[64,2,8,128]{3,2,1,0:T(8,128)S(1)}, u32[]{:S(2)}, u32[]{:S(2)}) async-start(f32[64,2,8,128]{3,2,1,0:T(8,128)} %shard_map.78), calls=%async_computation | async-start | bytes 1048576 | tf_op jit(solution)/shard_map/all_to_all | solution.py:214
  14.8 1.6 %copy-start = (f32[4,4,64,512]{3,2,1,0:T(8,128)S(1)}, f32[4,4,64,512]{3,2,1,0:T(8,128)}, u32[]{:S(2)}) copy-start(f32[4,4,64,512]{3,2,1,0:T(8,128)} %a_ref.1) | copy-start | bytes 6291460
  20.9 15.5 %copy-start.4 = (f32[64,8,640]{2,1,0:T(8,128)S(1)}, f32[64,8,640]{2,1,0:T(8,128)}, u32[]{:S(2)}) copy-start(f32[64,8,640]{2,1,0:T(8,128)} %b0) | copy-start | bytes 3932164
  32.0 52.2 %all-to-all-start.1 = ((f32[16,2,8,2048]{3,2,1,0:T(8,128)}), f32[16,2,8,2048]{3,2,1,0:T(8,128)}, u32[]{:S(2)}, u32[]{:S(2)}) async-start(f32[16,2,8,2048]{3,2,1,0:T(8,128)} %shard_map.77), calls=%async_computation.1 | async-start | bytes 4194304 | tf_op jit(solution)/shard_map/all_to_all | solution.py:214
  36.4 28.1 %copy-start.7 = (s32[512]{0:T(512)S(1)}, s32[512]{0:T(512)}, u32[]{:S(2)}) copy-start(s32[512]{0:T(512)} %param.10) | copy-start | bytes 6148
  36.4 28.3 %copy-start.1 = (f32[4,4,64,512]{3,2,1,0:T(8,128)S(1)}, f32[4,4,64,512]{3,2,1,0:T(8,128)}, u32[]{:S(2)}) copy-start(f32[4,4,64,512]{3,2,1,0:T(8,128)} %a_ref.1) | copy-start | bytes 6291460
  36.5 28.2 %copy-start.2 = (s32[32]{0:T(128)S(1)}, s32[32]{0:T(128)}, u32[]{:S(2)}) copy-start(s32[32]{0:T(128)} %occ_ref.1) | copy-start | bytes 388
  36.5 28.2 %copy-start.3 = (s32[128]{0:T(128)S(1)}, s32[128]{0:T(128)}, u32[]{:S(2)}) copy-start(s32[128]{0:T(128)} %param.11) | copy-start | bytes 1540
  36.6 17.2 %collective-permute-start.4 = (f32[32,8,640]{2,1,0:T(8,128)S(1)}, f32[32,8,640]{2,1,0:T(8,128)S(1)}, u32[]{:S(2)}, u32[]{:S(2)}) collective-permute-start(f32[32,8,640]{2,1,0:T(8,128)S(1)} %get-tuple-element.12), channel_id=1, source_target_pairs={{0,24},{8,0},{16,8},{24,16},{1,25},{9,1},{17,9},{25,17},{2,26},{10... | collective-permute-start | bytes 1966088 | tf_op jit(solution)/shard_map/ppermute | solution.py:228
  39.0 19.9 %collective-permute-start = (f32[32,8,640]{2,1,0:T(8,128)S(1)}, f32[32,8,640]{2,1,0:T(8,128)S(1)}, u32[]{:S(2)}, u32[]{:S(2)}) collective-permute-start(f32[32,8,640]{2,1,0:T(8,128)S(1)} %get-tuple-element.13), channel_id=1, source_target_pairs={{0,8},{8,16},{16,24},{24,0},{1,9},{9,17},{17,25},{25,1},{2,10},{10... | collective-permute-start | bytes 1966088 | tf_op jit(solution)/shard_map/ppermute | solution.py:227
  43.8 20.8 %collective-permute-start.6 = (f32[64,2,8,128]{3,2,1,0:T(8,128)S(1)}, f32[64,2,8,128]{3,2,1,0:T(8,128)S(1)}, u32[]{:S(2)}, u32[]{:S(2)}) collective-permute-start(f32[64,2,8,128]{3,2,1,0:T(8,128)S(1)} %all-to-all-done.own_ref), channel_id=1, source_target_pairs={{0,1},{1,0},{2,3},{3,2},{4,5},{5,4},{6,7},{7,6},{8,9},{9,8},{10,11... | collective-permute-start | bytes 1572872 | tf_op jit(solution)/shard_map/ppermute | solution.py:225
  45.7 27.3 %collective-permute-start.1 = (f32[32,8,640]{2,1,0:T(8,128)S(1)}, f32[32,8,640]{2,1,0:T(8,128)S(1)}, u32[]{:S(2)}, u32[]{:S(2)}) collective-permute-start(f32[32,8,640]{2,1,0:T(8,128)S(1)} %get-tuple-element.12), channel_id=1, source_target_pairs={{0,8},{8,16},{16,24},{24,0},{1,9},{9,17},{17,25},{25,1},{2,10},{10... | collective-permute-start | bytes 1966088 | tf_op jit(solution)/shard_map/ppermute | solution.py:229
  47.7 29.2 %collective-permute-start.2 = (f32[32,8,640]{2,1,0:T(8,128)S(1)}, f32[32,8,640]{2,1,0:T(8,128)S(1)}, u32[]{:S(2)}, u32[]{:S(2)}) collective-permute-start(f32[32,8,640]{2,1,0:T(8,128)S(1)} %get-tuple-element.13), channel_id=1, source_target_pairs={{0,24},{8,0},{16,8},{24,16},{1,25},{9,1},{17,9},{25,17},{2,26},{10... | collective-permute-start | bytes 1966088 | tf_op jit(solution)/shard_map/ppermute | solution.py:230
  53.8 30.4 %copy-start.5 = (f32[32,8,640]{2,1,0:T(8,128)}, f32[32,8,640]{2,1,0:T(8,128)S(1)}, u32[]{:S(2)}) copy-start(f32[32,8,640]{2,1,0:T(8,128)S(1)} %collective-permute-done.4.b3_far) | copy-start | bytes 1966084
  53.8 28.9 %collective-permute-start.5 = (f32[32,8,640]{2,1,0:T(8,128)S(1)}, f32[32,8,640]{2,1,0:T(8,128)S(1)}, u32[]{:S(2)}, u32[]{:S(2)}) collective-permute-start(f32[32,8,640]{2,1,0:T(8,128)S(1)} %collective-permute-done.4.b3_far), channel_id=1, source_target_pairs={{0,24},{8,0},{16,8},{24,16},{1,25},{9,1},{17,9},{25,17},{2,26},{10... | collective-permute-start | bytes 1966088 | tf_op jit(solution)/shard_map/ppermute | solution.py:232
  58.9 25.2 %collective-permute-start.3 = (f32[32,8,640]{2,1,0:T(8,128)S(1)}, f32[32,8,640]{2,1,0:T(8,128)}, u32[]{:S(2)}, u32[]{:S(2)}) collective-permute-start(f32[32,8,640]{2,1,0:T(8,128)S(1)} %collective-permute-done.b1), channel_id=1, source_target_pairs={{0,8},{8,16},{16,24},{24,0},{1,9},{9,17},{17,25},{25,1},{2,10},{10... | collective-permute-start | bytes 1966088 | tf_op jit(solution)/shard_map/ppermute | solution.py:231
  66.5 27.7 %collective-permute-start.9 = (f32[32,256]{1,0:T(8,128)S(1)}, f32[32,256]{1,0:T(8,128)S(1)}, u32[]{:S(2)}, u32[]{:S(2)}) collective-permute-start(f32[32,256]{1,0:T(8,128)S(1)} %get-tuple-element.14), channel_id=1, source_target_pairs={{0,24},{8,0},{16,8},{24,16},{1,25},{9,1},{17,9},{25,17},{2,26},{10... | collective-permute-start | bytes 98312 | tf_op jit(solution)/shard_map/ppermute | solution.py:236
  73.0 21.2 %collective-permute-start.8 = (f32[32,256]{1,0:T(8,128)S(1)}, f32[32,256]{1,0:T(8,128)S(1)}, u32[]{:S(2)}, u32[]{:S(2)}) collective-permute-start(f32[32,256]{1,0:T(8,128)S(1)} %get-tuple-element.15), channel_id=1, source_target_pairs={{0,16},{8,24},{16,0},{24,8},{1,17},{9,25},{17,1},{25,9},{2,18},{10... | collective-permute-start | bytes 98312 | tf_op jit(solution)/shard_map/ppermute | solution.py:236
  76.9 17.3 %collective-permute-start.7 = (f32[32,256]{1,0:T(8,128)S(1)}, f32[32,256]{1,0:T(8,128)S(1)}, u32[]{:S(2)}, u32[]{:S(2)}) collective-permute-start(f32[32,256]{1,0:T(8,128)S(1)} %get-tuple-element.16), channel_id=1, source_target_pairs={{0,8},{8,16},{16,24},{24,0},{1,9},{9,17},{17,25},{25,1},{2,10},{10... | collective-permute-start | bytes 98312 | tf_op jit(solution)/shard_map/ppermute | solution.py:236
  82.6 0.9 copy-start.6
  90.7 5.4 %all-to-all-start.2 = ((f32[2,128,640]{2,1,0:T(8,128)}), f32[2,128,640]{2,1,0:T(8,128)S(1)}, u32[]{:S(2)}, u32[]{:S(2)}) async-start(f32[2,128,640]{2,1,0:T(8,128)} %shard_map.79), calls=%async_computation.2 | async-start | bytes 1310720 | tf_op jit(solution)/shard_map/all_to_all | solution.py:214
  131.0 9.4 %collective-permute-start.10 = (f32[2,640]{1,0:T(2,128)S(1)}, f32[2,640]{1,0:T(2,128)S(1)}, u32[]{:S(2)}, u32[]{:S(2)}) collective-permute-start(f32[2,640]{1,0:T(2,128)S(1)} %get-tuple-element.10), channel_id=1, source_target_pairs={{0,0},{2,16},{4,32},{6,48},{8,2},{10,18},{12,34},{14,50},{16,4},{1... | collective-permute-start | bytes 15368 | tf_op jit(solution)/shard_map/ppermute | solution.py:251

commit v10 on v9

--- a/solution.py
+++ b/solution.py
@@ -62,12 +62,12 @@
 
 def ladder_kernel(b1, b1_far, b3, near, x_hbm, b0, b3_far, far, o_ref, x_ref, held, sems):
     me = lax.axis_index("x")
-
-    def copies(k):
-        part, half = pl.ds(k * 16, 16), pl.ds(k % 2 * 16, 16)
-        span = pl.ds(k * 512, 512)
+    pieces = ((0, 8), (8, 8), (16, 16), (32, 16), (48, 16))
+
+    def copies(k, c, size):
+        part, half, span = pl.ds(c, size), pl.ds(c % 32, size), pl.ds(c * 32, size * 32)
         found = [(0, b0.at[part])]
-        if k >= 2:
+        if c >= 32:
             found += [(1, b3_far.at[half]), (2, far.at[half])]
         return [
             pltpu.make_async_copy(x_hbm.at[:, :, :, span], x_ref.at[:, :, :, span], sems.at[3, k])
@@ -76,21 +76,20 @@
             for s, b in found
         ]
 
-    for k in range(4):
-        for copy in copies(k):
+    for k, (c, size) in enumerate(pieces):
+        for copy in copies(k, c, size):
             copy.start()
-    for k in range(4):
-        part, half = pl.ds(k * 16, 16), pl.ds(k % 2 * 16, 16)
-        held[lax.rem(me + 3, 4), part] = (b1 if k < 2 else b1_far)[half]
-        if k < 2:
+    for k, (c, size) in enumerate(pieces):
+        part, half, span = pl.ds(c, size), pl.ds(c % 32, size), pl.ds(c * 32, size * 32)
+        held[lax.rem(me + 3, 4), part] = (b1 if c < 32 else b1_far)[half]
+        if c < 32:
             held[lax.rem(me + 1, 4), part] = b3[half]
             held[lax.rem(me + 2, 4), part] = near[half]
-        span = pl.ds(k * 512, 512)
-        for copy in copies(k):
+        for copy in copies(k, c, size):
             copy.wait()
-        x = jnp.concatenate([x_ref[:, h, :, span].reshape(128, 512) for h in range(2)], axis=0)
-        xh, xl = split(x)
-        b = [held[o, k * 16 + c] for c in range(16) for o in range(4)]
+        rows = [x_ref[:, h, :, span].reshape(128, size * 32) for h in range(2)]
+        xh, xl = split(jnp.concatenate(rows, axis=0))
+        b = [held[o, c + d] for d in range(size) for o in range(4)]
         bh, bl = split(jnp.concatenate(b, axis=0))
         total = dot3(xh, xl, bh, bl).reshape(2, 128, 640)
         if k == 0:
@@ -126,7 +125,7 @@
         scratch_shapes=[
             pltpu.VMEM((16, 2, 8, 2048), F32),
             pltpu.VMEM((4, 64, 8, 640), F32),
-            pltpu.SemaphoreType.DMA((4, 4)),
+            pltpu.SemaphoreType.DMA((4, 5)),
         ],
         compiler_params=pltpu.CompilerParams(vmem_limit_bytes=LADDER_LIMIT),
         cost_estimate=pl.CostEstimate(

time: 142 us -> 142 us (level)
  no operation moved by 1% of the time
where the time goes in v10:
time: 142 us; the launch traced here: 141 us
  starting transfers between devices  57.6 us (41%)
  blocking collectives  34.8 us (25%)
  waiting for transfers between devices  29 us (20%)
  Pallas kernels  14.9 us (10%)
  local copies, waits for them, and re-layouts  4.01 us (3%)
    all_to_all x1, blocking collectives, exchange(): return lax.all_to_all(v, axes, split_axis=0, concat_axis=0, tiled=True)  34.8 us
    all_to_all x3, starting transfers between devices, exchange(): return lax.all_to_all(v, axes, split_axis=0, concat_axis=0, tiled=True)  20.4 us
    all_to_all x3, waiting for transfers between devices, exchange(): return lax.all_to_all(v, axes, split_axis=0, concat_axis=0, tiled=True)  12.9 us
    ppermute x3, starting transfers between devices, body(): lax.ppermute(parts[s], 'x', ring[s])  9.43 us
    pallas_call x1, Pallas kernels, ladder(): pl.pallas_call(ladder_kernel, in_specs=[VMEM] * 4 + [anywhere] * 4, out_s...  6.71 us
    ppermute x1, starting transfers between devices, body(): near = lax.ppermute(b1, 'x', ring[1])  5.59 us
    ppermute x1, starting transfers between devices, body(): ladder_resid = lax.ppermute(part, ('zl', 'x', 'zh'), move)  5.34 us
    ppermute x1, starting transfers between devices, body(): b1 = lax.ppermute(lower, 'x', ring[1])  4.75 us
  transfers between devices with their start and end apart: 14, of which 8 were waited for; matrix products, arithmetic and copies ran while one was open for 1% of the time, Pallas kernels for 9%

profile of v10, /device:TPU:6, one launch (start us, length us, event | category | flops | bytes accessed | tf_op | source)
XLA Modules:
  0.0 141.2 jit_solution(17547656811308436485)
XLA Ops:
  0.6 1.7 %shard_map.78 = f32[64,2,8,128]{3,2,1,0:T(8,128)} custom-call(f32[8,4,8,128]{3,2,1,0:T(8,128)} %bitcast.15), custom_call_target="tpu_custom_call" | custom-call | bytes 1048576 | tf_op jit(solution)/shard_map/pallas_call | solution.py:146
  2.3 12.4 %all-to-all-start = ((f32[64,2,8,128]{3,2,1,0:T(8,128)}), f32[64,2,8,128]{3,2,1,0:T(8,128)S(1)}, u32[]{:S(2)}, u32[]{:S(2)}) async-start(f32[64,2,8,128]{3,2,1,0:T(8,128)} %shard_map.78), calls=%async_computation | async-start | bytes 1048576 | tf_op jit(solution)/shard_map/all_to_all | solution.py:213
  14.8 0.0 copy-start
  14.8 1.6 %copy-done = f32[4,4,64,512]{3,2,1,0:T(8,128)S(1)} copy-done((f32[4,4,64,512]{3,2,1,0:T(8,128)S(1)}, f32[4,4,64,512]{3,2,1,0:T(8,128)}, u32[]{:S(2)}) %copy-start) | copy-done | bytes 2097176
  16.4 4.5 %shard_map.77 = f32[16,2,8,2048]{3,2,1,0:T(8,128)} custom-call(f32[4,2,2,64,512]{4,3,2,1,0:T(8,128)S(1)} %bitcast.13), custom_call_target="tpu_custom_call" | custom-call | flops 1048576 | bytes 4194304 | tf_op jit(solution)/shard_map/pallas_call | solution.py:52
  20.9 0.0 copy-start.4
  20.9 11.1 %all-to-all-done.own_ref = f32[64,2,8,128]{3,2,1,0:T(8,128)S(1)} async-done(((f32[64,2,8,128]{3,2,1,0:T(8,128)}), f32[64,2,8,128]{3,2,1,0:T(8,128)S(1)}, u32[]{:S(2)}, u32[]{:S(2)}) %all-to-all-start) | async-done | bytes 524320 | tf_op jit(solution)/shard_map/all_to_all | solution.py:213
  32.0 4.4 %all-to-all-start.1 = ((f32[16,2,8,2048]{3,2,1,0:T(8,128)}), f32[16,2,8,2048]{3,2,1,0:T(8,128)}, u32[]{:S(2)}, u32[]{:S(2)}) async-start(f32[16,2,8,2048]{3,2,1,0:T(8,128)} %shard_map.77), calls=%async_computation.1 | async-start | bytes 4194304 | tf_op jit(solution)/shard_map/all_to_all | solution.py:213
  36.4 0.0 copy-done.4
  36.4 0.0 copy-start.7
  36.4 0.0 copy-start.1
  36.5 0.0 copy-start.2
  36.5 0.0 copy-start.3
  36.5 0.1 fusion
  36.6 2.4 %collective-permute-start.4 = (f32[32,8,640]{2,1,0:T(8,128)S(1)}, f32[32,8,640]{2,1,0:T(8,128)S(1)}, u32[]{:S(2)}, u32[]{:S(2)}) collective-permute-start(f32[32,8,640]{2,1,0:T(8,128)S(1)} %get-tuple-element.12), channel_id=1, source_target_pairs={{0,24},{8,0},{16,8},{24,16},{1,25},{9,1},{17,9},{25,17},{2,26},{10... | collective-permute-start | bytes 1966088 | tf_op jit(solution)/shard_map/ppermute | solution.py:227
  39.0 4.8 %collective-permute-start = (f32[32,8,640]{2,1,0:T(8,128)S(1)}, f32[32,8,640]{2,1,0:T(8,128)S(1)}, u32[]{:S(2)}, u32[]{:S(2)}) collective-permute-start(f32[32,8,640]{2,1,0:T(8,128)S(1)} %get-tuple-element.13), channel_id=1, source_target_pairs={{0,8},{8,16},{16,24},{24,0},{1,9},{9,17},{17,25},{25,1},{2,10},{10... | collective-permute-start | bytes 1966088 | tf_op jit(solution)/shard_map/ppermute | solution.py:226
  43.8 1.9 %collective-permute-start.6 = (f32[64,2,8,128]{3,2,1,0:T(8,128)S(1)}, f32[64,2,8,128]{3,2,1,0:T(8,128)S(1)}, u32[]{:S(2)}, u32[]{:S(2)}) collective-permute-start(f32[64,2,8,128]{3,2,1,0:T(8,128)S(1)} %all-to-all-done.own_ref), channel_id=1, source_target_pairs={{0,1},{1,0},{2,3},{3,2},{4,5},{5,4},{6,7},{7,6},{8,9},{9,8},{10,11... | collective-permute-start | bytes 1572872 | tf_op jit(solution)/shard_map/ppermute | solution.py:224
  45.7 2.0 %collective-permute-start.1 = (f32[32,8,640]{2,1,0:T(8,128)S(1)}, f32[32,8,640]{2,1,0:T(8,128)S(1)}, u32[]{:S(2)}, u32[]{:S(2)}) collective-permute-start(f32[32,8,640]{2,1,0:T(8,128)S(1)} %get-tuple-element.12), channel_id=1, source_target_pairs={{0,8},{8,16},{16,24},{24,0},{1,9},{9,17},{17,25},{25,1},{2,10},{10... | collective-permute-start | bytes 1966088 | tf_op jit(solution)/shard_map/ppermute | solution.py:228
  47.7 3.8 %collective-permute-start.2 = (f32[32,8,640]{2,1,0:T(8,128)S(1)}, f32[32,8,640]{2,1,0:T(8,128)S(1)}, u32[]{:S(2)}, u32[]{:S(2)}) collective-permute-start(f32[32,8,640]{2,1,0:T(8,128)S(1)} %get-tuple-element.13), channel_id=1, source_target_pairs={{0,24},{8,0},{16,8},{24,16},{1,25},{9,1},{17,9},{25,17},{2,26},{10... | collective-permute-start | bytes 1966088 | tf_op jit(solution)/shard_map/ppermute | solution.py:229
  51.6 2.2 %collective-permute-done.4.b3_far = f32[32,8,640]{2,1,0:T(8,128)S(1)} collective-permute-done((f32[32,8,640]{2,1,0:T(8,128)S(1)}, f32[32,8,640]{2,1,0:T(8,128)S(1)}, u32[]{:S(2)}, u32[]{:S(2)}) %collective-permute-start.4) | collective-permute-done | bytes 655392 | tf_op jit(solution)/shard_map/ppermute | solution.py:227
  53.8 0.0 copy-start.5
  53.8 1.9 %collective-permute-start.5 = (f32[32,8,640]{2,1,0:T(8,128)S(1)}, f32[32,8,640]{2,1,0:T(8,128)S(1)}, u32[]{:S(2)}, u32[]{:S(2)}) collective-permute-start(f32[32,8,640]{2,1,0:T(8,128)S(1)} %collective-permute-done.4.b3_far), channel_id=1, source_target_pairs={{0,24},{8,0},{16,8},{24,16},{1,25},{9,1},{17,9},{25,17},{2,26},{10... | collective-permute-start | bytes 1966088 | tf_op jit(solution)/shard_map/ppermute | solution.py:231
  55.7 3.2 %collective-permute-done.b1 = f32[32,8,640]{2,1,0:T(8,128)S(1)} collective-permute-done((f32[32,8,640]{2,1,0:T(8,128)S(1)}, f32[32,8,640]{2,1,0:T(8,128)S(1)}, u32[]{:S(2)}, u32[]{:S(2)}) %collective-permute-start) | collective-permute-done | bytes 655392 | tf_op jit(solution)/shard_map/ppermute | solution.py:226
  58.9 5.6 %collective-permute-start.3 = (f32[32,8,640]{2,1,0:T(8,128)S(1)}, f32[32,8,640]{2,1,0:T(8,128)}, u32[]{:S(2)}, u32[]{:S(2)}) collective-permute-start(f32[32,8,640]{2,1,0:T(8,128)S(1)} %collective-permute-done.b1), channel_id=1, source_target_pairs={{0,8},{8,16},{16,24},{24,0},{1,9},{9,17},{17,25},{25,1},{2,10},{10... | collective-permute-start | bytes 1966088 | tf_op jit(solution)/shard_map/ppermute | solution.py:230
  64.5 0.0 collective-permute-done.6.other_ref
  64.6 0.0 copy-done.7
  64.6 0.1 broadcast_in_dim.4.vir_ref
  64.7 0.0 copy-done.1
  64.7 0.0 copy-done.2
  64.7 0.0 copy-done.3
  64.7 1.8 %shard_map.80 = f32[4,32,256]{2,1,0:T(8,128)S(1)} custom-call(s32[32]{0:T(128)S(1)} %copy-done.2, f32[4,4,64,512]{3,2,1,0:T(8,128)S(1)} %copy-done.1, f32[64,2,8,128]{3,2,1,0:T(8,128)S(1)} %all-to-all-done.own_ref, f32[64,2,8,128]{3,2,1,0:T(8,128)S(1)} %collective-permute-done.6.other_ref, s32[512,128]{1,0:T(8,128)S(1)} %broadcast_in_dim.4.vir_ref, ...), custom_call_target="tpu_custom_call" | custom-call | flops 402653184 | bytes 3145728 | tf_op jit(solution)/shard_map/pallas_call | solution.py:199
  66.5 1.9 %collective-permute-start.9 = (f32[32,256]{1,0:T(8,128)S(1)}, f32[32,256]{1,0:T(8,128)S(1)}, u32[]{:S(2)}, u32[]{:S(2)}) collective-permute-start(f32[32,256]{1,0:T(8,128)S(1)} %get-tuple-element.14), channel_id=1, source_target_pairs={{0,24},{8,0},{16,8},{24,16},{1,25},{9,1},{17,9},{25,17},{2,26},{10... | collective-permute-start | bytes 98312 | tf_op jit(solution)/shard_map/ppermute | solution.py:235
  68.5 4.5 %collective-permute-done.1.b1_far = f32[32,8,640]{2,1,0:T(8,128)S(1)} collective-permute-done((f32[32,8,640]{2,1,0:T(8,128)S(1)}, f32[32,8,640]{2,1,0:T(8,128)S(1)}, u32[]{:S(2)}, u32[]{:S(2)}) %collective-permute-start.1) | collective-permute-done | bytes 655392 | tf_op jit(solution)/shard_map/ppermute | solution.py:228
  73.0 3.9 %collective-permute-start.8 = (f32[32,256]{1,0:T(8,128)S(1)}, f32[32,256]{1,0:T(8,128)S(1)}, u32[]{:S(2)}, u32[]{:S(2)}) collective-permute-start(f32[32,256]{1,0:T(8,128)S(1)} %get-tuple-element.15), channel_id=1, source_target_pairs={{0,16},{8,24},{16,0},{24,8},{1,17},{9,25},{17,1},{25,9},{2,18},{10... | collective-permute-start | bytes 98312 | tf_op jit(solution)/shard_map/ppermute | solution.py:235
  76.9 0.0 collective-permute-done.2.b3
  76.9 3.6 %collective-permute-start.7 = (f32[32,256]{1,0:T(8,128)S(1)}, f32[32,256]{1,0:T(8,128)S(1)}, u32[]{:S(2)}, u32[]{:S(2)}) collective-permute-start(f32[32,256]{1,0:T(8,128)S(1)} %get-tuple-element.16), channel_id=1, source_target_pairs={{0,8},{8,16},{16,24},{24,0},{1,9},{9,17},{17,25},{25,1},{2,10},{10... | collective-permute-start | bytes 98312 | tf_op jit(solution)/shard_map/ppermute | solution.py:235
  80.5 2.1 %collective-permute-done.5.far = f32[32,8,640]{2,1,0:T(8,128)S(1)} collective-permute-done((f32[32,8,640]{2,1,0:T(8,128)S(1)}, f32[32,8,640]{2,1,0:T(8,128)S(1)}, u32[]{:S(2)}, u32[]{:S(2)}) %collective-permute-start.5) | collective-permute-done | bytes 655392 | tf_op jit(solution)/shard_map/ppermute | solution.py:231
  82.6 0.0 copy-start.6
  82.6 0.9 copy-done.6
  83.5 0.6 collective-permute-done.3.near
  84.1 0.0 all-to-all-done.1.x_hbm
  84.1 0.0 copy-done.5
  84.1 6.7 %shard_map.79 = f32[2,128,640]{2,1,0:T(8,128)} custom-call(f32[32,8,640]{2,1,0:T(8,128)S(1)} %collective-permute-done.b1, f32[32,8,640]{2,1,0:T(8,128)S(1)} %collective-permute-done.1.b1_far, f32[32,8,640]{2,1,0:T(8,128)S(1)} %collective-permute-done.2.b3, f32[32,8,640]{2,1,0:T(8,128)} %collective-permute-done.3.near, ...), custom_call_target="tpu_custom_call" | custom-call | flops 2013265920 | bytes 8388608 | tf_op jit(solution)/shard_map/pallas_call | solution.py:120
  90.9 3.5 %all-to-all-start.2 = ((f32[2,128,640]{2,1,0:T(8,128)}), f32[2,128,640]{2,1,0:T(8,128)S(1)}, u32[]{:S(2)}, u32[]{:S(2)}) async-start(f32[2,128,640]{2,1,0:T(8,128)} %shard_map.79), calls=%async_computation.2 | async-start | bytes 1310720 | tf_op jit(solution)/shard_map/all_to_all | solution.py:213
  94.4 0.0 collective-permute-done.9.c3
  94.4 0.0 collective-permute-done.8.c2
  94.4 0.0 collective-permute-done.7.c1
  94.4 1.8 %all-to-all-done.2.part_ref = f32[2,128,640]{2,1,0:T(8,128)S(1)} async-done(((f32[2,128,640]{2,1,0:T(8,128)}), f32[2,128,640]{2,1,0:T(8,128)S(1)}, u32[]{:S(2)}, u32[]{:S(2)}) %all-to-all-start.2) | async-done | bytes 655392 | tf_op jit(solution)/shard_map/all_to_all | solution.py:213
  96.2 0.2 shard_map.81
  96.4 34.8 %all_to_all.20.p_ref = f32[64,2,896]{2,1,0:T(2,128)S(1)} all-to-all(f32[64,2,896]{2,1,0:T(2,128)S(1)} %shard_map.81), channel_id=1, replica_groups=mesh['y'=8,'zl'=2,'x'=4,'zh'=4,'core'=2] {'y','zl','zh'}, dimensions={0} | all-to-all | bytes 917504 | tf_op jit(solution)/shard_map/all_to_all | solution.py:213
  131.2 5.3 %collective-permute-start.10 = (f32[2,640]{1,0:T(2,128)S(1)}, f32[2,640]{1,0:T(2,128)S(1)}, u32[]{:S(2)}, u32[]{:S(2)}) collective-permute-start(f32[2,640]{1,0:T(2,128)S(1)} %get-tuple-element.10), channel_id=1, source_target_pairs={{0,0},{2,16},{4,32},{6,48},{8,2},{10,18},{12,34},{14,50},{16,4},{1... | collective-permute-start | bytes 15368 | tf_op jit(solution)/shard_map/ppermute | solution.py:250
  136.5 0.1 reshape.19
  136.6 0.6 copy.8
  137.2 3.3 %collective-permute-done.10 = f32[2,640]{1,0:T(2,128)S(1)} collective-permute-done((f32[2,640]{1,0:T(2,128)S(1)}, f32[2,640]{1,0:T(2,128)S(1)}, u32[]{:S(2)}, u32[]{:S(2)}) %collective-permute-start.10) | collective-permute-done | bytes 5152 | tf_op jit(solution)/shard_map/ppermute | solution.py:250
  140.6 0.6 copy.10
  (2 shorter events, 0.0 us)
Async XLA Ops:
  2.3 29.6 %all-to-all-start = ((f32[64,2,8,128]{3,2,1,0:T(8,128)}), f32[64,2,8,128]{3,2,1,0:T(8,128)S(1)}, u32[]{:S(2)}, u32[]{:S(2)}) async-start(f32[64,2,8,128]{3,2,1,0:T(8,128)} %shard_map.78), calls=%async_computation | async-start | bytes 1048576 | tf_op jit(solution)/shard_map/all_to_all | solution.py:213
  14.8 1.6 %copy-start = (f32[4,4,64,512]{3,2,1,0:T(8,128)S(1)}, f32[4,4,64,512]{3,2,1,0:T(8,128)}, u32[]{:S(2)}) copy-start(f32[4,4,64,512]{3,2,1,0:T(8,128)} %a_ref.1) | copy-start | bytes 6291460
  20.9 15.5 %copy-start.4 = (f32[64,8,640]{2,1,0:T(8,128)S(1)}, f32[64,8,640]{2,1,0:T(8,128)}, u32[]{:S(2)}) copy-start(f32[64,8,640]{2,1,0:T(8,128)} %b0) | copy-start | bytes 3932164
  32.0 52.2 %all-to-all-start.1 = ((f32[16,2,8,2048]{3,2,1,0:T(8,128)}), f32[16,2,8,2048]{3,2,1,0:T(8,128)}, u32[]{:S(2)}, u32[]{:S(2)}) async-start(f32[16,2,8,2048]{3,2,1,0:T(8,128)} %shard_map.77), calls=%async_computation.1 | async-start | bytes 4194304 | tf_op jit(solution)/shard_map/all_to_all | solution.py:213
  36.4 28.1 %copy-start.7 = (s32[512]{0:T(512)S(1)}, s32[512]{0:T(512)}, u32[]{:S(2)}) copy-start(s32[512]{0:T(512)} %param.10) | copy-start | bytes 6148
  36.4 28.3 %copy-start.1 = (f32[4,4,64,512]{3,2,1,0:T(8,128)S(1)}, f32[4,4,64,512]{3,2,1,0:T(8,128)}, u32[]{:S(2)}) copy-start(f32[4,4,64,512]{3,2,1,0:T(8,128)} %a_ref.1) | copy-start | bytes 6291460
  36.5 28.2 %copy-start.2 = (s32[32]{0:T(128)S(1)}, s32[32]{0:T(128)}, u32[]{:S(2)}) copy-start(s32[32]{0:T(128)} %occ_ref.1) | copy-start | bytes 388
  36.5 28.2 %copy-start.3 = (s32[128]{0:T(128)S(1)}, s32[128]{0:T(128)}, u32[]{:S(2)}) copy-start(s32[128]{0:T(128)} %param.11) | copy-start | bytes 1540
  36.6 17.2 %collective-permute-start.4 = (f32[32,8,640]{2,1,0:T(8,128)S(1)}, f32[32,8,640]{2,1,0:T(8,128)S(1)}, u32[]{:S(2)}, u32[]{:S(2)}) collective-permute-start(f32[32,8,640]{2,1,0:T(8,128)S(1)} %get-tuple-element.12), channel_id=1, source_target_pairs={{0,24},{8,0},{16,8},{24,16},{1,25},{9,1},{17,9},{25,17},{2,26},{10... | collective-permute-start | bytes 1966088 | tf_op jit(solution)/shard_map/ppermute | solution.py:227
  39.0 19.9 %collective-permute-start = (f32[32,8,640]{2,1,0:T(8,128)S(1)}, f32[32,8,640]{2,1,0:T(8,128)S(1)}, u32[]{:S(2)}, u32[]{:S(2)}) collective-permute-start(f32[32,8,640]{2,1,0:T(8,128)S(1)} %get-tuple-element.13), channel_id=1, source_target_pairs={{0,8},{8,16},{16,24},{24,0},{1,9},{9,17},{17,25},{25,1},{2,10},{10... | collective-permute-start | bytes 1966088 | tf_op jit(solution)/shard_map/ppermute | solution.py:226
  43.8 20.8 %collective-permute-start.6 = (f32[64,2,8,128]{3,2,1,0:T(8,128)S(1)}, f32[64,2,8,128]{3,2,1,0:T(8,128)S(1)}, u32[]{:S(2)}, u32[]{:S(2)}) collective-permute-start(f32[64,2,8,128]{3,2,1,0:T(8,128)S(1)} %all-to-all-done.own_ref), channel_id=1, source_target_pairs={{0,1},{1,0},{2,3},{3,2},{4,5},{5,4},{6,7},{7,6},{8,9},{9,8},{10,11... | collective-permute-start | bytes 1572872 | tf_op jit(solution)/shard_map/ppermute | solution.py:224
  45.7 27.3 %collective-permute-start.1 = (f32[32,8,640]{2,1,0:T(8,128)S(1)}, f32[32,8,640]{2,1,0:T(8,128)S(1)}, u32[]{:S(2)}, u32[]{:S(2)}) collective-permute-start(f32[32,8,640]{2,1,0:T(8,128)S(1)} %get-tuple-element.12), channel_id=1, source_target_pairs={{0,8},{8,16},{16,24},{24,0},{1,9},{9,17},{17,25},{25,1},{2,10},{10... | collective-permute-start | bytes 1966088 | tf_op jit(solution)/shard_map/ppermute | solution.py:228
  47.7 29.2 %collective-permute-start.2 = (f32[32,8,640]{2,1,0:T(8,128)S(1)}, f32[32,8,640]{2,1,0:T(8,128)S(1)}, u32[]{:S(2)}, u32[]{:S(2)}) collective-permute-start(f32[32,8,640]{2,1,0:T(8,128)S(1)} %get-tuple-element.13), channel_id=1, source_target_pairs={{0,24},{8,0},{16,8},{24,16},{1,25},{9,1},{17,9},{25,17},{2,26},{10... | collective-permute-start | bytes 1966088 | tf_op jit(solution)/shard_map/ppermute | solution.py:229
  53.8 30.4 %copy-start.5 = (f32[32,8,640]{2,1,0:T(8,128)}, f32[32,8,640]{2,1,0:T(8,128)S(1)}, u32[]{:S(2)}) copy-start(f32[32,8,640]{2,1,0:T(8,128)S(1)} %collective-permute-done.4.b3_far) | copy-start | bytes 1966084
  53.8 28.9 %collective-permute-start.5 = (f32[32,8,640]{2,1,0:T(8,128)S(1)}, f32[32,8,640]{2,1,0:T(8,128)S(1)}, u32[]{:S(2)}, u32[]{:S(2)}) collective-permute-start(f32[32,8,640]{2,1,0:T(8,128)S(1)} %collective-permute-done.4.b3_far), channel_id=1, source_target_pairs={{0,24},{8,0},{16,8},{24,16},{1,25},{9,1},{17,9},{25,17},{2,26},{10... | collective-permute-start | bytes 1966088 | tf_op jit(solution)/shard_map/ppermute | solution.py:231
  58.9 25.2 %collective-permute-start.3 = (f32[32,8,640]{2,1,0:T(8,128)S(1)}, f32[32,8,640]{2,1,0:T(8,128)}, u32[]{:S(2)}, u32[]{:S(2)}) collective-permute-start(f32[32,8,640]{2,1,0:T(8,128)S(1)} %collective-permute-done.b1), channel_id=1, source_target_pairs={{0,8},{8,16},{16,24},{24,0},{1,9},{9,17},{17,25},{25,1},{2,10},{10... | collective-permute-start | bytes 1966088 | tf_op jit(solution)/shard_map/ppermute | solution.py:230
  66.5 27.8 %collective-permute-start.9 = (f32[32,256]{1,0:T(8,128)S(1)}, f32[32,256]{1,0:T(8,128)S(1)}, u32[]{:S(2)}, u32[]{:S(2)}) collective-permute-start(f32[32,256]{1,0:T(8,128)S(1)} %get-tuple-element.14), channel_id=1, source_target_pairs={{0,24},{8,0},{16,8},{24,16},{1,25},{9,1},{17,9},{25,17},{2,26},{10... | collective-permute-start | bytes 98312 | tf_op jit(solution)/shard_map/ppermute | solution.py:235
  73.0 21.4 %collective-permute-start.8 = (f32[32,256]{1,0:T(8,128)S(1)}, f32[32,256]{1,0:T(8,128)S(1)}, u32[]{:S(2)}, u32[]{:S(2)}) collective-permute-start(f32[32,256]{1,0:T(8,128)S(1)} %get-tuple-element.15), channel_id=1, source_target_pairs={{0,16},{8,24},{16,0},{24,8},{1,17},{9,25},{17,1},{25,9},{2,18},{10... | collective-permute-start | bytes 98312 | tf_op jit(solution)/shard_map/ppermute | solution.py:235
  76.9 17.5 %collective-permute-start.7 = (f32[32,256]{1,0:T(8,128)S(1)}, f32[32,256]{1,0:T(8,128)S(1)}, u32[]{:S(2)}, u32[]{:S(2)}) collective-permute-start(f32[32,256]{1,0:T(8,128)S(1)} %get-tuple-element.16), channel_id=1, source_target_pairs={{0,8},{8,16},{16,24},{24,0},{1,9},{9,17},{17,25},{25,1},{2,10},{10... | collective-permute-start | bytes 98312 | tf_op jit(solution)/shard_map/ppermute | solution.py:235
  82.6 0.9 copy-start.6
  90.9 5.4 %all-to-all-start.2 = ((f32[2,128,640]{2,1,0:T(8,128)}), f32[2,128,640]{2,1,0:T(8,128)S(1)}, u32[]{:S(2)}, u32[]{:S(2)}) async-start(f32[2,128,640]{2,1,0:T(8,128)} %shard_map.79), calls=%async_computation.2 | async-start | bytes 1310720 | tf_op jit(solution)/shard_map/all_to_all | solution.py:213
  131.2 9.4 %collective-permute-start.10 = (f32[2,640]{1,0:T(2,128)S(1)}, f32[2,640]{1,0:T(2,128)S(1)}, u32[]{:S(2)}, u32[]{:S(2)}) collective-permute-start(f32[2,640]{1,0:T(2,128)S(1)} %get-tuple-element.10), channel_id=1, source_target_pairs={{0,0},{2,16},{4,32},{6,48},{8,2},{10,18},{12,34},{14,50},{16,4},{1... | collective-permute-start | bytes 15368 | tf_op jit(solution)/shard_map/ppermute | solution.py:250

commit v11 on v10

--- a/solution.py
+++ b/solution.py
@@ -62,12 +62,12 @@
 
 def ladder_kernel(b1, b1_far, b3, near, x_hbm, b0, b3_far, far, o_ref, x_ref, held, sems):
     me = lax.axis_index("x")
-    pieces = ((0, 8), (8, 8), (16, 16), (32, 16), (48, 16))
+    pieces = ((0, 8), (8, 12), (20, 16), (36, 16), (52, 12))
 
     def copies(k, c, size):
-        part, half, span = pl.ds(c, size), pl.ds(c % 32, size), pl.ds(c * 32, size * 32)
+        part, half, span = pl.ds(c, size), pl.ds(c % 36, size), pl.ds(c * 32, size * 32)
         found = [(0, b0.at[part])]
-        if c >= 32:
+        if c >= 36:
             found += [(1, b3_far.at[half]), (2, far.at[half])]
         return [
             pltpu.make_async_copy(x_hbm.at[:, :, :, span], x_ref.at[:, :, :, span], sems.at[3, k])
@@ -80,9 +80,9 @@
         for copy in copies(k, c, size):
             copy.start()
     for k, (c, size) in enumerate(pieces):
-        part, half, span = pl.ds(c, size), pl.ds(c % 32, size), pl.ds(c * 32, size * 32)
-        held[lax.rem(me + 3, 4), part] = (b1 if c < 32 else b1_far)[half]
-        if c < 32:
+        part, half, span = pl.ds(c, size), pl.ds(c % 36, size), pl.ds(c * 32, size * 32)
+        held[lax.rem(me + 3, 4), part] = (b1 if c < 36 else b1_far)[half]
+        if c < 36:
             held[lax.rem(me + 1, 4), part] = b3[half]
             held[lax.rem(me + 2, 4), part] = near[half]
         for copy in copies(k, c, size):
@@ -222,7 +222,7 @@
     sent, own = lax.optimization_barrier((sent, own))
     x = exchange(sent, ("y", "zl"))
     other = lax.ppermute(own, "core", [(0, 1), (1, 0)])
-    lower, upper = ladder_ints[:32], ladder_ints[32:]
+    lower, upper = ladder_ints[:36], ladder_ints[36:]
     b1 = lax.ppermute(lower, "x", ring[1])
     b3_far = lax.ppermute(upper, "x", ring[3])
     b1_far = lax.ppermute(upper, "x", ring[1])

time: 142 us -> 150 us (1.056)
  waiting for transfers between devices: 29 us -> 42.1 us
  starting transfers between devices: 57.6 us -> 52.3 us
    ppermute x1, waiting for transfers between devices: 4.52 us -> 15 us  [body(): b1_far = lax.ppermute(upper, 'x', ring[1])]
    ppermute x1, waiting for transfers between devices: 3.25 us -> 7.47 us  [body(): b1 = lax.ppermute(lower, 'x', ring[1])]
    ppermute x1, waiting for transfers between devices: 3.34 us -> 6.75 us  [body(): ladder_resid = lax.ppermute(part, ('zl', 'x', 'zh'), move)]
    ppermute x1, starting transfers between devices: 5.34 us -> 1.93 us  [body(): ladder_resid = lax.ppermute(part, ('zl', 'x', 'zh'), move)]
    ppermute x1, waiting for transfers between devices: 2.21 us -> 0.01 us  [body(): b3_far = lax.ppermute(upper, 'x', ring[3])]
    ppermute x1, waiting for transfers between devices: 2.11 us -> 0.01 us  [body(): far = lax.ppermute(b3_far, 'x', ring[3])]
    ppermute x1, starting transfers between devices: 1.91 us -> 3.92 us  [body(): far = lax.ppermute(b3_far, 'x', ring[3])]
    ppermute x1, starting transfers between devices: 3.82 us -> 2.3 us  [body(): b3 = lax.ppermute(lower, 'x', ring[3])]
  transfers between devices with their start and end apart: 14 -> 14, of which waited for: 8 -> 5; matrix products, arithmetic and copies ran while one was open for 1% -> 1% of each run, Pallas kernels for 9% -> 9%
where the time goes in v11:
time: 150 us; the launch traced here: 149 us
  starting transfers between devices  52.3 us (35%)
  waiting for transfers between devices  42.1 us (28%)
  blocking collectives  34.6 us (23%)
  Pallas kernels  15.6 us (10%)
  local copies, waits for them, and re-layouts  3.17 us (2%)
    all_to_all x1, blocking collectives, exchange(): return lax.all_to_all(v, axes, split_axis=0, concat_axis=0, tiled=True)  34.6 us
    all_to_all x3, starting transfers between devices, exchange(): return lax.all_to_all(v, axes, split_axis=0, concat_axis=0, tiled=True)  20.4 us
    ppermute x1, waiting for transfers between devices, body(): b1_far = lax.ppermute(upper, 'x', ring[1])  15 us
    all_to_all x3, waiting for transfers between devices, exchange(): return lax.all_to_all(v, axes, split_axis=0, concat_axis=0, tiled=True)  12.8 us
    ppermute x3, starting transfers between devices, body(): lax.ppermute(parts[s], 'x', ring[s])  9.46 us
    ppermute x1, waiting for transfers between devices, body(): b1 = lax.ppermute(lower, 'x', ring[1])  7.47 us
    pallas_call x1, Pallas kernels, ladder(): pl.pallas_call(ladder_kernel, in_specs=[VMEM] * 4 + [anywhere] * 4, out_s...  7.4 us
    ppermute x1, waiting for transfers between devices, body(): ladder_resid = lax.ppermute(part, ('zl', 'x', 'zh'), move)  6.75 us
  transfers between devices with their start and end apart: 14, of which 5 were waited for; matrix products, arithmetic and copies ran while one was open for 1% of the time, Pallas kernels for 9%

profile of v11, /device:TPU:6, one launch (start us, length us, event | category | flops | bytes accessed | tf_op | source)
XLA Modules:
  0.0 148.8 jit_solution(5010928284985699092)
XLA Ops:
  0.6 1.7 %shard_map.78 = f32[64,2,8,128]{3,2,1,0:T(8,128)} custom-call(f32[8,4,8,128]{3,2,1,0:T(8,128)} %bitcast.15), custom_call_target="tpu_custom_call" | custom-call | bytes 1048576 | tf_op jit(solution)/shard_map/pallas_call | solution.py:146
  2.3 12.4 %all-to-all-start = ((f32[64,2,8,128]{3,2,1,0:T(8,128)}), f32[64,2,8,128]{3,2,1,0:T(8,128)S(1)}, u32[]{:S(2)}, u32[]{:S(2)}) async-start(f32[64,2,8,128]{3,2,1,0:T(8,128)} %shard_map.78), calls=%async_computation | async-start | bytes 1048576 | tf_op jit(solution)/shard_map/all_to_all | solution.py:213
  14.7 0.0 copy-start
  14.8 1.6 %copy-done = f32[4,4,64,512]{3,2,1,0:T(8,128)S(1)} copy-done((f32[4,4,64,512]{3,2,1,0:T(8,128)S(1)}, f32[4,4,64,512]{3,2,1,0:T(8,128)}, u32[]{:S(2)}) %copy-start) | copy-done | bytes 2097176
  16.3 4.6 %shard_map.77 = f32[16,2,8,2048]{3,2,1,0:T(8,128)} custom-call(f32[4,2,2,64,512]{4,3,2,1,0:T(8,128)S(1)} %bitcast.13), custom_call_target="tpu_custom_call" | custom-call | flops 1048576 | bytes 4194304 | tf_op jit(solution)/shard_map/pallas_call | solution.py:52
  20.9 0.0 copy-start.4
  20.9 11.1 %all-to-all-done.own_ref = f32[64,2,8,128]{3,2,1,0:T(8,128)S(1)} async-done(((f32[64,2,8,128]{3,2,1,0:T(8,128)}), f32[64,2,8,128]{3,2,1,0:T(8,128)S(1)}, u32[]{:S(2)}, u32[]{:S(2)}) %all-to-all-start) | async-done | bytes 524320 | tf_op jit(solution)/shard_map/all_to_all | solution.py:213
  32.0 4.4 %all-to-all-start.1 = ((f32[16,2,8,2048]{3,2,1,0:T(8,128)}), f32[16,2,8,2048]{3,2,1,0:T(8,128)}, u32[]{:S(2)}, u32[]{:S(2)}) async-start(f32[16,2,8,2048]{3,2,1,0:T(8,128)} %shard_map.77), calls=%async_computation.1 | async-start | bytes 4194304 | tf_op jit(solution)/shard_map/all_to_all | solution.py:213
  36.4 0.0 copy-done.4
  36.4 0.0 copy-start.7
  36.4 0.0 copy-start.1
  36.4 0.0 copy-start.2
  36.5 0.0 copy-start.3
  36.5 3.4 %collective-permute-start = (f32[36,8,640]{2,1,0:T(8,128)S(1)}, f32[36,8,640]{2,1,0:T(8,128)S(1)}, u32[]{:S(2)}, u32[]{:S(2)}) collective-permute-start(f32[36,8,640]{2,1,0:T(8,128)S(1)} %slice.18), channel_id=1, source_target_pairs={{0,8},{8,16},{16,24},{24,0},{1,9},{9,17},{17,25},{25,1},{2,10},{10... | collective-permute-start | bytes 2211848 | tf_op jit(solution)/shard_map/ppermute | solution.py:226
  40.0 2.6 %collective-permute-start.4 = (f32[28,8,640]{2,1,0:T(8,128)S(1)}, f32[28,8,640]{2,1,0:T(8,128)S(1)}, u32[]{:S(2)}, u32[]{:S(2)}) collective-permute-start(f32[28,8,640]{2,1,0:T(8,128)S(1)} %slice.19), channel_id=1, source_target_pairs={{0,24},{8,0},{16,8},{24,16},{1,25},{9,1},{17,9},{25,17},{2,26},{10... | collective-permute-start | bytes 1720328 | tf_op jit(solution)/shard_map/ppermute | solution.py:227
  42.6 1.9 %collective-permute-start.6 = (f32[64,2,8,128]{3,2,1,0:T(8,128)S(1)}, f32[64,2,8,128]{3,2,1,0:T(8,128)S(1)}, u32[]{:S(2)}, u32[]{:S(2)}) collective-permute-start(f32[64,2,8,128]{3,2,1,0:T(8,128)S(1)} %all-to-all-done.own_ref), channel_id=1, source_target_pairs={{0,1},{1,0},{2,3},{3,2},{4,5},{5,4},{6,7},{7,6},{8,9},{9,8},{10,11... | collective-permute-start | bytes 1572872 | tf_op jit(solution)/shard_map/ppermute | solution.py:224
  44.5 2.3 %collective-permute-start.2 = (f32[36,8,640]{2,1,0:T(8,128)S(1)}, f32[36,8,640]{2,1,0:T(8,128)S(1)}, u32[]{:S(2)}, u32[]{:S(2)}) collective-permute-start(f32[36,8,640]{2,1,0:T(8,128)S(1)} %slice.18), channel_id=1, source_target_pairs={{0,24},{8,0},{16,8},{24,16},{1,25},{9,1},{17,9},{25,17},{2,26},{10... | collective-permute-start | bytes 2211848 | tf_op jit(solution)/shard_map/ppermute | solution.py:229
  46.8 7.5 %collective-permute-done.b1 = f32[36,8,640]{2,1,0:T(8,128)S(1)} collective-permute-done((f32[36,8,640]{2,1,0:T(8,128)S(1)}, f32[36,8,640]{2,1,0:T(8,128)S(1)}, u32[]{:S(2)}, u32[]{:S(2)}) %collective-permute-start) | collective-permute-done | bytes 737312 | tf_op jit(solution)/shard_map/ppermute | solution.py:226
  54.3 0.0 copy-start.5
  54.3 4.5 %collective-permute-start.3 = (f32[36,8,640]{2,1,0:T(8,128)S(1)}, f32[36,8,640]{2,1,0:T(8,128)}, u32[]{:S(2)}, u32[]{:S(2)}) collective-permute-start(f32[36,8,640]{2,1,0:T(8,128)S(1)} %collective-permute-done.b1), channel_id=1, source_target_pairs={{0,8},{8,16},{16,24},{24,0},{1,9},{9,17},{17,25},{25,1},{2,10},{10... | collective-permute-start | bytes 2211848 | tf_op jit(solution)/shard_map/ppermute | solution.py:230
  58.8 1.9 %collective-permute-start.1 = (f32[28,8,640]{2,1,0:T(8,128)S(1)}, f32[28,8,640]{2,1,0:T(8,128)S(1)}, u32[]{:S(2)}, u32[]{:S(2)}) collective-permute-start(f32[28,8,640]{2,1,0:T(8,128)S(1)} %slice.19), channel_id=1, source_target_pairs={{0,8},{8,16},{16,24},{24,0},{1,9},{9,17},{17,25},{25,1},{2,10},{10... | collective-permute-start | bytes 1720328 | tf_op jit(solution)/shard_map/ppermute | solution.py:228
  60.7 0.0 collective-permute-done.4.b3_far
  60.7 3.9 %collective-permute-start.5 = (f32[28,8,640]{2,1,0:T(8,128)S(1)}, f32[28,8,640]{2,1,0:T(8,128)S(1)}, u32[]{:S(2)}, u32[]{:S(2)}) collective-permute-start(f32[28,8,640]{2,1,0:T(8,128)S(1)} %collective-permute-done.4.b3_far), channel_id=1, source_target_pairs={{0,24},{8,0},{16,8},{24,16},{1,25},{9,1},{17,9},{25,17},{2,26},{10... | collective-permute-start | bytes 1720328 | tf_op jit(solution)/shard_map/ppermute | solution.py:231
  64.7 0.0 collective-permute-done.6.other_ref
  64.7 0.0 copy-done.7
  64.7 0.1 broadcast_in_dim.4.vir_ref
  64.8 0.0 copy-done.1
  64.8 0.0 copy-done.2
  64.8 0.0 copy-done.3
  64.9 1.8 %shard_map.80 = f32[4,32,256]{2,1,0:T(8,128)S(1)} custom-call(s32[32]{0:T(128)S(1)} %copy-done.2, f32[4,4,64,512]{3,2,1,0:T(8,128)S(1)} %copy-done.1, f32[64,2,8,128]{3,2,1,0:T(8,128)S(1)} %all-to-all-done.own_ref, f32[64,2,8,128]{3,2,1,0:T(8,128)S(1)} %collective-permute-done.6.other_ref, s32[512,128]{1,0:T(8,128)S(1)} %broadcast_in_dim.4.vir_ref, ...), custom_call_target="tpu_custom_call" | custom-call | flops 402653184 | bytes 3145728 | tf_op jit(solution)/shard_map/pallas_call | solution.py:199
  66.7 1.9 %collective-permute-start.9 = (f32[32,256]{1,0:T(8,128)S(1)}, f32[32,256]{1,0:T(8,128)S(1)}, u32[]{:S(2)}, u32[]{:S(2)}) collective-permute-start(f32[32,256]{1,0:T(8,128)S(1)} %get-tuple-element.12), channel_id=1, source_target_pairs={{0,24},{8,0},{16,8},{24,16},{1,25},{9,1},{17,9},{25,17},{2,26},{10... | collective-permute-start | bytes 98312 | tf_op jit(solution)/shard_map/ppermute | solution.py:235
  68.6 15.0 %collective-permute-done.1.b1_far = f32[28,8,640]{2,1,0:T(8,128)S(1)} collective-permute-done((f32[28,8,640]{2,1,0:T(8,128)S(1)}, f32[28,8,640]{2,1,0:T(8,128)S(1)}, u32[]{:S(2)}, u32[]{:S(2)}) %collective-permute-start.1) | collective-permute-done | bytes 573472 | tf_op jit(solution)/shard_map/ppermute | solution.py:228
  83.6 4.1 %collective-permute-start.8 = (f32[32,256]{1,0:T(8,128)S(1)}, f32[32,256]{1,0:T(8,128)S(1)}, u32[]{:S(2)}, u32[]{:S(2)}) collective-permute-start(f32[32,256]{1,0:T(8,128)S(1)} %get-tuple-element.13), channel_id=1, source_target_pairs={{0,16},{8,24},{16,0},{24,8},{1,17},{9,25},{17,1},{25,9},{2,18},{10... | collective-permute-start | bytes 98312 | tf_op jit(solution)/shard_map/ppermute | solution.py:235
  87.7 0.0 collective-permute-done.2.b3
  87.7 0.0 copy-start.6
  87.7 3.4 %collective-permute-start.7 = (f32[32,256]{1,0:T(8,128)S(1)}, f32[32,256]{1,0:T(8,128)S(1)}, u32[]{:S(2)}, u32[]{:S(2)}) collective-permute-start(f32[32,256]{1,0:T(8,128)S(1)} %get-tuple-element.14), channel_id=1, source_target_pairs={{0,8},{8,16},{16,24},{24,0},{1,9},{9,17},{17,25},{25,1},{2,10},{10... | collective-permute-start | bytes 98312 | tf_op jit(solution)/shard_map/ppermute | solution.py:235
  91.2 0.0 collective-permute-done.5.far
  91.2 0.0 copy-done.6
  91.2 0.0 collective-permute-done.3.near
  91.2 0.0 all-to-all-done.1.x_hbm
  91.2 0.0 copy-done.5
  91.2 7.4 %shard_map.79 = f32[2,128,640]{2,1,0:T(8,128)} custom-call(f32[36,8,640]{2,1,0:T(8,128)} %copy-done.5, f32[28,8,640]{2,1,0:T(8,128)S(1)} %collective-permute-done.1.b1_far, f32[36,8,640]{2,1,0:T(8,128)} %copy-done.6, f32[36,8,640]{2,1,0:T(8,128)} %collective-permute-done.3.near, f32[16,2,8,2048]{3,2,1,0:T(8,128)} %all-to-all-done.1.x_hbm, f32[64,8,640]{2,1,0:T(8,128)} %b0, ...), custom_call_target="tpu_custom_call" | custom-call | flops 2013265920 | bytes 8388608 | tf_op jit(solution)/shard_map/pallas_call | solution.py:120
  98.6 3.5 %all-to-all-start.2 = ((f32[2,128,640]{2,1,0:T(8,128)}), f32[2,128,640]{2,1,0:T(8,128)S(1)}, u32[]{:S(2)}, u32[]{:S(2)}) async-start(f32[2,128,640]{2,1,0:T(8,128)} %shard_map.79), calls=%async_computation.2 | async-start | bytes 1310720 | tf_op jit(solution)/shard_map/all_to_all | solution.py:213
  102.1 0.0 collective-permute-done.9.c3
  102.1 0.0 collective-permute-done.8.c2
  102.2 0.0 collective-permute-done.7.c1
  102.2 1.8 %all-to-all-done.2.part_ref = f32[2,128,640]{2,1,0:T(8,128)S(1)} async-done(((f32[2,128,640]{2,1,0:T(8,128)}), f32[2,128,640]{2,1,0:T(8,128)S(1)}, u32[]{:S(2)}, u32[]{:S(2)}) %all-to-all-start.2) | async-done | bytes 655392 | tf_op jit(solution)/shard_map/all_to_all | solution.py:213
  104.0 0.2 shard_map.81
  104.1 34.6 %all_to_all.20.p_ref = f32[64,2,896]{2,1,0:T(2,128)S(1)} all-to-all(f32[64,2,896]{2,1,0:T(2,128)S(1)} %shard_map.81), channel_id=1, replica_groups=mesh['y'=8,'zl'=2,'x'=4,'zh'=4,'core'=2] {'y','zl','zh'}, dimensions={0} | all-to-all | bytes 917504 | tf_op jit(solution)/shard_map/all_to_all | solution.py:213
  138.8 1.9 %collective-permute-start.10 = (f32[2,640]{1,0:T(2,128)S(1)}, f32[2,640]{1,0:T(2,128)S(1)}, u32[]{:S(2)}, u32[]{:S(2)}) collective-permute-start(f32[2,640]{1,0:T(2,128)S(1)} %get-tuple-element.10), channel_id=1, source_target_pairs={{0,0},{2,16},{4,32},{6,48},{8,2},{10,18},{12,34},{14,50},{16,4},{1... | collective-permute-start | bytes 15368 | tf_op jit(solution)/shard_map/ppermute | solution.py:250
  140.7 0.1 reshape.19
  140.8 0.6 copy.8
  141.4 6.8 %collective-permute-done.10 = f32[2,640]{1,0:T(2,128)S(1)} collective-permute-done((f32[2,640]{1,0:T(2,128)S(1)}, f32[2,640]{1,0:T(2,128)S(1)}, u32[]{:S(2)}, u32[]{:S(2)}) %collective-permute-start.10) | collective-permute-done | bytes 5152 | tf_op jit(solution)/shard_map/ppermute | solution.py:250
  148.2 0.6 copy.10
  (4 shorter events, 0.1 us)
Async XLA Ops:
  2.3 29.6 %all-to-all-start = ((f32[64,2,8,128]{3,2,1,0:T(8,128)}), f32[64,2,8,128]{3,2,1,0:T(8,128)S(1)}, u32[]{:S(2)}, u32[]{:S(2)}) async-start(f32[64,2,8,128]{3,2,1,0:T(8,128)} %shard_map.78), calls=%async_computation | async-start | bytes 1048576 | tf_op jit(solution)/shard_map/all_to_all | solution.py:213
  14.7 1.6 %copy-start = (f32[4,4,64,512]{3,2,1,0:T(8,128)S(1)}, f32[4,4,64,512]{3,2,1,0:T(8,128)}, u32[]{:S(2)}) copy-start(f32[4,4,64,512]{3,2,1,0:T(8,128)} %a_ref.1) | copy-start | bytes 6291460
  20.9 15.5 %copy-start.4 = (f32[64,8,640]{2,1,0:T(8,128)S(1)}, f32[64,8,640]{2,1,0:T(8,128)}, u32[]{:S(2)}) copy-start(f32[64,8,640]{2,1,0:T(8,128)} %b0) | copy-start | bytes 3932164
  32.0 59.2 %all-to-all-start.1 = ((f32[16,2,8,2048]{3,2,1,0:T(8,128)}), f32[16,2,8,2048]{3,2,1,0:T(8,128)}, u32[]{:S(2)}, u32[]{:S(2)}) async-start(f32[16,2,8,2048]{3,2,1,0:T(8,128)} %shard_map.77), calls=%async_computation.1 | async-start | bytes 4194304 | tf_op jit(solution)/shard_map/all_to_all | solution.py:213
  36.4 28.3 %copy-start.7 = (s32[512]{0:T(512)S(1)}, s32[512]{0:T(512)}, u32[]{:S(2)}) copy-start(s32[512]{0:T(512)} %param.10) | copy-start | bytes 6148
  36.4 28.4 %copy-start.1 = (f32[4,4,64,512]{3,2,1,0:T(8,128)S(1)}, f32[4,4,64,512]{3,2,1,0:T(8,128)}, u32[]{:S(2)}) copy-start(f32[4,4,64,512]{3,2,1,0:T(8,128)} %a_ref.1) | copy-start | bytes 6291460
  36.4 28.4 %copy-start.2 = (s32[32]{0:T(128)S(1)}, s32[32]{0:T(128)}, u32[]{:S(2)}) copy-start(s32[32]{0:T(128)} %occ_ref.1) | copy-start | bytes 388
  36.5 28.4 %copy-start.3 = (s32[128]{0:T(128)S(1)}, s32[128]{0:T(128)}, u32[]{:S(2)}) copy-start(s32[128]{0:T(128)} %param.11) | copy-start | bytes 1540
  36.5 17.7 %collective-permute-start = (f32[36,8,640]{2,1,0:T(8,128)S(1)}, f32[36,8,640]{2,1,0:T(8,128)S(1)}, u32[]{:S(2)}, u32[]{:S(2)}) collective-permute-start(f32[36,8,640]{2,1,0:T(8,128)S(1)} %slice.18), channel_id=1, source_target_pairs={{0,8},{8,16},{16,24},{24,0},{1,9},{9,17},{17,25},{25,1},{2,10},{10... | collective-permute-start | bytes 2211848 | tf_op jit(solution)/shard_map/ppermute | solution.py:226
  40.0 20.8 %collective-permute-start.4 = (f32[28,8,640]{2,1,0:T(8,128)S(1)}, f32[28,8,640]{2,1,0:T(8,128)S(1)}, u32[]{:S(2)}, u32[]{:S(2)}) collective-permute-start(f32[28,8,640]{2,1,0:T(8,128)S(1)} %slice.19), channel_id=1, source_target_pairs={{0,24},{8,0},{16,8},{24,16},{1,25},{9,1},{17,9},{25,17},{2,26},{10... | collective-permute-start | bytes 1720328 | tf_op jit(solution)/shard_map/ppermute | solution.py:227
  42.6 22.1 %collective-permute-start.6 = (f32[64,2,8,128]{3,2,1,0:T(8,128)S(1)}, f32[64,2,8,128]{3,2,1,0:T(8,128)S(1)}, u32[]{:S(2)}, u32[]{:S(2)}) collective-permute-start(f32[64,2,8,128]{3,2,1,0:T(8,128)S(1)} %all-to-all-done.own_ref), channel_id=1, source_target_pairs={{0,1},{1,0},{2,3},{3,2},{4,5},{5,4},{6,7},{7,6},{8,9},{9,8},{10,11... | collective-permute-start | bytes 1572872 | tf_op jit(solution)/shard_map/ppermute | solution.py:224
  44.5 43.2 %collective-permute-start.2 = (f32[36,8,640]{2,1,0:T(8,128)S(1)}, f32[36,8,640]{2,1,0:T(8,128)S(1)}, u32[]{:S(2)}, u32[]{:S(2)}) collective-permute-start(f32[36,8,640]{2,1,0:T(8,128)S(1)} %slice.18), channel_id=1, source_target_pairs={{0,24},{8,0},{16,8},{24,16},{1,25},{9,1},{17,9},{25,17},{2,26},{10... | collective-permute-start | bytes 2211848 | tf_op jit(solution)/shard_map/ppermute | solution.py:229
  54.3 36.9 %copy-start.5 = (f32[36,8,640]{2,1,0:T(8,128)}, f32[36,8,640]{2,1,0:T(8,128)S(1)}, u32[]{:S(2)}) copy-start(f32[36,8,640]{2,1,0:T(8,128)S(1)} %collective-permute-done.b1) | copy-start | bytes 2211844
  54.3 36.9 %collective-permute-start.3 = (f32[36,8,640]{2,1,0:T(8,128)S(1)}, f32[36,8,640]{2,1,0:T(8,128)}, u32[]{:S(2)}, u32[]{:S(2)}) collective-permute-start(f32[36,8,640]{2,1,0:T(8,128)S(1)} %collective-permute-done.b1), channel_id=1, source_target_pairs={{0,8},{8,16},{16,24},{24,0},{1,9},{9,17},{17,25},{25,1},{2,10},{10... | collective-permute-start | bytes 2211848 | tf_op jit(solution)/shard_map/ppermute | solution.py:230
  58.8 24.8 %collective-permute-start.1 = (f32[28,8,640]{2,1,0:T(8,128)S(1)}, f32[28,8,640]{2,1,0:T(8,128)S(1)}, u32[]{:S(2)}, u32[]{:S(2)}) collective-permute-start(f32[28,8,640]{2,1,0:T(8,128)S(1)} %slice.19), channel_id=1, source_target_pairs={{0,8},{8,16},{16,24},{24,0},{1,9},{9,17},{17,25},{25,1},{2,10},{10... | collective-permute-start | bytes 1720328 | tf_op jit(solution)/shard_map/ppermute | solution.py:228
  60.7 30.4 %collective-permute-start.5 = (f32[28,8,640]{2,1,0:T(8,128)S(1)}, f32[28,8,640]{2,1,0:T(8,128)S(1)}, u32[]{:S(2)}, u32[]{:S(2)}) collective-permute-start(f32[28,8,640]{2,1,0:T(8,128)S(1)} %collective-permute-done.4.b3_far), channel_id=1, source_target_pairs={{0,24},{8,0},{16,8},{24,16},{1,25},{9,1},{17,9},{25,17},{2,26},{10... | collective-permute-start | bytes 1720328 | tf_op jit(solution)/shard_map/ppermute | solution.py:231
  66.7 35.5 %collective-permute-start.9 = (f32[32,256]{1,0:T(8,128)S(1)}, f32[32,256]{1,0:T(8,128)S(1)}, u32[]{:S(2)}, u32[]{:S(2)}) collective-permute-start(f32[32,256]{1,0:T(8,128)S(1)} %get-tuple-element.12), channel_id=1, source_target_pairs={{0,24},{8,0},{16,8},{24,16},{1,25},{9,1},{17,9},{25,17},{2,26},{10... | collective-permute-start | bytes 98312 | tf_op jit(solution)/shard_map/ppermute | solution.py:235
  83.6 18.6 %collective-permute-start.8 = (f32[32,256]{1,0:T(8,128)S(1)}, f32[32,256]{1,0:T(8,128)S(1)}, u32[]{:S(2)}, u32[]{:S(2)}) collective-permute-start(f32[32,256]{1,0:T(8,128)S(1)} %get-tuple-element.13), channel_id=1, source_target_pairs={{0,16},{8,24},{16,0},{24,8},{1,17},{9,25},{17,1},{25,9},{2,18},{10... | collective-permute-start | bytes 98312 | tf_op jit(solution)/shard_map/ppermute | solution.py:235
  87.7 3.5 %copy-start.6 = (f32[36,8,640]{2,1,0:T(8,128)}, f32[36,8,640]{2,1,0:T(8,128)S(1)}, u32[]{:S(2)}) copy-start(f32[36,8,640]{2,1,0:T(8,128)S(1)} %collective-permute-done.2.b3) | copy-start | bytes 2211844
  87.7 14.5 %collective-permute-start.7 = (f32[32,256]{1,0:T(8,128)S(1)}, f32[32,256]{1,0:T(8,128)S(1)}, u32[]{:S(2)}, u32[]{:S(2)}) collective-permute-start(f32[32,256]{1,0:T(8,128)S(1)} %get-tuple-element.14), channel_id=1, source_target_pairs={{0,8},{8,16},{16,24},{24,0},{1,9},{9,17},{17,25},{25,1},{2,10},{10... | collective-permute-start | bytes 98312 | tf_op jit(solution)/shard_map/ppermute | solution.py:235
  98.6 5.4 %all-to-all-start.2 = ((f32[2,128,640]{2,1,0:T(8,128)}), f32[2,128,640]{2,1,0:T(8,128)S(1)}, u32[]{:S(2)}, u32[]{:S(2)}) async-start(f32[2,128,640]{2,1,0:T(8,128)} %shard_map.79), calls=%async_computation.2 | async-start | bytes 1310720 | tf_op jit(solution)/shard_map/all_to_all | solution.py:213
  138.8 9.4 %collective-permute-start.10 = (f32[2,640]{1,0:T(2,128)S(1)}, f32[2,640]{1,0:T(2,128)S(1)}, u32[]{:S(2)}, u32[]{:S(2)}) collective-permute-start(f32[2,640]{1,0:T(2,128)S(1)} %get-tuple-element.10), channel_id=1, source_target_pairs={{0,0},{2,16},{4,32},{6,48},{8,2},{10,18},{12,34},{14,50},{16,4},{1... | collective-permute-start | bytes 15368 | tf_op jit(solution)/shard_map/ppermute | solution.py:250
